TPU v7x, 32 devices: a whole 2x2x4 slice. The times are simulated.
32 devices in a mesh: dp: 4 (over x, core), tensor: 8 (over z, y).
Axes of the slice: x: 2, y: 2, z: 4, core: 2. Of those that a mesh axis runs over, the one named last changes fastest.
Arguments:
- hidden_in: bfloat16 [8192, 2048], P('dp'), may hold values from -6 to 6
- cotangent: bfloat16 [8192, 2048], P('dp'), may hold values from -6 to 6
- routes: int32 [8192, 8], P('dp'), may hold values from 0 to 15, all different within a row
- segments: int32 [8, 1024], P('dp'), may hold values from 0 to 3, never falling along the last dimension, each value on 1 to 512 neighbouring positions
- gain_in: bfloat16 [2048], replicated, may hold values from 0.25 to 1.75
- w_query: bfloat16 [2048, 2048], P(None, 'tensor'), may hold values from -0.125 to 0.125
- w_key: bfloat16 [2048, 2048], P(None, 'tensor'), may hold values from -0.125 to 0.125
- w_value: bfloat16 [2048, 2048], P(None, 'tensor'), may hold values from -0.125 to 0.125
- w_out: bfloat16 [2048, 2048], P(None, 'tensor'), may hold values from -2 to 2
- gain_query: bfloat16 [2048], P('tensor'), may hold values from 0.25 to 1.75
- gain_key: bfloat16 [2048], P('tensor'), may hold values from 0.25 to 1.75
- gain_mid: bfloat16 [2048], replicated, may hold values from 0.25 to 1.75
- w_router: bfloat16 [2048, 16], replicated, may hold values from -0.0625 to 0.0625
- w_gate: bfloat16 [16, 2048, 1024], P(None, None, 'tensor'), may hold values from -0.125 to 0.125
- w_up: bfloat16 [16, 2048, 1024], P(None, None, 'tensor'), may hold values from -0.125 to 0.125
- w_down: bfloat16 [16, 2048, 1024], P(None, None, 'tensor'), may hold values from -1.5 to 1.5
Outputs:
- output: bfloat16 [8192, 2048], P('dp', 'tensor')
- grad_input: bfloat16 [8192, 2048], P('dp', 'tensor')
- grad_w_query: float32 [2048, 2048], P('dp', 'tensor')
- grad_w_key: float32 [2048, 2048], P('dp', 'tensor')
- grad_w_value: float32 [2048, 2048], P('dp', 'tensor')
- grad_w_out: float32 [2048, 2048], P('dp', 'tensor')
- grad_gain_in: float32 [2048], P('tensor')
- grad_gain_query: float32 [2048], P('tensor')
- grad_gain_key: float32 [2048], P('tensor')
- grad_gain_mid: float32 [2048], P('dp')
- grad_w_router: float32 [2048, 16], P('dp')
- grad_w_gate: float32 [16, 2048, 1024], P('dp', None, 'tensor')
- grad_w_up: float32 [16, 2048, 1024], P('dp', None, 'tensor')
- grad_w_down: float32 [16, 2048, 1024], P('dp', None, 'tensor')
Inputs may be any that keep to these rules, and one draw needn't show every extreme that they name: `routes`: each row names 8 different experts; every expert is named by some row. `segments`: numbers never fall along a row; each document holds 1 to 512 tokens, and some document holds exactly that many.
All inputs are finite; a program needn't handle non-finite values.
Results may differ from a plain program's by a relative error of at most 0.015.
The roundings to bfloat16 on the way count: a program that leaves them out, or rounds other values in their place, can miss the bound.
Values sent between devices are 32-bit elements; how exact they have to be, the bound alone decides.
No kernel may reach another device: no remote copies, remote signals or barrier semaphores. Data moves between devices by JAX's collectives and lax.ppermute only.
A program may use at most 448 MiB of HBM per device.

v0:
```python
import math

import jax
import jax.numpy as jnp
from jax import lax
from jax.sharding import PartitionSpec as P

HEAD = 128
WINDOW = 1024
CAP = 1280


EPSILON = 1e-05
MASKED = -1e30


def norm_scale(values):
    return lax.rsqrt(jnp.mean(values * values, axis=-1, keepdims=True) + EPSILON)


def document_positions(segments):
    index = jnp.broadcast_to(
        jnp.arange(segments.shape[1], dtype=jnp.int32)[None, :], segments.shape
    )
    previous = jnp.concatenate([segments[:, :1] - 1, segments[:, :-1]], axis=1)
    starts = lax.cummax(jnp.where(segments != previous, index, 0), axis=1)
    return index - starts


def rotary_tables(positions, head):
    half = head // 2
    freq = 10000.0 ** (-2.0 * jnp.arange(half, dtype=jnp.float32) / head)
    angle = positions.astype(jnp.float32)[:, None] * freq[None, :]
    return (jnp.cos(angle), jnp.sin(angle))


def rotate(values, cosine, sine):
    half = values.shape[-1] // 2
    first = values[..., :half]
    second = values[..., half:]
    cos_part = cosine[:, None, :]
    sin_part = sine[:, None, :]
    return jnp.concatenate(
        [first * cos_part - second * sin_part, second * cos_part + first * sin_part], axis=-1
    )


def rotate_back(grads, cosine, sine):
    half = grads.shape[-1] // 2
    first = grads[..., :half]
    second = grads[..., half:]
    cos_part = cosine[:, None, :]
    sin_part = sine[:, None, :]
    return jnp.concatenate(
        [first * cos_part + second * sin_part, second * cos_part - first * sin_part], axis=-1
    )


def allowed_mask(segment_row):
    index = jnp.arange(segment_row.shape[0], dtype=jnp.int32)
    distance = index[:, None] - index[None, :]
    return (segment_row[:, None] == segment_row[None, :]) & (distance >= 0) & (distance < WINDOW)


def slot_table(routes, experts, capacity):
    flat = routes.reshape(-1)
    hits = (flat[:, None] == jnp.arange(experts, dtype=jnp.int32)[None, :]).astype(jnp.int32)
    rank = jnp.sum((jnp.cumsum(hits, axis=0, dtype=jnp.int32) - 1) * hits, axis=1, dtype=jnp.int32)
    place = jnp.where(rank < capacity, flat * capacity + rank, experts * capacity)
    pairs = jnp.arange(flat.shape[0], dtype=jnp.int32) + 1
    owner = jnp.zeros((experts * capacity + 1,), jnp.int32).at[place].add(pairs)
    return (place, owner[: experts * capacity] - 1)


def token_slots(routes, place_grid, expert, experts, capacity):
    match = (routes == expert) & (place_grid < experts * capacity)
    rank = place_grid - expert * capacity
    found = jnp.any(match, axis=1).astype(jnp.int32)
    return jnp.sum(jnp.where(match, rank, 0), axis=1, dtype=jnp.int32) + capacity * (1 - found)


def gather_back(rows, slots):
    padded = jnp.concatenate([rows, jnp.zeros((1, rows.shape[1]), rows.dtype)], axis=0)
    return jnp.take(padded, slots, axis=0)


def contract(left, right, left_dim, right_dim):
    return lax.dot_general(
        left, right, (((left_dim,), (right_dim,)), ((), ())), preferred_element_type=jnp.float32
    )


def masked_scores(block_query, block_key, block_segments, scale):
    mask = allowed_mask(block_segments)[None]
    scores = (
        jnp.einsum("qhd,khd->hqk", block_query, block_key, preferred_element_type=jnp.float32)
        * scale
    )
    return jnp.where(mask, scores, MASKED)


def on_device(
    hidden_in,
    cotangent,
    routes,
    segments,
    gain_in,
    w_query,
    w_key,
    w_value,
    w_out,
    gain_query,
    gain_key,
    gain_mid,
    w_router,
    w_gate,
    w_up,
    w_down,
):
    tensor_count = lax.axis_size("tensor")
    tensor_rank = lax.axis_index("tensor")
    tok_rows, width = hidden_in.shape
    local_width = w_query.shape[1]
    heads_here = local_width // HEAD
    full_width = local_width * tensor_count
    seq_count, seq_len = segments.shape
    share = width // tensor_count
    experts = w_gate.shape[0]
    top_count = routes.shape[1]
    scale = 1.0 / math.sqrt(HEAD)
    shaped = (seq_count, seq_len, heads_here, HEAD)
    hidden = hidden_in.astype(jnp.float32)
    in_scale = norm_scale(hidden)
    in_hat = hidden * in_scale
    normed = (in_hat * gain_in.astype(jnp.float32)).astype(jnp.bfloat16)
    query_raw = jnp.dot(normed, w_query, preferred_element_type=jnp.float32)
    key_raw = jnp.dot(normed, w_key, preferred_element_type=jnp.float32)
    value_low = jnp.dot(normed, w_value, preferred_element_type=jnp.float32).astype(jnp.bfloat16)
    square_sums = lax.psum(
        (jnp.sum(query_raw * query_raw, axis=1), jnp.sum(key_raw * key_raw, axis=1)), "tensor"
    )
    query_scale = lax.rsqrt(square_sums[0] / full_width + EPSILON)[:, None]
    key_scale = lax.rsqrt(square_sums[1] / full_width + EPSILON)[:, None]
    query_hat = query_raw * query_scale
    key_hat = key_raw * key_scale
    cosine, sine = rotary_tables(document_positions(segments).reshape(-1), HEAD)
    query_low = rotate(
        (query_hat * gain_query.astype(jnp.float32)).reshape(tok_rows, heads_here, HEAD),
        cosine,
        sine,
    ).astype(jnp.bfloat16)
    key_low = rotate(
        (key_hat * gain_key.astype(jnp.float32)).reshape(tok_rows, heads_here, HEAD), cosine, sine
    ).astype(jnp.bfloat16)

    def forward_block(block):
        block_query, block_key, block_value, block_segments = block
        scores = masked_scores(block_query, block_key, block_segments, scale)
        top = jnp.max(scores, axis=-1, keepdims=True)
        expo = jnp.exp(scores - top)
        total = jnp.sum(expo, axis=-1, keepdims=True)
        weights = (expo / total).astype(jnp.bfloat16)
        out = jnp.einsum("hqk,khd->qhd", weights, block_value, preferred_element_type=jnp.float32)
        return (out, top[..., 0] + jnp.log(total[..., 0]))

    attended, log_totals = lax.map(
        forward_block,
        (query_low.reshape(shaped), key_low.reshape(shaped), value_low.reshape(shaped), segments),
    )
    attended_low = attended.reshape(tok_rows, local_width).astype(jnp.bfloat16)
    branch = lax.psum(contract(attended_low, w_out, 1, 1), "tensor")
    middle = hidden + branch
    mid_scale = norm_scale(middle)
    mid_hat = middle * mid_scale
    mixed = (mid_hat * gain_mid.astype(jnp.float32)).astype(jnp.bfloat16)
    logits = jnp.dot(mixed, w_router, preferred_element_type=jnp.float32)
    router_probs = jax.nn.softmax(logits, axis=-1)
    choice_hits = (
        routes[:, :, None] == jnp.arange(experts, dtype=jnp.int32)[None, None, :]
    ).astype(jnp.float32)
    gates = jnp.sum(router_probs[:, None, :] * choice_hits, axis=-1).reshape(-1)
    place, owner = slot_table(routes, experts, CAP)
    place_grid = place.reshape(tok_rows, top_count)
    owner_safe = jnp.maximum(owner, 0)
    slot_token = (owner_safe // top_count).reshape(experts, CAP)
    slot_gate = jnp.where(owner >= 0, gates[owner_safe], 0.0).reshape(experts, CAP)
    expert_ids = jnp.arange(experts, dtype=jnp.int32)

    def expert_forward(total, item):
        tokens, gate, gate_w, up_w, down_w, expert = item
        rows_in = jnp.take(mixed, tokens, axis=0)
        gate_act = jnp.dot(rows_in, gate_w, preferred_element_type=jnp.float32)
        up_act = jnp.dot(rows_in, up_w, preferred_element_type=jnp.float32)
        inner = (jax.nn.silu(gate_act) * up_act).astype(jnp.bfloat16)
        out = contract(inner, down_w, 1, 1)
        target = jnp.take(cotangent, tokens, axis=0).astype(jnp.float32)
        dots = jnp.sum(out * target, axis=1)
        saved = (dots, gate_act, up_act)
        slots = token_slots(routes, place_grid, expert, experts, CAP)
        return (total + gather_back(out * gate[:, None], slots), saved)

    moe_part, saved = lax.scan(
        expert_forward,
        jnp.zeros((tok_rows, width), jnp.float32),
        (slot_token, slot_gate, w_gate, w_up, w_down, expert_ids),
    )
    moe_share = lax.psum_scatter(moe_part, "tensor", scatter_dimension=1, tiled=True)
    middle_share = lax.dynamic_slice_in_dim(middle, tensor_rank * share, share, 1)
    output = (middle_share + moe_share).astype(jnp.bfloat16)
    gate_totals = lax.psum(saved[0], "tensor")
    pair_grad = jnp.concatenate([gate_totals.reshape(-1), jnp.zeros((1,), jnp.float32)])[place]
    prob_grad = jnp.sum(pair_grad.reshape(tok_rows, top_count)[:, :, None] * choice_hits, axis=1)
    logit_grad = (
        router_probs * (prob_grad - jnp.sum(router_probs * prob_grad, axis=-1, keepdims=True))
    ).astype(jnp.bfloat16)
    router_back = contract(logit_grad, w_router, 1, 1)
    grad_router = contract(mixed, logit_grad, 0, 0)
    stored = (saved[1], saved[2])

    def expert_backward(total, item):
        tokens, gate, gate_w, up_w, down_w, expert, kept = item
        rows_in = jnp.take(mixed, tokens, axis=0)
        gate_act, up_act = kept
        sigmoid_gate = jax.nn.sigmoid(gate_act)
        silu_gate = gate_act * sigmoid_gate
        inner = (silu_gate * up_act).astype(jnp.bfloat16)
        out_grad = (jnp.take(cotangent, tokens, axis=0).astype(jnp.float32) * gate[:, None]).astype(
            jnp.bfloat16
        )
        grad_down = contract(out_grad, inner, 0, 0)
        inner_grad = jnp.dot(out_grad, down_w, preferred_element_type=jnp.float32)
        gate_grad_act = (
            inner_grad * up_act * sigmoid_gate * (1.0 + gate_act * (1.0 - sigmoid_gate))
        ).astype(jnp.bfloat16)
        up_grad_act = (inner_grad * silu_gate).astype(jnp.bfloat16)
        grad_gate_w = contract(rows_in, gate_grad_act, 0, 0)
        grad_up_w = contract(rows_in, up_grad_act, 0, 0)
        grad_rows = contract(gate_grad_act, gate_w, 1, 1) + contract(up_grad_act, up_w, 1, 1)
        slots = token_slots(routes, place_grid, expert, experts, CAP)
        return (total + gather_back(grad_rows, slots), (grad_gate_w, grad_up_w, grad_down))

    mixed_part, expert_grads = lax.scan(
        expert_backward,
        jnp.zeros((tok_rows, width), jnp.float32),
        (slot_token, slot_gate, w_gate, w_up, w_down, expert_ids, stored),
    )
    mixed_grad = lax.psum(mixed_part, "tensor") + router_back
    grad_gain_mid = jnp.sum(mixed_grad * mid_hat, axis=0)
    mid_scaled = mixed_grad * gain_mid.astype(jnp.float32)
    middle_grad = cotangent.astype(jnp.float32) + mid_scale * (
        mid_scaled - mid_hat * jnp.mean(mid_scaled * mid_hat, axis=1, keepdims=True)
    )
    middle_low = middle_grad.astype(jnp.bfloat16)
    grad_w_out = contract(middle_low, attended_low, 0, 0)
    attended_grad = jnp.dot(middle_low, w_out, preferred_element_type=jnp.float32).astype(
        jnp.bfloat16
    )

    def backward_block(block):
        block_query, block_key, block_value, block_segments, block_log, block_grad = block
        scores = masked_scores(block_query, block_key, block_segments, scale)
        probs = jnp.exp(scores - block_log[..., None])
        weights = probs.astype(jnp.bfloat16)
        value_grad = jnp.einsum(
            "hqk,qhd->khd", weights, block_grad, preferred_element_type=jnp.float32
        )
        weight_grad = jnp.einsum(
            "qhd,khd->hqk", block_grad, block_value, preferred_element_type=jnp.float32
        )
        delta = jnp.sum(probs * weight_grad, axis=-1, keepdims=True)
        score_grad = (probs * (weight_grad - delta)).astype(jnp.bfloat16)
        query_grad = (
            jnp.einsum("hqk,khd->qhd", score_grad, block_key, preferred_element_type=jnp.float32)
            * scale
        )
        key_grad = (
            jnp.einsum("hqk,qhd->khd", score_grad, block_query, preferred_element_type=jnp.float32)
            * scale
        )
        return (query_grad, key_grad, value_grad)

    query_rot_grad, key_rot_grad, value_grad = lax.map(
        backward_block,
        (
            query_low.reshape(shaped),
            key_low.reshape(shaped),
            value_low.reshape(shaped),
            segments,
            log_totals,
            attended_grad.reshape(shaped),
        ),
    )
    query_norm_grad = rotate_back(
        query_rot_grad.reshape(tok_rows, heads_here, HEAD), cosine, sine
    ).reshape(tok_rows, local_width)
    key_norm_grad = rotate_back(
        key_rot_grad.reshape(tok_rows, heads_here, HEAD), cosine, sine
    ).reshape(tok_rows, local_width)
    grad_gain_query = jnp.sum(query_norm_grad * query_hat, axis=0)
    grad_gain_key = jnp.sum(key_norm_grad * key_hat, axis=0)
    query_scaled = query_norm_grad * gain_query.astype(jnp.float32)
    key_scaled = key_norm_grad * gain_key.astype(jnp.float32)
    head_totals = lax.psum(
        (jnp.sum(query_scaled * query_hat, axis=1), jnp.sum(key_scaled * key_hat, axis=1)), "tensor"
    )
    query_raw_grad = (
        query_scale * (query_scaled - query_hat * (head_totals[0] / full_width)[:, None])
    ).astype(jnp.bfloat16)
    key_raw_grad = (
        key_scale * (key_scaled - key_hat * (head_totals[1] / full_width)[:, None])
    ).astype(jnp.bfloat16)
    value_grad_low = value_grad.reshape(tok_rows, local_width).astype(jnp.bfloat16)
    grad_w_query = contract(normed, query_raw_grad, 0, 0)
    grad_w_key = contract(normed, key_raw_grad, 0, 0)
    grad_w_value = contract(normed, value_grad_low, 0, 0)
    normed_part = (
        contract(query_raw_grad, w_query, 1, 1)
        + contract(key_raw_grad, w_key, 1, 1)
        + contract(value_grad_low, w_value, 1, 1)
    )
    normed_share = lax.psum_scatter(normed_part, "tensor", scatter_dimension=1, tiled=True)
    in_hat_share = lax.dynamic_slice_in_dim(in_hat, tensor_rank * share, share, 1)
    gain_share = lax.dynamic_slice_in_dim(
        gain_in.astype(jnp.float32), tensor_rank * share, share, 0
    )
    in_scaled = normed_share * gain_share
    row_totals = lax.psum(jnp.sum(in_scaled * in_hat_share, axis=1), "tensor")
    middle_grad_share = lax.dynamic_slice_in_dim(middle_grad, tensor_rank * share, share, 1)
    grad_input = (
        middle_grad_share + in_scale * (in_scaled - in_hat_share * (row_totals / width)[:, None])
    ).astype(jnp.bfloat16)
    grad_gain_in = jnp.sum(normed_share * in_hat_share, axis=0)
    gain_totals = lax.psum((grad_gain_in, grad_gain_query, grad_gain_key), "dp")
    totals = (
        lax.psum_scatter(grad_w_query, "dp", scatter_dimension=0, tiled=True),
        lax.psum_scatter(grad_w_key, "dp", scatter_dimension=0, tiled=True),
        lax.psum_scatter(grad_w_value, "dp", scatter_dimension=0, tiled=True),
        lax.psum_scatter(grad_w_out, "dp", scatter_dimension=0, tiled=True),
        lax.psum_scatter(expert_grads[0], "dp", scatter_dimension=0, tiled=True),
        lax.psum_scatter(expert_grads[1], "dp", scatter_dimension=0, tiled=True),
        lax.psum_scatter(expert_grads[2], "dp", scatter_dimension=0, tiled=True),
        lax.psum_scatter(grad_router, "dp", scatter_dimension=0, tiled=True),
        lax.psum_scatter(grad_gain_mid, "dp", scatter_dimension=0, tiled=True),
    )
    attention_totals = totals[:4]
    expert_totals = totals[4:]
    return (
        output,
        grad_input,
        attention_totals[0],
        attention_totals[1],
        attention_totals[2],
        attention_totals[3],
        gain_totals[0],
        gain_totals[1],
        gain_totals[2],
        expert_totals[4],
        expert_totals[3],
        expert_totals[0],
        expert_totals[1],
        expert_totals[2],
    )


def solution(mesh):
    in_specs = (
        P("dp", None),
        P("dp", None),
        P("dp", None),
        P("dp", None),
        P(),
        P(None, "tensor"),
        P(None, "tensor"),
        P(None, "tensor"),
        P(None, "tensor"),
        P("tensor"),
        P("tensor"),
        P(),
        P(),
        P(None, None, "tensor"),
        P(None, None, "tensor"),
        P(None, None, "tensor"),
    )
    out_specs = (
        P("dp", "tensor"),
        P("dp", "tensor"),
        P("dp", "tensor"),
        P("dp", "tensor"),
        P("dp", "tensor"),
        P("dp", "tensor"),
        P("tensor"),
        P("tensor"),
        P("tensor"),
        P("dp"),
        P("dp", None),
        P("dp", None, "tensor"),
        P("dp", None, "tensor"),
        P("dp", None, "tensor"),
    )
    return jax.shard_map(
        on_device, mesh=mesh, in_specs=in_specs, out_specs=out_specs, check_vma=False
    )
```

profile of v0, /device:TPU:0, one launch (start us, length us, event | category | flops | bytes accessed | tf_op | source)
XLA Modules:
  0.0 5476.0 jit_solution(3717259157589678925)
XLA Ops:
  36.2 39.5 all-reduce.4
  121.5 37.2 while.60
  183.2 85.8 %scatter_custom_fusion = s32[20481]{0:T(1024)S(1)} fusion(s32[16384]{0:T(1024)S(1)} %bitcast.343, s32[16384]{0:T(1024)S(1)} %iota_add_fusion, s32[]{:T(128)} %constant.203.clone.1), kind=kCustom, calls=%fused_computation.248 | custom fusion | flops 16384 | bytes 81928 | tf_op jit(solution)/shard_map/scatter-add | solution.py:71
  269.6 408.5 %all-reduce.10.cloned.1.call-done = f32[2048,2048]{1,0:T(8,128)} async-done(((f32[2048,2048]{1,0:T(8,128)}), f32[2048,2048]{1,0:T(8,128)}) %all-reduce.10.cloned.1.call-update) | async-done | bytes 16777232 | tf_op jit(solution)/shard_map/psum | solution.py:171
  699.8 113.0 %gather_fusion.6 = f32[20480]{0:T(1024)S(1)} fusion(f32[16384]{0:T(1024)S(1)} %reshape.405, s32[20480]{0:T(1024)S(1)} %get-tuple-element.713), kind=kCustom, calls=%fused_computation.6 | custom fusion | bytes 245760 | tf_op jit(solution)/shard_map/gather | solution.py:186
  812.9 1427.5 %while.62 = (s32[]{:T(128)}, f32[2048,2048]{1,0:T(8,128)}, f32[16,1280]{1,0:T(8,128)}, f32[16,1280,128]{2,1,0:T(8,128)}, f32[16,1280,128]{2,1,0:T(8,128)}, /*ind...) while((s32[]{:T(128)}, f32[2048,2048]{1,0:T(8,128)}, ...), condition=%wide.region_24.27_spmd.clone, body=%wide.region_20.26_spmd.clone.sunk | while | flops 2045341696 | bytes 194635088 | solution.py:202
  863.2 20.5 gather_fusion.2
  946.8 20.5 gather_fusion.2
  1036.4 20.5 gather_fusion.2
  1126.0 20.5 gather_fusion.2
  1215.5 20.5 gather_fusion.2
  1305.1 20.5 gather_fusion.2
  1394.6 20.5 gather_fusion.2
  1663.4 20.5 gather_fusion.2
  2200.6 20.5 gather_fusion.2
  2240.4 1579.7 %while.63 = (s32[]{:T(128)}, f32[2048,2048]{1,0:T(8,128)}, f32[16,2048,128]{2,1,0:T(8,128)}, f32[16,2048,128]{2,1,0:T(8,128)}, f32[16,2048,128]{2,1,0:T(8,128)},...) while((s32[]{:T(128)}, f32[2048,2048]{1,0:T(8,128)}, ...), condition=%wide.region_29.32_spmd.clone, body=%wide.region_26.31_spmd.clone.sunk | while | flops 4071224576 | bytes 224631376 | solution.py:242
  2365.9 20.5 gather_fusion.4
  2861.2 20.5 gather_fusion.4
  2960.3 20.5 gather_fusion.4
  3455.6 20.5 gather_fusion.4
  3752.9 20.5 gather_fusion.4
  3821.6 512.1 %all-reduce.12.cloned.1.call-done = (f32[2048,2048]{1,0:T(8,128)}, f32[20480]{0:T(1024)}) async-done(((f32[2048,2048]{1,0:T(8,128)}, f32[20480]{0:T(1024)}), (f32[2048,2048]{1,0:T(8,128)}, f32[20480]{0:T(1024)})) %all-reduce.12.cloned.1.call-update) | async-done | bytes 16859152 | tf_op jit(solution)/shard_map/psum | solution.py:247
  4334.7 90.5 %gather_fusion.7 = f32[16384]{0:T(1024)S(1)} fusion(f32[20481]{0:T(1024)S(1)} %pad_maximum_fusion.4, s32[16384]{0:T(1024)S(1)} %broadcast_clamp_fusion), kind=kCustom, calls=%fused_computation.7 | custom fusion | bytes 196608 | tf_op jit(solution)/shard_map/gather | solution.py:211
  4471.7 67.2 %while.61 = (s32[]{:T(128)}, f32[2,1024,2,128]{3,1,0,2:T(8,128)}, f32[2,1024,2,128]{3,1,0,2:T(8,128)}, bf16[2,1024,2,128]{1,3,2,0:T(8,128)(2,1)}, bf16[2,1024,2,...) while((s32[]{:T(128)}, f32[2,1024,2,128]{3,1,0,2:T(8,128)}, ...), condition=%wide.region_37.40_spmd, body=%wide.region_35.39_spmd.sunk | while | flops 2722625536 | bytes 149493072 | solution.py:282
  4564.3 37.1 all-reduce.3
  4687.1 234.0 %reduce-scatter.13.cloned.1.call-done = f32[2048,256]{1,0:T(8,128)} async-done(((f32[2048,2048]{1,0:T(8,128)}), f32[2048,256]{1,0:T(8,128)}) %reduce-scatter.13.cloned.1.call-update) | async-done | bytes 2097168 | tf_op jit(solution)/shard_map/reduce_scatter | solution.py:321
  4977.2 34.7 reduce-scatter.17.cloned.1.call-done
  5011.9 34.6 reduce-scatter.19.cloned.1.call-done
  5046.5 34.7 reduce-scatter.21.cloned.1.call-done
  5081.3 129.2 %reduce-scatter.25.cloned.1.call-done = f32[4,2048,128]{2,1,0:T(8,128)} async-done(((f32[16,2048,128]{2,1,0:T(8,128)}), f32[4,2048,128]{2,1,0:T(8,128)}) %reduce-scatter.25.cloned.1.call-update) | async-done | bytes 4194320 | tf_op jit(solution)/shard_map/reduce_scatter | solution.py:339
  5210.4 129.5 %reduce-scatter.27.cloned.1.call-done = f32[4,2048,128]{2,1,0:T(8,128)} async-done(((f32[16,2048,128]{2,1,0:T(8,128)}), f32[4,2048,128]{2,1,0:T(8,128)}) %reduce-scatter.27.cloned.1.call-update) | async-done | bytes 4194320 | tf_op jit(solution)/shard_map/reduce_scatter | solution.py:340
  5339.9 129.1 %reduce-scatter.29.cloned.1.call-done = f32[4,2048,128]{2,1,0:T(8,128)} async-done(((f32[16,2048,128]{2,1,0:T(8,128)}), f32[4,2048,128]{2,1,0:T(8,128)}) %reduce-scatter.29.cloned.1.call-update) | async-done | bytes 4194320 | tf_op jit(solution)/shard_map/reduce_scatter | solution.py:341
  (1236 shorter events, 3135.9 us)
Async XLA Ops:
  7.2 25.3 copy-start
  7.2 670.9 %all-reduce.10.cloned.1.call-start = ((), (), s32[]{:S(2)}) async-start(), calls=%async_computation.10 | async-start | bytes 33554432 | tf_op jit(solution)/shard_map/psum | solution.py:171
  32.5 43.3 copy-start.18
  32.5 43.3 copy-start.67
  36.2 47.7 copy-start.43
  36.2 48.7 copy-start.74
  171.2 4162.5 %all-reduce.12.cloned.1.call-start = ((), (), s32[]{:S(2)}) async-start(), calls=%async_computation.21 | async-start | bytes 33718272 | tf_op jit(solution)/shard_map/psum | solution.py:247
  172.3 96.9 %copy-start.72 = (bf16[2048]{0:T(1024)(128)(2,1)S(1)}, bf16[2048]{0:T(1024)(128)(2,1)}, u32[]{:S(2)}) copy-start(bf16[2048]{0:T(1024)(128)(2,1)} %param.39) | copy-start | bytes 12292
  183.2 85.9 %copy-start.47 = (s32[16384,1]{0,1:T(1,128)}, s32[16384,1]{0,1:T(1,128)S(1)}, u32[]{:S(2)}) copy-start(s32[16384,1]{0,1:T(1,128)S(1)} %compare_select_fusion.4) | copy-start | bytes 196612
  269.3 418.0 %copy-start.57 = (f32[2048]{0:T(1024)}, f32[2048]{0:T(1024)S(1)}, u32[]{:S(2)}) copy-start(f32[2048]{0:T(1024)S(1)} %convert_element_type.127) | copy-start | bytes 24580
  698.6 114.2 %copy-start.36 = (f32[2048,16]{0,1:T(8,128)}, f32[2048,16]{0,1:T(8,128)S(1)}, u32[]{:S(2)}) copy-start(f32[2048,16]{0,1:T(8,128)S(1)} %get-tuple-element.722) | copy-start | bytes 393220
  698.6 114.2 %copy-start.49 = (f32[2048]{0:T(1024)}, f32[2048]{0:T(1024)S(1)}, u32[]{:S(2)}) copy-start(f32[2048]{0:T(1024)S(1)} %get-tuple-element.721) | copy-start | bytes 24580
  698.6 114.2 %copy-start.55 = (f32[2048]{0:T(1024)}, f32[2048]{0:T(1024)S(1)}, u32[]{:S(2)}) copy-start(f32[2048]{0:T(1024)S(1)} %fusion.120) | copy-start | bytes 24580
  2240.4 1579.7 %copy-start.63 = (f32[16,1280]{1,0:T(8,128)S(1)}, f32[16,1280]{1,0:T(8,128)}, u32[]{:S(2)}) copy-start(f32[16,1280]{1,0:T(8,128)} %get-tuple-element.283) | copy-start | bytes 245764
  3820.7 862.7 %reduce-scatter.11.cloned.1.call-start = ((), (), s32[]{:S(2)}) async-start(), calls=%async_computation.11 | async-start | bytes 18874368 | tf_op jit(solution)/shard_map/reduce_scatter | solution.py:207
  3821.5 1099.6 %reduce-scatter.13.cloned.1.call-start = ((), (), s32[]{:S(2)}) async-start(), calls=%async_computation.12 | async-start | bytes 18874368 | tf_op jit(solution)/shard_map/reduce_scatter | solution.py:321
  4334.6 91.6 %copy-start.37 = (f32[2048,16]{0,1:T(8,128)S(1)}, f32[2048,16]{0,1:T(8,128)}, u32[]{:S(2)}) copy-start(f32[2048,16]{0,1:T(8,128)} %copy-done.36) | copy-start | bytes 393220
  4334.6 91.6 %copy-start.50 = (f32[2048]{0:T(1024)S(1)}, f32[2048]{0:T(1024)}, u32[]{:S(2)}) copy-start(f32[2048]{0:T(1024)} %copy-done.49) | copy-start | bytes 24580
  4334.6 91.6 %copy-start.56 = (f32[2048]{0:T(1024)S(1)}, f32[2048]{0:T(1024)}, u32[]{:S(2)}) copy-start(f32[2048]{0:T(1024)} %copy-done.55) | copy-start | bytes 24580
  4334.6 91.7 %copy-start.46 = (bf16[2048,16]{0,1:T(8,128)(2,1)S(1)}, bf16[2048,16]{0,1:T(8,128)(2,1)}, u32[]{:S(2)}) copy-start(bf16[2048,16]{0,1:T(8,128)(2,1)} %param.40) | copy-start | bytes 196612
  4334.7 91.7 %copy-start.58 = (f32[2048]{0:T(1024)S(1)}, f32[2048]{0:T(1024)}, u32[]{:S(2)}) copy-start(f32[2048]{0:T(1024)} %copy-done.57) | copy-start | bytes 24580
  4334.7 91.7 %copy-start.60 = (f32[2048]{0:T(1024)S(1)}, f32[2048]{0:T(1024)}, u32[]{:S(2)}) copy-start(f32[2048]{0:T(1024)} %copy-done.59) | copy-start | bytes 24580
  4641.2 318.7 %reduce-scatter.23.cloned.1.call-start = ((), (), s32[]{:S(2)}) async-start(), calls=%async_computation.17 | async-start | bytes 163840 | tf_op jit(solution)/shard_map/reduce_scatter | solution.py:342
  4647.3 329.9 %reduce-scatter.15.cloned.1.call-start = ((), (), s32[]{:S(2)}) async-start(), calls=%async_computation.13 | async-start | bytes 2621440 | tf_op jit(solution)/shard_map/reduce_scatter | solution.py:335
  4654.9 357.1 %reduce-scatter.17.cloned.1.call-start = ((), (), s32[]{:S(2)}) async-start(), calls=%async_computation.14 | async-start | bytes 2621440 | tf_op jit(solution)/shard_map/reduce_scatter | solution.py:336
  4662.4 384.1 %reduce-scatter.19.cloned.1.call-start = ((), (), s32[]{:S(2)}) async-start(), calls=%async_computation.15 | async-start | bytes 2621440 | tf_op jit(solution)/shard_map/reduce_scatter | solution.py:337
  4669.8 411.5 %reduce-scatter.21.cloned.1.call-start = ((), (), s32[]{:S(2)}) async-start(), calls=%async_computation.16 | async-start | bytes 2621440 | tf_op jit(solution)/shard_map/reduce_scatter | solution.py:338
  4679.5 530.9 %reduce-scatter.25.cloned.1.call-start = ((), (), s32[]{:S(2)}) async-start(), calls=%async_computation.18 | async-start | bytes 20971520 | tf_op jit(solution)/shard_map/reduce_scatter | solution.py:339
  4680.1 659.8 %reduce-scatter.27.cloned.1.call-start = ((), (), s32[]{:S(2)}) async-start(), calls=%async_computation.19 | async-start | bytes 20971520 | tf_op jit(solution)/shard_map/reduce_scatter | solution.py:340
  4680.8 788.2 %reduce-scatter.29.cloned.1.call-start = ((), (), s32[]{:S(2)}) async-start(), calls=%async_computation.20 | async-start | bytes 20971520 | tf_op jit(solution)/shard_map/reduce_scatter | solution.py:341
  4681.4 242.4 %copy-start.66 = (f32[2048]{0:T(1024)S(1)}, f32[2048]{0:T(1024)}, u32[]{:S(2)}) copy-start(f32[2048]{0:T(1024)} %get-tuple-element.557) | copy-start | bytes 24580
  4681.4 274.5 %copy-start.65 = (f32[2048]{0:T(1024)S(1)}, f32[2048]{0:T(1024)}, u32[]{:S(2)}) copy-start(f32[2048]{0:T(1024)} %copy-done.64) | copy-start | bytes 24580
  (160 other events, 838.3 us)
Sparse Core Ops, SparseCore 0:
  171.3 506.7 all-reduce.9
  3820.9 512.8 all-reduce.11
  4338.0 282.1 reduce-scatter.10
  4641.3 279.7 reduce-scatter.12
  4924.1 18.6 reduce-scatter.22
  4945.7 31.4 reduce-scatter.14
  4980.5 31.4 reduce-scatter.16
  5015.0 31.4 reduce-scatter.18
  5049.8 31.4 reduce-scatter.20
  5084.3 126.1 reduce-scatter.24
  5213.7 126.0 reduce-scatter.26
  5342.9 126.0 reduce-scatter.28
where the time goes:
time: 5490 us; the launch traced here: 5480 us
  local copies, waits for them, and re-layouts  2140 us (39%)
  waiting for transfers between devices  1670 us (30%)
  other arithmetic  778 us (14%)
  matrix products  744 us (14%)
  blocking collectives  108 us (2%)
    gather x32, local copies, waits for them, and re-layouts, gather_back(): return jnp.take(padded, slots, axis=0)  656 us
    psum x1, waiting for transfers between devices, on_device(): mixed_grad = lax.psum(mixed_part, 'tensor') + router_back  512 us
    dot_general x106, matrix products, contract(): lax.dot_general(left, right, (((left_dim,), (right_dim,)), ((), ())), pre...  450 us
    psum x1, waiting for transfers between devices, on_device(): branch = lax.psum(contract(attended_low, w_out, 1, 1), 'tensor')  409 us
    add x16, other arithmetic, expert_backward(): total + gather_back(grad_rows, slots)  280 us
    add x16, other arithmetic, expert_forward(): return (total + gather_back(out * gate[:, None], slots), saved)  279 us
    gather x16, local copies, waits for them, and re-layouts, expert_forward(): rows_in = jnp.take(mixed, tokens, axis=0)  245 us
    gather x16, local copies, waits for them, and re-layouts, expert_forward(): target = jnp.take(cotangent, tokens, axis=0).astype(jnp.float32)  245 us
  transfers between devices with their start and end apart: 12, of which 10 were waited for; matrix products, arithmetic and copies ran while one was open for 7% of the time, Pallas kernels for 0%

commit v1 on v0

v1 whole, which is shorter than its diff:
```python
import functools
import math

import jax
import jax.numpy as jnp
from jax import lax
from jax.experimental import pallas as pl
from jax.experimental.pallas import tpu as pltpu
from jax.sharding import PartitionSpec as P

HEAD = 128
CAP = 1280
LONGEST = 512
EPSILON = 1e-05
MASKED = -1e30
LANES = 128
MIB = 1 << 20
BF = jnp.bfloat16
F32 = jnp.float32


def norm_scale(values):
    return lax.rsqrt(jnp.mean(values * values, axis=-1, keepdims=True) + EPSILON)


def document_positions(segments):
    index = jnp.broadcast_to(
        jnp.arange(segments.shape[1], dtype=jnp.int32)[None, :], segments.shape
    )
    previous = jnp.concatenate([segments[:, :1] - 1, segments[:, :-1]], axis=1)
    starts = lax.cummax(jnp.where(segments != previous, index, 0), axis=1)
    return index - starts


def rotary_tables(positions, head):
    half = head // 2
    freq = 10000.0 ** (-2.0 * jnp.arange(half, dtype=F32) / head)
    angle = positions.astype(F32)[:, None] * freq[None, :]
    return (jnp.cos(angle), jnp.sin(angle))


def rotate(values, cosine, sine):
    half = values.shape[-1] // 2
    first = values[..., :half]
    second = values[..., half:]
    cos_part = cosine[:, None, :]
    sin_part = sine[:, None, :]
    return jnp.concatenate(
        [first * cos_part - second * sin_part, second * cos_part + first * sin_part], axis=-1
    )


def rotate_back(grads, cosine, sine):
    return rotate(grads, cosine, -sine)


def dot(left, right, left_dim=1, right_dim=0):
    return lax.dot_general(
        left, right, (((left_dim,), (right_dim,)), ((), ())), preferred_element_type=F32
    )


def whole_spec(shape):
    return pl.BlockSpec(
        shape, lambda *_: (0,) * len(shape), pipeline_mode=pl.Buffered(buffer_count=1)
    )


def params(mib):
    return pltpu.CompilerParams(vmem_limit_bytes=mib * MIB)


def cost(flops, moved):
    return pl.CostEstimate(flops=int(flops), bytes_accessed=int(moved), transcendentals=0)


def key_span(block, rows):
    start = max(0, block * rows - LONGEST)
    return start, (block + 1) * rows


def masked_scores(q_rows, k_rows, seg_col, seg_row, row0, key0, scale):
    scores = dot(q_rows, k_rows, 1, 1) * scale
    row = lax.broadcasted_iota(jnp.int32, scores.shape, 0) + row0
    key = lax.broadcasted_iota(jnp.int32, scores.shape, 1) + key0
    return jnp.where((seg_col == seg_row) & (row >= key), scores, MASKED)


def attend_kernel(scale, block, q_ref, k_ref, v_ref, col_ref, row_ref, out_ref):
    length = q_ref.shape[0]
    for index in range(length // block):
        start, stop = key_span(index, block)
        rows = slice(index * block, (index + 1) * block)
        scores = masked_scores(
            q_ref[rows, :],
            k_ref[start:stop, :],
            col_ref[rows, :],
            row_ref[0, :, start:stop],
            index * block,
            start,
            scale,
        )
        expo = jnp.exp(scores - jnp.max(scores, axis=1, keepdims=True))
        weights = (expo / jnp.sum(expo, axis=1, keepdims=True)).astype(BF)
        out_ref[rows, :] = dot(weights, v_ref[start:stop, :]).astype(out_ref.dtype)


def attend_back_kernel(
    scale, block, q_ref, k_ref, v_ref, g_ref, col_ref, row_ref, dq_ref, dk_ref, dv_ref
):
    length = q_ref.shape[0]
    dk_ref[...] = jnp.zeros_like(dk_ref)
    dv_ref[...] = jnp.zeros_like(dv_ref)
    for index in range(length // block):
        start, stop = key_span(index, block)
        rows = slice(index * block, (index + 1) * block)
        q_rows = q_ref[rows, :]
        g_rows = g_ref[rows, :]
        k_rows = k_ref[start:stop, :]
        scores = masked_scores(
            q_rows, k_rows, col_ref[rows, :], row_ref[0, :, start:stop], index * block, start, scale
        )
        expo = jnp.exp(scores - jnp.max(scores, axis=1, keepdims=True))
        probs = expo / jnp.sum(expo, axis=1, keepdims=True)
        weight_grad = dot(g_rows, v_ref[start:stop, :], 1, 1)
        delta = jnp.sum(probs * weight_grad, axis=1, keepdims=True)
        score_grad = (probs * (weight_grad - delta)).astype(BF)
        dv_ref[start:stop, :] += dot(probs.astype(BF), g_rows, 0, 0)
        dk_ref[start:stop, :] += dot(score_grad, q_rows, 0, 0) * scale
        dq_ref[rows, :] = dot(score_grad, k_rows) * scale


def attention_specs(length):
    block = pl.BlockSpec((length, HEAD), lambda seq, head: (seq, head))
    col = pl.BlockSpec((length, 1), lambda seq, head: (seq, 0))
    row = pl.BlockSpec((1, 1, length), lambda seq, head: (seq, 0, 0))
    return block, col, row


def attend(q, k, v, segments, scale):
    seqs, length = segments.shape
    heads = q.shape[1] // HEAD
    block, col, row = attention_specs(length)
    work = seqs * heads * length * length * HEAD
    return pl.pallas_call(
        functools.partial(attend_kernel, scale, min(256, length)),
        grid=(seqs, heads),
        in_specs=[block, block, block, col, row],
        out_specs=block,
        out_shape=jax.ShapeDtypeStruct(q.shape, BF),
        compiler_params=params(48),
        cost_estimate=cost(4 * work, q.size * 8),
        name="attend",
    )(q, k, v, segments.reshape(-1, 1), segments[:, None, :])


def attend_back(q, k, v, grad, segments, scale):
    seqs, length = segments.shape
    heads = q.shape[1] // HEAD
    block, col, row = attention_specs(length)
    work = seqs * heads * length * length * HEAD
    return pl.pallas_call(
        functools.partial(attend_back_kernel, scale, min(256, length)),
        grid=(seqs, heads),
        in_specs=[block, block, block, block, col, row],
        out_specs=[block, block, block],
        out_shape=[jax.ShapeDtypeStruct(q.shape, F32)] * 3,
        compiler_params=params(48),
        cost_estimate=cost(10 * work, q.size * 20),
        name="attend_back",
    )(q, k, v, grad, segments.reshape(-1, 1), segments[:, None, :])


def expert_terms(gate_act, up_act, low_grad, gate):
    sigmoid = 1.0 / (1.0 + jnp.exp(-gate_act))
    silu = gate_act * sigmoid
    inner = (silu * up_act).astype(BF).astype(F32)
    inner_grad = low_grad * gate
    gate_grad = inner_grad * up_act * sigmoid * (1.0 + gate_act * (1.0 - sigmoid))
    return (
        (inner * gate).astype(BF),
        gate_grad.astype(BF),
        (inner_grad * silu).astype(BF),
        inner * low_grad,
    )


def expert_kernel(
    rows,
    mixed_ref,
    dy_ref,
    gates_ref,
    wg_ref,
    wu_ref,
    wd_ref,
    gi_ref,
    gg_ref,
    ug_ref,
    dots_ref,
    both,
    down,
):
    step = pl.program_id(0)
    many, _, hid = wg_ref.shape
    for part in range(many):
        both[:, part * hid : (part + 1) * hid] = wg_ref[part]
        both[:, (many + part) * hid : (many + part + 1) * hid] = wu_ref[part]
        down[:, part * hid : (part + 1) * hid] = wd_ref[part]

    @pl.when(step == 0)
    def _():
        dots_ref[...] = jnp.zeros_like(dots_ref)

    def body(index, carry):
        here = pl.ds(pl.multiple_of(index * rows, rows), rows)
        acts = dot(mixed_ref[here, :], both[...])
        low_grads = dot(dy_ref[here, :], down[...])
        gates = gates_ref[here, :]
        totals = dots_ref[here, :]
        lane = lax.broadcasted_iota(jnp.int32, gates.shape, 1)
        for part in range(many):
            chosen = lane == step * many + part
            gate = jnp.sum(jnp.where(chosen, gates, 0.0), axis=1, keepdims=True)
            span = slice(part * hid, (part + 1) * hid)
            other = slice((many + part) * hid, (many + part + 1) * hid)
            gi, gg, ug, terms = expert_terms(acts[:, span], acts[:, other], low_grads[:, span], gate)
            gi_ref[here, span] = gi
            gg_ref[here, span] = gg
            ug_ref[here, span] = ug
            totals = jnp.where(chosen, jnp.sum(terms, axis=1, keepdims=True), totals)
        dots_ref[here, :] = totals
        return carry

    lax.fori_loop(0, mixed_ref.shape[0] // rows, body, 0)


def expert_acts(mixed, dy, gates, w_gate, w_up, w_down):
    tokens, width = mixed.shape
    experts, _, hid = w_gate.shape
    many = 2
    weight = pl.BlockSpec((many, width, hid), lambda e: (e, 0, 0))
    wide = pl.BlockSpec((tokens, many * hid), lambda e: (0, e))
    wide_shape = jax.ShapeDtypeStruct((tokens, experts * hid), BF)
    return pl.pallas_call(
        functools.partial(expert_kernel, min(256, tokens)),
        grid=(experts // many,),
        in_specs=[
            whole_spec(mixed.shape),
            whole_spec(dy.shape),
            whole_spec(gates.shape),
            weight,
            weight,
            weight,
        ],
        out_specs=[wide, wide, wide, whole_spec(gates.shape)],
        out_shape=[wide_shape, wide_shape, wide_shape, jax.ShapeDtypeStruct(gates.shape, F32)],
        scratch_shapes=[
            pltpu.VMEM((width, 2 * many * hid), BF),
            pltpu.VMEM((width, many * hid), BF),
        ],
        compiler_params=params(58),
        cost_estimate=cost(6 * tokens * width * experts * hid, 12 * tokens * width),
        name="expert_acts",
    )(mixed, dy, gates, w_gate, w_up, w_down)


def back_kernel(rows, count, *refs):
    lefts, weights, out_ref, scratch = refs[:count], refs[count : 2 * count], refs[-1 - count], refs[-count:]
    experts, _, hid = weights[0].shape
    for weight, held in zip(weights, scratch):
        for expert in range(experts):
            held[:, expert * hid : (expert + 1) * hid] = weight[expert]

    def body(index, carry):
        here = pl.ds(pl.multiple_of(index * rows, rows), rows)
        total = dot(lefts[0][here, :], scratch[0][...], 1, 1)
        for left, held in zip(lefts[1:], scratch[1:]):
            total = total + dot(left[here, :], held[...], 1, 1)
        out_ref[here, :] = total
        return carry

    lax.fori_loop(0, out_ref.shape[0] // rows, body, 0)


def experts_back(lefts, weights):
    tokens = lefts[0].shape[0]
    experts, width, hid = weights[0].shape
    count = len(lefts)
    block = min(256, width)
    return pl.pallas_call(
        functools.partial(back_kernel, min(512, tokens), count),
        grid=(width // block,),
        in_specs=[whole_spec(left.shape) for left in lefts]
        + [pl.BlockSpec((experts, block, hid), lambda d: (0, d, 0))] * count,
        out_specs=pl.BlockSpec((tokens, block), lambda d: (0, d)),
        out_shape=jax.ShapeDtypeStruct((tokens, width), F32),
        scratch_shapes=[pltpu.VMEM((block, experts * hid), BF)] * count,
        compiler_params=params(56),
        cost_estimate=cost(
            2 * count * tokens * width * experts * hid, (4 + 4 * count) * tokens * width
        ),
        name="experts_back",
    )(*lefts, *weights)


def grads_kernel(rows, left_ref, *refs):
    count = (len(refs) - 1) // 2
    rights, outs, held = refs[:count], refs[count : 2 * count], refs[-1]
    many, width, hid = outs[0].shape
    for index, right in enumerate(rights):
        held[:, index * many * hid : (index + 1) * many * hid] = right[...]

    def body(index, carry):
        here = pl.ds(pl.multiple_of(index * rows, rows), rows)
        total = dot(left_ref[here, :], held[...])
        for which, out in enumerate(outs):
            for part in range(many):
                place = (which * many + part) * hid
                out[part, here, :] = total[:, place : place + hid]
        return carry

    lax.fori_loop(0, width // rows, body, 0)


def expert_grads(left, rights, experts):
    width, tokens = left.shape
    hid = rights[0].shape[1] // experts
    many = 2
    count = len(rights)
    return pl.pallas_call(
        functools.partial(grads_kernel, min(512, width)),
        grid=(experts // many,),
        in_specs=[whole_spec(left.shape)]
        + [pl.BlockSpec((tokens, many * hid), lambda e: (0, e))] * count,
        out_specs=[pl.BlockSpec((many, width, hid), lambda e: (e, 0, 0))] * count,
        out_shape=[jax.ShapeDtypeStruct((experts, width, hid), F32)] * count,
        scratch_shapes=[pltpu.VMEM((tokens, count * many * hid), BF)],
        compiler_params=params(56),
        cost_estimate=cost(
            2 * count * tokens * width * experts * hid, 6 * count * experts * hid * width
        ),
        name="expert_grads",
    )(left, *rights)


def plain_experts(mixed, dy, gates, w_gate, w_up, w_down):
    acts = jnp.einsum("td,edh->teh", mixed, w_gate, preferred_element_type=F32)
    ups = jnp.einsum("td,edh->teh", mixed, w_up, preferred_element_type=F32)
    low = jnp.einsum("td,edh->teh", dy, w_down, preferred_element_type=F32)
    gi, gg, ug, terms = expert_terms(acts, ups, low, gates[:, :, None])
    flat = (mixed.shape[0], -1)
    return gi.reshape(flat), gg.reshape(flat), ug.reshape(flat), jnp.sum(terms, axis=2)


def plain_back(lefts, weights):
    experts, _, hid = weights[0].shape
    total = 0.0
    for left, weight in zip(lefts, weights):
        total = total + jnp.einsum(
            "teh,edh->td", left.reshape(-1, experts, hid), weight, preferred_element_type=F32
        )
    return total


def plain_grads(left, rights, experts):
    return [
        jnp.einsum(
            "dt,teh->edh",
            left,
            right.reshape(right.shape[0], experts, -1),
            preferred_element_type=F32,
        )
        for right in rights
    ]


def on_device(
    hidden_in,
    cotangent,
    routes,
    segments,
    gain_in,
    w_query,
    w_key,
    w_value,
    w_out,
    gain_query,
    gain_key,
    gain_mid,
    w_router,
    w_gate,
    w_up,
    w_down,
):
    tensor_count = lax.axis_size("tensor")
    tensor_rank = lax.axis_index("tensor")
    tok_rows, width = hidden_in.shape
    local_width = w_query.shape[1]
    heads_here = local_width // HEAD
    full_width = local_width * tensor_count
    share = width // tensor_count
    experts = w_gate.shape[0]
    scale = 1.0 / math.sqrt(HEAD)
    tiled = w_gate.shape[2] % LANES == 0
    acts_of = expert_acts if tiled else plain_experts
    back_of = experts_back if tiled else plain_back
    grads_of = expert_grads if tiled else plain_grads

    hidden = hidden_in.astype(F32)
    in_scale = norm_scale(hidden)
    in_hat = hidden * in_scale
    normed = (in_hat * gain_in.astype(F32)).astype(BF)
    query_raw = dot(normed, w_query)
    key_raw = dot(normed, w_key)
    value_low = dot(normed, w_value).astype(BF)
    square_sums = lax.psum(
        (jnp.sum(query_raw * query_raw, axis=1), jnp.sum(key_raw * key_raw, axis=1)), "tensor"
    )
    query_scale = lax.rsqrt(square_sums[0] / full_width + EPSILON)[:, None]
    key_scale = lax.rsqrt(square_sums[1] / full_width + EPSILON)[:, None]
    query_hat = query_raw * query_scale
    key_hat = key_raw * key_scale
    cosine, sine = rotary_tables(document_positions(segments).reshape(-1), HEAD)

    def turn(values, gain):
        scaled = (values * gain.astype(F32)).reshape(tok_rows, heads_here, HEAD)
        return rotate(scaled, cosine, sine).astype(BF).reshape(tok_rows, local_width)

    query_low = turn(query_hat, gain_query)
    key_low = turn(key_hat, gain_key)
    attended_low = attend(query_low, key_low, value_low, segments, scale)
    branch = lax.psum(dot(attended_low, w_out, 1, 1), "tensor")
    middle = hidden + branch
    mid_scale = norm_scale(middle)
    mid_hat = middle * mid_scale
    mixed = (mid_hat * gain_mid.astype(F32)).astype(BF)
    router_probs = jax.nn.softmax(dot(mixed, w_router), axis=-1)
    expert_ids = jnp.arange(experts, dtype=jnp.int32)
    hits = jnp.any(routes[:, :, None] == expert_ids[None, None, :], axis=1)
    counts = hits.astype(jnp.int32)
    kept = hits & (jnp.cumsum(counts, axis=0, dtype=jnp.int32) - counts < CAP)
    gates = jnp.where(kept, router_probs, 0.0)

    gi, gg, ug, dots = acts_of(mixed, cotangent, gates, w_gate, w_up, w_down)
    mixed_part = back_of([gg, ug], [w_gate, w_up])
    moe_part = back_of([gi], [w_down])
    moe_share = lax.psum_scatter(moe_part, "tensor", scatter_dimension=1, tiled=True)
    middle_share = lax.dynamic_slice_in_dim(middle, tensor_rank * share, share, 1)
    output = (middle_share + moe_share).astype(BF)
    prob_grad = jnp.where(kept, lax.psum(dots.T, "tensor").T, 0.0)
    logit_grad = (
        router_probs * (prob_grad - jnp.sum(router_probs * prob_grad, axis=-1, keepdims=True))
    ).astype(BF)
    router_back = dot(logit_grad, w_router, 1, 1)
    grad_router = dot(mixed, logit_grad, 0, 0)
    grad_gate, grad_up = grads_of(mixed.T, [gg, ug], experts)
    (grad_down,) = grads_of(cotangent.T, [gi], experts)

    mixed_grad = lax.psum(mixed_part, "tensor") + router_back
    grad_gain_mid = jnp.sum(mixed_grad * mid_hat, axis=0)
    mid_scaled = mixed_grad * gain_mid.astype(F32)
    middle_grad = cotangent.astype(F32) + mid_scale * (
        mid_scaled - mid_hat * jnp.mean(mid_scaled * mid_hat, axis=1, keepdims=True)
    )
    middle_low = middle_grad.astype(BF)
    grad_w_out = dot(middle_low, attended_low, 0, 0)
    attended_grad = dot(middle_low, w_out).astype(BF)
    query_rot_grad, key_rot_grad, value_grad = attend_back(
        query_low, key_low, value_low, attended_grad, segments, scale
    )

    def turn_back(grads):
        shaped = grads.reshape(tok_rows, heads_here, HEAD)
        return rotate_back(shaped, cosine, sine).reshape(tok_rows, local_width)

    query_norm_grad = turn_back(query_rot_grad)
    key_norm_grad = turn_back(key_rot_grad)
    grad_gain_query = jnp.sum(query_norm_grad * query_hat, axis=0)
    grad_gain_key = jnp.sum(key_norm_grad * key_hat, axis=0)
    query_scaled = query_norm_grad * gain_query.astype(F32)
    key_scaled = key_norm_grad * gain_key.astype(F32)
    head_totals = lax.psum(
        (jnp.sum(query_scaled * query_hat, axis=1), jnp.sum(key_scaled * key_hat, axis=1)), "tensor"
    )
    query_raw_grad = (
        query_scale * (query_scaled - query_hat * (head_totals[0] / full_width)[:, None])
    ).astype(BF)
    key_raw_grad = (
        key_scale * (key_scaled - key_hat * (head_totals[1] / full_width)[:, None])
    ).astype(BF)
    value_grad_low = value_grad.astype(BF)
    grad_w_query = dot(normed, query_raw_grad, 0, 0)
    grad_w_key = dot(normed, key_raw_grad, 0, 0)
    grad_w_value = dot(normed, value_grad_low, 0, 0)
    normed_part = (
        dot(query_raw_grad, w_query, 1, 1)
        + dot(key_raw_grad, w_key, 1, 1)
        + dot(value_grad_low, w_value, 1, 1)
    )
    normed_share = lax.psum_scatter(normed_part, "tensor", scatter_dimension=1, tiled=True)
    in_hat_share = lax.dynamic_slice_in_dim(in_hat, tensor_rank * share, share, 1)
    gain_share = lax.dynamic_slice_in_dim(gain_in.astype(F32), tensor_rank * share, share, 0)
    in_scaled = normed_share * gain_share
    row_totals = lax.psum(jnp.sum(in_scaled * in_hat_share, axis=1), "tensor")
    middle_grad_share = lax.dynamic_slice_in_dim(middle_grad, tensor_rank * share, share, 1)
    grad_input = (
        middle_grad_share + in_scale * (in_scaled - in_hat_share * (row_totals / width)[:, None])
    ).astype(BF)
    grad_gain_in = jnp.sum(normed_share * in_hat_share, axis=0)
    gain_totals = lax.psum((grad_gain_in, grad_gain_query, grad_gain_key), "dp")

    def over_dp(grad):
        return lax.psum_scatter(grad, "dp", scatter_dimension=0, tiled=True)

    return (
        output,
        grad_input,
        over_dp(grad_w_query),
        over_dp(grad_w_key),
        over_dp(grad_w_value),
        over_dp(grad_w_out),
        gain_totals[0],
        gain_totals[1],
        gain_totals[2],
        over_dp(grad_gain_mid),
        over_dp(grad_router),
        over_dp(grad_gate),
        over_dp(grad_up),
        over_dp(grad_down),
    )


def solution(mesh):
    in_specs = (
        P("dp", None),
        P("dp", None),
        P("dp", None),
        P("dp", None),
        P(),
        P(None, "tensor"),
        P(None, "tensor"),
        P(None, "tensor"),
        P(None, "tensor"),
        P("tensor"),
        P("tensor"),
        P(),
        P(),
        P(None, None, "tensor"),
        P(None, None, "tensor"),
        P(None, None, "tensor"),
    )
    out_specs = (
        P("dp", "tensor"),
        P("dp", "tensor"),
        P("dp", "tensor"),
        P("dp", "tensor"),
        P("dp", "tensor"),
        P("dp", "tensor"),
        P("tensor"),
        P("tensor"),
        P("tensor"),
        P("dp"),
        P("dp", None),
        P("dp", None, "tensor"),
        P("dp", None, "tensor"),
        P("dp", None, "tensor"),
    )
    return jax.shard_map(
        on_device, mesh=mesh, in_specs=in_specs, out_specs=out_specs, check_vma=False
    )
```

time: 5490 us -> 2520 us (0.46)
  local copies, waits for them, and re-layouts: 2140 us -> 132 us
  other arithmetic: 778 us -> 122 us
  matrix products: 744 us -> 125 us
  Pallas kernels: 0 us -> 272 us
  waiting for transfers between devices: 1670 us -> 1740 us
    gather x98 -> x0, local copies, waits for them, and re-layouts: 1840 us -> none  [the longest x32 656 us: gather_back(): return jnp.take(padded, slots, axis=0)]
    dot_general x173 -> x15, matrix products: 744 us -> 125 us  [dot(): lax.dot_general(left, right, (((left_dim,), (right_dim,)), ((), ())), pre...]
    add x35 -> x1, other arithmetic: 581 us -> 20.9 us  [on_device(): cotangent.astype(F32)]
    pallas_call x0 -> x7, Pallas kernels: none -> 272 us  [the longest x1 85.9 us: expert_acts(): pl.pallas_call(functools.partial(expert_kernel, min(256, tokens)), grid=(...]
    concatenate x34 -> x0, local copies, waits for them, and re-layouts: 159 us -> none  [the longest x32 155 us: gather_back(): jnp.concatenate([rows, jnp.zeros((1, rows.shape[1]), rows.dtype)], axis=0)]
    psum x1, waiting for transfers between devices: 409 us -> 495 us  [on_device(): branch = lax.psum(dot(attended_low, w_out, 1, 1), 'tensor')]
    scatter-add x1 -> x0, other arithmetic: 85.8 us -> none  [slot_table(): owner = jnp.zeros((experts * capacity + 1,), jnp.int32).at[place].add(pairs)]
  transfers between devices with their start and end apart: 12 -> 12, of which waited for: 10 -> 10; matrix products, arithmetic and copies ran while one was open for 7% -> 9% of each run, Pallas kernels for 0% -> 5%
where the time goes in v1:
time: 2520 us; the launch traced here: 2510 us
  waiting for transfers between devices  1740 us (69%)
  Pallas kernels  272 us (11%)
  local copies, waits for them, and re-layouts  132 us (5%)
  matrix products  125 us (5%)
  other arithmetic  122 us (5%)
  blocking collectives  106 us (4%)
    reduce_scatter x8, waiting for transfers between devices, over_dp(): return lax.psum_scatter(grad, 'dp', scatter_dimension=0, tiled=True)  508 us
    psum x1, waiting for transfers between devices, on_device(): branch = lax.psum(dot(attended_low, w_out, 1, 1), 'tensor')  495 us
    psum x1, waiting for transfers between devices, on_device(): mixed_grad = lax.psum(mixed_part, 'tensor') + router_back  478 us
    reduce_scatter x1, waiting for transfers between devices, on_device(): lax.psum_scatter(normed_part, 'tensor', scatter_dimension=1, tiled=True)  257 us
    dot_general x15, matrix products, dot(): lax.dot_general(left, right, (((left_dim,), (right_dim,)), ((), ())), pre...  125 us
    pallas_call x1, Pallas kernels, expert_acts(): pl.pallas_call(functools.partial(expert_kernel, min(256, tokens)), grid=(...  85.9 us
    pallas_call x2, Pallas kernels, experts_back(): pl.pallas_call(functools.partial(back_kernel, min(512, tokens), count), g...  85.1 us
    pallas_call x2, Pallas kernels, expert_grads(): pl.pallas_call(functools.partial(grads_kernel, min(512, width)), grid=(ex...  76.1 us
  transfers between devices with their start and end apart: 12, of which 10 were waited for; matrix products, arithmetic and copies ran while one was open for 9% of the time, Pallas kernels for 5%

profile of v1, /device:TPU:0, one launch (start us, length us, event | category | flops | bytes accessed | tf_op | source)
XLA Modules:
  0.0 2511.9 jit_solution(1850423188722756184)
XLA Ops:
  8.7 12.3 copy.103
  40.4 39.2 %all-reduce.2 = (f32[2048]{0:T(1024)S(1)}, f32[2048]{0:T(1024)S(1)}) all-reduce(f32[2048]{0:T(1024)S(1)} %get-tuple-element.131, f32[2048]{0:T(1024)S(1)} %get-tuple-element.133), channel_id=1, replica_groups=mesh['dp'=4,'tensor'=8] {'tensor'}, use_global_device_ids=true, to_apply=%region_2.0 | all-reduce | flops 4096 | bytes 32768 | tf_op jit(solution)/shard_map/psum | solution.py:416
  119.4 9.7 attend.1
  149.7 495.4 %all-reduce.8.cloned.1.call-done = f32[2048,2048]{0,1:T(8,128)} async-done(((f32[2048,2048]{0,1:T(8,128)}), f32[2048,2048]{0,1:T(8,128)}) %all-reduce.8.cloned.1.call-update) | async-done | bytes 16777232 | tf_op jit(solution)/shard_map/psum | solution.py:432
  645.1 9.3 multiply_reduce_fusion.2
  664.6 12.4 copy.115.mixed_ref
  687.6 85.9 %expert_acts.1 = (bf16[2048,2048]{1,0:T(8,128)(2,1)}, bf16[2048,2048]{1,0:T(8,128)(2,1)}, bf16[2048,2048]{1,0:T(8,128)(2,1)}, f32[2048,16]{1,0:T(8,128)}) custom-call(bf16[2048,2048]{1,0:T(8,128)(2,1)} %copy.115.mixed_ref, bf16[2048,2048]{1,0:T(8,128)(2,1)} %dy_ref.1, f32[2048,16]{1,0:T(8,128)} %get-tuple-element.106.gates_ref, ...), custom_call_target="tpu_custom_call" | custom-call | flops 51539607552 | bytes 50331648 | tf_op jit(solution)/shard_map/expert_acts/pallas_call | solution.py:244
  773.5 53.7 %experts_back.3 = f32[2048,2048]{1,0:T(8,128)} custom-call(bf16[2048,2048]{1,0:T(8,128)(2,1)} %get-tuple-element.24.refs_0_, bf16[2048,2048]{1,0:T(8,128)(2,1)} %get-tuple-element.25.refs_1_, bf16[16,2048,128]{2,1,0:T(8,128)(2,1)} %refs_2_.1, bf16[16,2048,128]{2,1,0:T(8,128)(2,1)} %refs_3_.1), custom_call_target="tpu_custom_call" | custom-call | flops 34359738368 | bytes 50331648 | tf_op jit(solution)/shard_map/experts_back/pallas_call | solution.py:290
  827.2 17.6 copy.118
  844.9 31.4 %experts_back.2 = f32[2048,2048]{1,0:T(8,128)} custom-call(bf16[2048,2048]{1,0:T(8,128)(2,1)} %get-tuple-element.23.refs_0_, bf16[16,2048,128]{2,1,0:T(8,128)(2,1)} %refs_1_.1), custom_call_target="tpu_custom_call" | custom-call | flops 17179869184 | bytes 33554432 | tf_op jit(solution)/shard_map/experts_back/pallas_call | solution.py:290
  876.3 17.7 copy.116
  894.0 12.8 copy.117
  906.8 478.0 %all-reduce.10.cloned.1.call-done = (f32[2048,2048]{0,1:T(8,128)}, f32[2048,16]{1,0:T(8,128)}) async-done(((f32[2048,2048]{0,1:T(8,128)}, f32[2048,16]{1,0:T(8,128)}), (f32[2048,2048]{0,1:T(8,128)}, f32[2048,16]{1,0:T(8,128)})) %all-reduce.10.cloned.1.call-update) | async-done | bytes 16908304 | tf_op jit(solution)/shard_map/psum | solution.py:459
  1387.1 21.6 multiply_reduce_fusion
  1408.7 20.9 multiply_add_fusion
  1438.5 15.4 attend_back.1
  1488.3 36.3 %all-reduce.1 = (f32[2048]{0:T(1024)S(1)}, f32[2048]{0:T(1024)S(1)}) all-reduce(f32[2048]{0:T(1024)S(1)} %get-tuple-element.95, f32[2048]{0:T(1024)S(1)} %get-tuple-element.93), channel_id=1, replica_groups=mesh['dp'=4,'tensor'=8] {'tensor'}, use_global_device_ids=true, to_apply=%region_20.21 | all-reduce | flops 4096 | bytes 32768 | tf_op jit(solution)/shard_map/psum | solution.py:482
  1545.5 18.7 add_add_fusion
  1588.4 9.5 fusion.1
  1607.3 9.5 fusion.55.left_ref
  1616.8 47.6 %expert_grads.2 = (f32[16,2048,128]{2,1,0:T(8,128)}, f32[16,2048,128]{2,1,0:T(8,128)}) custom-call(bf16[2048,2048]{1,0:T(8,128)(2,1)} %fusion.55.left_ref, bf16[2048,2048]{1,0:T(8,128)(2,1)} %get-tuple-element.24.refs_0_, bf16[2048,2048]{1,0:T(8,128)(2,1)} %get-tuple-element.25.refs_1_), custom_call_target="tpu_custom_call" | custom-call | flops 34359738368 | bytes 50331648 | tf_op jit(solution)/shard_map/expert_grads/pallas_call | solution.py:330
  1665.2 28.5 %expert_grads.3 = f32[16,2048,128]{2,1,0:T(8,128)} custom-call(bf16[2048,2048]{1,0:T(8,128)(2,1)} %bitcast.94, bf16[2048,2048]{1,0:T(8,128)(2,1)} %get-tuple-element.23.refs_0_), custom_call_target="tpu_custom_call" | custom-call | flops 17179869184 | bytes 25165824 | tf_op jit(solution)/shard_map/expert_grads/pallas_call | solution.py:330
  1699.6 257.2 %reduce-scatter.13.cloned.1.call-done = f32[2048,256]{0,1:T(8,128)} async-done(((f32[2048,2048]{0,1:T(8,128)}), f32[2048,256]{0,1:T(8,128)}) %reduce-scatter.13.cloned.1.call-update) | async-done | bytes 2097168 | tf_op jit(solution)/shard_map/reduce_scatter | solution.py:500
  1959.7 19.7 psum.84
  1985.7 10.7 all-reduce.4
  1997.0 15.9 reduce-scatter.17.cloned.1.call-done
  2012.9 34.6 %reduce-scatter.15.cloned.1.call-done = f32[512,256]{1,0:T(8,128)} async-done(((f32[2048,256]{1,0:T(8,128)}), f32[512,256]{1,0:T(8,128)}) %reduce-scatter.15.cloned.1.call-update) | async-done | bytes 524304 | tf_op jit(solution)/shard_map/reduce_scatter | solution.py:513
  2047.5 34.8 %reduce-scatter.21.cloned.1.call-done = f32[512,256]{1,0:T(8,128)} async-done(((f32[2048,256]{1,0:T(8,128)}), f32[512,256]{1,0:T(8,128)}) %reduce-scatter.21.cloned.1.call-update) | async-done | bytes 524304 | tf_op jit(solution)/shard_map/reduce_scatter | solution.py:513
  2082.2 34.6 %reduce-scatter.19.cloned.1.call-done = f32[512,256]{1,0:T(8,128)} async-done(((f32[2048,256]{1,0:T(8,128)}), f32[512,256]{1,0:T(8,128)}) %reduce-scatter.19.cloned.1.call-update) | async-done | bytes 524304 | tf_op jit(solution)/shard_map/reduce_scatter | solution.py:513
  2116.8 129.4 %reduce-scatter.25.cloned.1.call-done = f32[4,2048,128]{2,1,0:T(8,128)} async-done(((f32[16,2048,128]{2,1,0:T(8,128)}), f32[4,2048,128]{2,1,0:T(8,128)}) %reduce-scatter.25.cloned.1.call-update) | async-done | bytes 4194320 | tf_op jit(solution)/shard_map/reduce_scatter | solution.py:513
  2246.2 129.4 %reduce-scatter.27.cloned.1.call-done = f32[4,2048,128]{2,1,0:T(8,128)} async-done(((f32[16,2048,128]{2,1,0:T(8,128)}), f32[4,2048,128]{2,1,0:T(8,128)}) %reduce-scatter.27.cloned.1.call-update) | async-done | bytes 4194320 | tf_op jit(solution)/shard_map/reduce_scatter | solution.py:513
  2375.5 129.4 %reduce-scatter.29.cloned.1.call-done = f32[4,2048,128]{2,1,0:T(8,128)} async-done(((f32[16,2048,128]{2,1,0:T(8,128)}), f32[4,2048,128]{2,1,0:T(8,128)}) %reduce-scatter.29.cloned.1.call-update) | async-done | bytes 4194320 | tf_op jit(solution)/shard_map/reduce_scatter | solution.py:513
  (225 shorter events, 217.4 us)
Async XLA Ops:
  7.2 26.1 %copy-start = (bf16[2048,256]{1,0:T(8,128)(2,1)S(1)}, bf16[2048,256]{1,0:T(8,128)(2,1)}, u32[]{:S(2)}) copy-start(bf16[2048,256]{1,0:T(8,128)(2,1)} %param.21) | copy-start | bytes 3145732
  7.2 637.9 %all-reduce.8.cloned.1.call-start = ((), (), s32[]{:S(2)}) async-start(), calls=%async_computation.10 | async-start | bytes 33554432 | tf_op jit(solution)/shard_map/psum | solution.py:432
  36.6 43.0 %copy-start.10 = (f32[2048,256]{0,1:T(8,128)}, f32[2048,256]{0,1:T(8,128)S(1)}, u32[]{:S(2)}) copy-start(f32[2048,256]{0,1:T(8,128)S(1)} %get-tuple-element.132) | copy-start | bytes 6291460
  40.4 39.5 %copy-start.46 = (f32[256]{0:T(256)}, f32[256]{0:T(256)S(1)}, u32[]{:S(2)}) copy-start(f32[256]{0:T(256)S(1)} %convert_element_type.82) | copy-start | bytes 3076
  94.0 18.0 slice-start
  99.4 12.7 slice-start.1
  119.4 10.7 copy-start.21
  138.2 1246.6 %all-reduce.10.cloned.1.call-start = ((), (), s32[]{:S(2)}) async-start(), calls=%async_computation.21 | async-start | bytes 35651584 | tf_op jit(solution)/shard_map/psum | solution.py:459
  139.0 515.5 %copy-start.33 = (f32[2048]{0:T(1024)}, f32[2048]{0:T(1024)S(1)}, u32[]{:S(2)}) copy-start(f32[2048]{0:T(1024)S(1)} %convert_element_type.88) | copy-start | bytes 24580
  654.5 10.1 copy-start.35
  664.6 12.4 copy-start.32
  844.8 850.9 %reduce-scatter.11.cloned.1.call-start = ((), (), s32[]{:S(2)}) async-start(), calls=%async_computation.11 | async-start | bytes 18874368 | tf_op jit(solution)/shard_map/reduce_scatter | solution.py:447
  894.0 1062.8 %reduce-scatter.13.cloned.1.call-start = ((), (), s32[]{:S(2)}) async-start(), calls=%async_computation.12 | async-start | bytes 18874368 | tf_op jit(solution)/shard_map/reduce_scatter | solution.py:500
  906.8 480.2 %copy-start.34 = (f32[2048]{0:T(1024)S(1)}, f32[2048]{0:T(1024)}, u32[]{:S(2)}) copy-start(f32[2048]{0:T(1024)} %copy-done.33) | copy-start | bytes 24580
  906.8 480.2 %copy-start.36 = (f32[2048]{0:T(1024)S(1)}, f32[2048]{0:T(1024)}, u32[]{:S(2)}) copy-start(f32[2048]{0:T(1024)} %copy-done.35) | copy-start | bytes 24580
  1408.7 20.9 copy-start.22
  1429.6 8.9 copy-start.4
  1429.6 8.9 copy-start.6
  1529.1 8.2 copy-start.24
  1529.1 8.2 copy-start.27
  1529.1 8.2 copy-start.30
  1537.3 8.2 copy-start.26
  1564.3 432.7 %reduce-scatter.23.cloned.1.call-start = ((), (), s32[]{:S(2)}) async-start(), calls=%async_computation.17 | async-start | bytes 163840 | tf_op jit(solution)/shard_map/reduce_scatter | solution.py:513
  1571.3 441.6 %reduce-scatter.17.cloned.1.call-start = ((), (), s32[]{:S(2)}) async-start(), calls=%async_computation.14 | async-start | bytes 2621440 | tf_op jit(solution)/shard_map/reduce_scatter | solution.py:513
  1578.8 468.6 %reduce-scatter.15.cloned.1.call-start = ((), (), s32[]{:S(2)}) async-start(), calls=%async_computation.13 | async-start | bytes 2621440 | tf_op jit(solution)/shard_map/reduce_scatter | solution.py:513
  1587.2 495.0 %reduce-scatter.21.cloned.1.call-start = ((), (), s32[]{:S(2)}) async-start(), calls=%async_computation.16 | async-start | bytes 2621440 | tf_op jit(solution)/shard_map/reduce_scatter | solution.py:513
  1597.9 518.9 %reduce-scatter.19.cloned.1.call-start = ((), (), s32[]{:S(2)}) async-start(), calls=%async_computation.15 | async-start | bytes 2621440 | tf_op jit(solution)/shard_map/reduce_scatter | solution.py:513
  1607.2 638.9 %reduce-scatter.25.cloned.1.call-start = ((), (), s32[]{:S(2)}) async-start(), calls=%async_computation.18 | async-start | bytes 20971520 | tf_op jit(solution)/shard_map/reduce_scatter | solution.py:513
  1664.4 711.2 %reduce-scatter.27.cloned.1.call-start = ((), (), s32[]{:S(2)}) async-start(), calls=%async_computation.19 | async-start | bytes 20971520 | tf_op jit(solution)/shard_map/reduce_scatter | solution.py:513
  1665.1 839.8 %reduce-scatter.29.cloned.1.call-start = ((), (), s32[]{:S(2)}) async-start(), calls=%async_computation.20 | async-start | bytes 20971520 | tf_op jit(solution)/shard_map/reduce_scatter | solution.py:513
  1956.8 22.6 copy-start.19
  1956.8 22.6 copy-start.43
  (37 other events, 116.2 us)
Sparse Core Ops, SparseCore 0:
  138.3 506.7 all-reduce.7
  845.0 539.8 all-reduce.9
  1388.6 282.2 reduce-scatter.10
  1675.0 281.7 reduce-scatter.12
  1959.7 18.5 reduce-scatter.22
  1981.4 31.4 reduce-scatter.16
  2016.0 31.4 reduce-scatter.14
  2050.7 31.4 reduce-scatter.20
  2085.3 31.4 reduce-scatter.18
  2120.0 126.1 reduce-scatter.24
  2249.3 126.1 reduce-scatter.26
  2378.7 126.1 reduce-scatter.28

commit v2 on v1

v2 whole, which is shorter than its diff:
```python
import functools
import math

import jax
import jax.numpy as jnp
from jax import lax
from jax.experimental import pallas as pl
from jax.experimental.pallas import tpu as pltpu
from jax.sharding import PartitionSpec as P

HEAD = 128
CAP = 1280
LONGEST = 512
EPSILON = 1e-05
MASKED = -1e30
LANES = 128
MIB = 1 << 20
BF = jnp.bfloat16
F32 = jnp.float32


ANY = pl.BlockSpec(memory_space=pl.ANY)


def norm_scale(values):
    return lax.rsqrt(jnp.mean(values * values, axis=-1, keepdims=True) + EPSILON)


def document_positions(segments):
    index = jnp.broadcast_to(
        jnp.arange(segments.shape[1], dtype=jnp.int32)[None, :], segments.shape
    )
    previous = jnp.concatenate([segments[:, :1] - 1, segments[:, :-1]], axis=1)
    starts = lax.cummax(jnp.where(segments != previous, index, 0), axis=1)
    return index - starts


def rotary_tables(positions, head):
    half = head // 2
    freq = 10000.0 ** (-2.0 * jnp.arange(half, dtype=F32) / head)
    angle = positions.astype(F32)[:, None] * freq[None, :]
    return (jnp.cos(angle), jnp.sin(angle))


def dot(left, right, left_dim=1, right_dim=0):
    return lax.dot_general(
        left, right, (((left_dim,), (right_dim,)), ((), ())), preferred_element_type=F32
    )


def whole_spec(shape):
    return pl.BlockSpec(
        shape, lambda *_: (0,) * len(shape), pipeline_mode=pl.Buffered(buffer_count=1)
    )


def params(mib):
    return pltpu.CompilerParams(vmem_limit_bytes=max(mib, 58) * MIB)


def cost(flops, moved, last=False):
    if last:
        flops, moved = 1024, 1024
    return pl.CostEstimate(flops=int(flops), bytes_accessed=int(moved), transcendentals=0)


def across_lanes(row):
    return jnp.broadcast_to(row, (LANES, row.shape[1])).T


def along_lanes(column):
    return jnp.broadcast_to(column, (column.shape[0], LANES)).T[:8]


def project_kernel(x_ref, gain_ref, wq_ref, wk_ref, wv_ref, n_ref, q_ref, k_ref, v_ref, sums_ref):
    x = x_ref[...].astype(F32)
    normed = (x * norm_scale(x) * gain_ref[...].astype(F32)).astype(BF)
    n_ref[...] = normed
    query = dot(normed, wq_ref[...])
    key = dot(normed, wk_ref[...])
    q_ref[...] = query
    k_ref[...] = key
    v_ref[...] = dot(normed, wv_ref[...]).astype(BF)
    q_sum = along_lanes(jnp.sum(query * query, axis=1, keepdims=True))
    k_sum = along_lanes(jnp.sum(key * key, axis=1, keepdims=True))
    first = lax.broadcasted_iota(jnp.int32, q_sum.shape, 0) == 0
    sums_ref[...] = jnp.where(first, q_sum, k_sum)


def project(hidden, gain, w_query, w_key, w_value):
    tokens, width = hidden.shape
    wide = w_query.shape[1]
    rows = min(256, tokens)
    out = pl.BlockSpec((rows, wide), lambda i: (i, 0))
    return pl.pallas_call(
        project_kernel,
        grid=(tokens // rows,),
        in_specs=[pl.BlockSpec((rows, width), lambda i: (i, 0)), whole_spec((1, width))]
        + [whole_spec(w_query.shape)] * 3,
        out_specs=[
            pl.BlockSpec((rows, width), lambda i: (i, 0)),
            out,
            out,
            out,
            pl.BlockSpec((8, rows), lambda i: (0, i)),
        ],
        out_shape=[
            jax.ShapeDtypeStruct((tokens, width), BF),
            jax.ShapeDtypeStruct((tokens, wide), F32),
            jax.ShapeDtypeStruct((tokens, wide), F32),
            jax.ShapeDtypeStruct((tokens, wide), BF),
            jax.ShapeDtypeStruct((8, tokens), F32),
        ],
        compiler_params=params(48),
        cost_estimate=cost(6 * tokens * width * wide, 4 * tokens * width),
        name="project",
    )(hidden, gain.reshape(1, -1), w_query, w_key, w_value)


def key_span(block, rows):
    start = max(0, block * rows - LONGEST)
    return start, (block + 1) * rows


def masked_scores(q_rows, k_rows, seg_col, seg_row, row0, key0, scale):
    scores = dot(q_rows, k_rows, 1, 1) * scale
    row = lax.broadcasted_iota(jnp.int32, scores.shape, 0) + row0
    key = lax.broadcasted_iota(jnp.int32, scores.shape, 1) + key0
    return jnp.where((seg_col == seg_row) & (row >= key), scores, MASKED)


def both_halves(angles):
    other = pltpu.roll(angles, HEAD // 2, 1)
    low = lax.broadcasted_iota(jnp.int32, angles.shape, 1) < HEAD // 2
    return jnp.where(low, angles, other), jnp.where(low, -other, angles)


def turn(values, cosine, sine):
    return values * cosine + pltpu.roll(values, HEAD // 2, 1) * sine


def hat_scale(sums_ref, which, full):
    return lax.rsqrt(across_lanes(sums_ref[which : which + 1, :]) / full + EPSILON)


def attend_kernel(
    scale,
    block,
    full,
    q_ref,
    k_ref,
    v_ref,
    sums_ref,
    gq_ref,
    gk_ref,
    angle_ref,
    col_ref,
    row_ref,
    out_ref,
    ql_ref,
    kl_ref,
):
    length = q_ref.shape[0]
    cosine, sine = both_halves(angle_ref[...])
    for raw, which, gain, low in ((q_ref, 0, gq_ref, ql_ref), (k_ref, 1, gk_ref, kl_ref)):
        hat = raw[...] * hat_scale(sums_ref, which, full)
        low[...] = turn(hat * gain[...].astype(F32), cosine, sine).astype(BF)
    for index in range(length // block):
        start, stop = key_span(index, block)
        rows = slice(index * block, (index + 1) * block)
        scores = masked_scores(
            ql_ref[rows, :],
            kl_ref[start:stop, :],
            col_ref[rows, :],
            row_ref[0, :, start:stop],
            index * block,
            start,
            scale,
        )
        expo = jnp.exp(scores - jnp.max(scores, axis=1, keepdims=True))
        weights = (expo / jnp.sum(expo, axis=1, keepdims=True)).astype(BF)
        out_ref[rows, :] = dot(weights, v_ref[start:stop, :]).astype(BF).astype(F32)


def attend(q, k, v, sums, gains, angles, segments, chunk, scale, full):
    seqs, length = segments.shape
    heads = q.shape[1] // HEAD
    block = pl.BlockSpec((length, HEAD), lambda head: (chunk, head))
    mine = pl.BlockSpec((length, HEAD), lambda head: (0, head))
    gain = pl.BlockSpec((1, HEAD), lambda head: (0, head))
    work = heads * length * length * HEAD
    return pl.pallas_call(
        functools.partial(attend_kernel, scale, min(256, length), full),
        grid=(heads,),
        in_specs=[
            block,
            block,
            block,
            pl.BlockSpec((8, length), lambda head: (0, chunk)),
            gain,
            gain,
            pl.BlockSpec((length, HEAD), lambda head: (chunk, 0)),
            pl.BlockSpec((length, 1), lambda head: (chunk, 0)),
            pl.BlockSpec((1, 1, length), lambda head: (chunk, 0, 0)),
        ],
        out_specs=[mine] * 3,
        out_shape=[jax.ShapeDtypeStruct((length, q.shape[1]), kind) for kind in (F32, BF, BF)],
        compiler_params=params(48),
        cost_estimate=cost(4 * work, length * heads * HEAD * 22),
        name="attend",
    )(q, k, v, sums, *gains, angles, segments.reshape(-1, 1), segments[:, None, :])


def attend_back_kernel(
    scale,
    block,
    full,
    after,
    place_ref,
    q_ref,
    k_ref,
    v_ref,
    grad_ref,
    qr_ref,
    kr_ref,
    sums_ref,
    gq_ref,
    gk_ref,
    angle_ref,
    col_ref,
    row_ref,
    *refs,
):
    qs_ref, ks_ref, dv_out, totals_ref, gains_ref, g_ref, dq_ref, dk_ref, dv_ref = refs[after:]
    length = q_ref.shape[0]
    parts, part_rows, _ = grad_ref.shape
    for part in range(parts):
        here = slice(part * part_rows, (part + 1) * part_rows)
        g_ref[here, :] = grad_ref[place_ref[part]].astype(BF)
    dk_ref[...] = jnp.zeros_like(dk_ref)
    dv_ref[...] = jnp.zeros_like(dv_ref)
    for index in range(length // block):
        start, stop = key_span(index, block)
        rows = slice(index * block, (index + 1) * block)
        q_rows = q_ref[rows, :]
        g_rows = g_ref[rows, :]
        k_rows = k_ref[start:stop, :]
        scores = masked_scores(
            q_rows, k_rows, col_ref[rows, :], row_ref[0, :, start:stop], index * block, start, scale
        )
        expo = jnp.exp(scores - jnp.max(scores, axis=1, keepdims=True))
        probs = expo / jnp.sum(expo, axis=1, keepdims=True)
        weight_grad = dot(g_rows, v_ref[start:stop, :], 1, 1)
        delta = jnp.sum(probs * weight_grad, axis=1, keepdims=True)
        score_grad = (probs * (weight_grad - delta)).astype(BF)
        dv_ref[start:stop, :] += dot(probs.astype(BF), g_rows, 0, 0)
        dk_ref[start:stop, :] += dot(score_grad, q_rows, 0, 0) * scale
        dq_ref[rows, :] = dot(score_grad, k_rows) * scale
    dv_out[...] = dv_ref[...].astype(BF)
    cosine, sine = both_halves(angle_ref[...])
    sums, gains = [], []
    for grad, raw, which, gain, out in (
        (dq_ref, qr_ref, 0, gq_ref, qs_ref),
        (dk_ref, kr_ref, 1, gk_ref, ks_ref),
    ):
        norm_grad = turn(grad[...], cosine, -sine)
        hat = raw[...] * hat_scale(sums_ref, which, full)
        gains.append(jnp.sum(norm_grad * hat, axis=0, keepdims=True))
        scaled = norm_grad * gain[...].astype(F32)
        out[...] = scaled
        sums.append(along_lanes(jnp.sum(scaled * hat, axis=1, keepdims=True)))
    first = lax.broadcasted_iota(jnp.int32, sums[0].shape, 0) == 0
    total = jnp.where(first, sums[0], sums[1])
    if_first = pl.program_id(1) == 0
    totals_ref[...] = jnp.where(if_first, total, totals_ref[...] + total)
    row = lax.broadcasted_iota(jnp.int32, gains_ref.shape, 0)
    gains_ref[...] = jnp.where(row == 0, gains[0], jnp.where(row == 1, gains[1], 0.0))


def attend_back(
    q, k, v, grad, raws, sums, gains, angles, place, segments, scale, full, after=()
):
    seqs, length = segments.shape
    heads = q.shape[1] // HEAD
    block = pl.BlockSpec((length, HEAD), lambda seq, head, _: (seq, head))
    gain = pl.BlockSpec((1, HEAD), lambda seq, head, _: (0, head))
    line = pl.BlockSpec((8, length), lambda seq, head, _: (0, seq))
    work = seqs * heads * length * length * HEAD
    return pl.pallas_call(
        functools.partial(attend_back_kernel, scale, min(256, length), full, len(after)),
        grid_spec=pltpu.PrefetchScalarGridSpec(
            num_scalar_prefetch=1,
            grid=(seqs, heads),
            in_specs=[
                block,
                block,
                block,
                pl.BlockSpec(
                    (grad.shape[0], grad.shape[1] // seqs, HEAD),
                    lambda seq, head, _: (0, seq, head),
                ),
                block,
                block,
                line,
                gain,
                gain,
                pl.BlockSpec((length, HEAD), lambda seq, head, _: (seq, 0)),
                pl.BlockSpec((length, 1), lambda seq, head, _: (seq, 0)),
                pl.BlockSpec((1, 1, length), lambda seq, head, _: (seq, 0, 0)),
            ]
            + [ANY] * len(after),
            out_specs=[
                block,
                block,
                block,
                line,
                pl.BlockSpec((8, HEAD), lambda seq, head, _: (seq, head)),
            ],
            scratch_shapes=[pltpu.VMEM((length, HEAD), BF)]
            + [pltpu.VMEM((length, HEAD), F32)] * 3,
        ),
        out_shape=[
            jax.ShapeDtypeStruct(q.shape, F32),
            jax.ShapeDtypeStruct(q.shape, F32),
            jax.ShapeDtypeStruct(q.shape, BF),
            jax.ShapeDtypeStruct((8, q.shape[0]), F32),
            jax.ShapeDtypeStruct((8 * seqs, q.shape[1]), F32),
        ],
        compiler_params=params(48),
        cost_estimate=cost(10 * work, q.size * 30),
        name="attend_back",
    )(
        place,
        q,
        k,
        v,
        grad,
        *raws,
        sums,
        *gains,
        angles,
        segments.reshape(-1, 1),
        segments[:, None, :],
        *after,
    )


def raw_grads_kernel(full, qs_ref, ks_ref, qr_ref, kr_ref, sums_ref, totals_ref, dq_ref, dk_ref):
    for which, scaled, raw, out in ((0, qs_ref, qr_ref, dq_ref), (1, ks_ref, kr_ref, dk_ref)):
        scale = hat_scale(sums_ref, which, full)
        total = across_lanes(totals_ref[which : which + 1, :]) / full
        out[...] = (scale * (scaled[...] - raw[...] * scale * total)).astype(BF)


def raw_grads(scaled, raws, sums, totals, full):
    tokens, wide = raws[0].shape
    rows = min(512, tokens)
    block = pl.BlockSpec((rows, HEAD), lambda i, head: (i, head))
    line = pl.BlockSpec((8, rows), lambda i, head: (0, i))
    return pl.pallas_call(
        functools.partial(raw_grads_kernel, full),
        grid=(tokens // rows, wide // HEAD),
        in_specs=[block] * 4 + [line] * 2,
        out_specs=[block] * 2,
        out_shape=[jax.ShapeDtypeStruct((tokens, wide), BF)] * 2,
        compiler_params=params(48),
        cost_estimate=cost(0, 20 * tokens * wide),
        name="raw_grads",
    )(*scaled, *raws, sums, totals)


def expert_terms(gate_act, up_act, low_grad, gate):
    sigmoid = 1.0 / (1.0 + jnp.exp(-gate_act))
    silu = gate_act * sigmoid
    inner = (silu * up_act).astype(BF).astype(F32)
    inner_grad = low_grad * gate
    gate_grad = inner_grad * up_act * sigmoid * (1.0 + gate_act * (1.0 - sigmoid))
    return (
        (inner * gate).astype(BF),
        gate_grad.astype(BF),
        (inner_grad * silu).astype(BF),
        inner * low_grad,
    )


def expert_kernel(rows, after, mixed_ref, dy_ref, gates_ref, wg_ref, wu_ref, wd_ref, *refs):
    gi_ref, gg_ref, ug_ref, dots_ref, both, down = refs[after:]
    step = pl.program_id(0)
    many, _, hid = wg_ref.shape
    for part in range(many):
        both[:, part * hid : (part + 1) * hid] = wg_ref[part]
        both[:, (many + part) * hid : (many + part + 1) * hid] = wu_ref[part]
        down[:, part * hid : (part + 1) * hid] = wd_ref[part]

    @pl.when(step == 0)
    def _():
        dots_ref[...] = jnp.zeros_like(dots_ref)

    def body(index, carry):
        here = pl.ds(pl.multiple_of(index * rows, rows), rows)
        acts = dot(mixed_ref[here, :], both[...])
        low_grads = dot(dy_ref[here, :], down[...])
        gates = gates_ref[here, :]
        totals = dots_ref[here, :]
        lane = lax.broadcasted_iota(jnp.int32, gates.shape, 1)
        spot = lax.broadcasted_iota(jnp.int32, totals.shape, 1)
        for part in range(many):
            chosen = lane == step * many + part
            gate = jnp.sum(jnp.where(chosen, gates, 0.0), axis=1, keepdims=True)
            span = slice(part * hid, (part + 1) * hid)
            other = slice((many + part) * hid, (many + part + 1) * hid)
            gi, gg, ug, terms = expert_terms(acts[:, span], acts[:, other], low_grads[:, span], gate)
            gi_ref[here, span] = gi
            gg_ref[here, span] = gg
            ug_ref[here, span] = ug
            mine = spot == step * many + part
            totals = jnp.where(mine, jnp.sum(terms, axis=1, keepdims=True), totals)
        dots_ref[here, :] = totals
        return carry

    lax.fori_loop(0, mixed_ref.shape[0] // rows, body, 0)


def expert_acts(mixed, dy, chunk, gates, w_gate, w_up, w_down, after=(), last=False):
    tokens, width = mixed.shape
    experts, _, hid = w_gate.shape
    many = 2
    weight = pl.BlockSpec((many, width, hid), lambda e: (e, 0, 0))
    wide = pl.BlockSpec((tokens, many * hid), lambda e: (0, e))
    wide_shape = jax.ShapeDtypeStruct((tokens, experts * hid), BF)
    return pl.pallas_call(
        functools.partial(expert_kernel, min(256, tokens), len(after)),
        grid=(experts // many,),
        in_specs=[
            whole_spec(mixed.shape),
            pl.BlockSpec(
                mixed.shape, lambda e: (chunk, 0), pipeline_mode=pl.Buffered(buffer_count=1)
            ),
            whole_spec(gates.shape),
            weight,
            weight,
            weight,
        ]
        + [ANY] * len(after),
        out_specs=[wide, wide, wide, whole_spec((tokens, LANES))],
        out_shape=[wide_shape, wide_shape, wide_shape, jax.ShapeDtypeStruct((tokens, LANES), F32)],
        scratch_shapes=[
            pltpu.VMEM((width, 2 * many * hid), BF),
            pltpu.VMEM((width, many * hid), BF),
        ],
        compiler_params=params(58),
        cost_estimate=cost(6 * tokens * width * experts * hid, 12 * tokens * width, last),
        name="expert_acts",
    )(mixed, dy, gates, w_gate, w_up, w_down, *after)


def fill(held, weight):
    experts, _, hid = weight.shape
    for expert in range(experts):
        held[:, expert * hid : (expert + 1) * hid] = weight[expert]


def back_columns_kernel(rows, count, extra, after, table_ref, rank_ref, *refs):
    lefts, weights = refs[:count], refs[count : 2 * count]
    more = refs[2 * count : 2 * count + extra]
    refs = refs[2 * count + extra + after :]
    outs, held = refs[:-count], refs[-count:]
    step = pl.program_id(0)
    for index in range(count):
        fill(held[index], weights[index])
    places = [out.at[part] for out in outs for part in range(out.shape[0])]
    for number, out_ref in enumerate(places):

        @pl.when(step == number)
        def _(out_ref=out_ref):
            def body(index, carry):
                here = pl.ds(pl.multiple_of(index * rows, rows), rows)
                total = dot(lefts[0][here, :], held[0][...], 1, 1)
                for left, right in zip(lefts[1:], held[1:]):
                    total = total + dot(left[here, :], right[...], 1, 1)
                out_ref[here, :] = total
                return carry

            lax.fori_loop(0, out_ref.shape[0] // rows, body, 0)
            for added in more:
                own = added.shape[0]
                out_ref[pl.ds(pl.multiple_of(rank_ref[0] * own, own), own), :] += added[...]


def back_columns(
    lefts, weights, table, groups, after=(), last=False, rank=None, added=(), chunk=0
):
    rank = jnp.zeros((1,), jnp.int32) if rank is None else rank.reshape(1)
    table = table[jnp.array([k for group in groups for k in group], jnp.int32)]
    tokens = lefts[0].shape[0]
    experts, width, hid = weights[0].shape
    count, parts = len(lefts), table.shape[0]
    block = width // parts
    return pl.pallas_call(
        functools.partial(
            back_columns_kernel, min(512, tokens), count, len(added), len(after)
        ),
        grid_spec=pltpu.PrefetchScalarGridSpec(
            num_scalar_prefetch=2,
            grid=(parts,),
            in_specs=[whole_spec(left.shape) for left in lefts]
            + [pl.BlockSpec((experts, block, hid), lambda d, table, _: (0, table[d], 0))] * count
            + [
                pl.BlockSpec((tokens // parts, block), lambda d, table, _: (chunk, table[d]))
                for item in added
            ]
            + [ANY] * len(after),
            out_specs=[whole_spec((len(group), tokens, block)) for group in groups],
            scratch_shapes=[pltpu.VMEM((block, experts * hid), BF)] * count,
        ),
        out_shape=[jax.ShapeDtypeStruct((len(group), tokens, block), F32) for group in groups],
        compiler_params=params(56),
        cost_estimate=cost(
            2 * count * tokens * width * experts * hid, (4 + 4 * count) * tokens * width, last
        ),
        name="back_columns",
    )(table, rank, *lefts, *weights, *added, *after)


def back_rows_kernel(rows, count, after, table_ref, *refs):
    lefts, weights, dots_ref = refs[:count], refs[count : 2 * count], refs[2 * count]
    refs = refs[2 * count + 1 + after :]
    outs, held, turned = refs[: -2 * count], refs[-2 * count : -count], refs[-count:]
    outs = [out.at[part] for out in outs for part in range(out.shape[0])]
    part_rows = outs[0].shape[0]
    block = held[0].shape[0]
    width = outs[0].shape[1] - LANES
    for index in range(count):
        fill(held[index], weights[index])

    @pl.when(pl.program_id(0) == 0)
    def _():
        for number in range(len(outs)):
            here = pl.ds(pl.multiple_of(table_ref[number] * part_rows, part_rows), part_rows)
            there = slice(number * part_rows, (number + 1) * part_rows)
            for index in range(count):
                turned[index][there, :] = lefts[index][here, :]
            outs[number][:, width:] = dots_ref[here, :]

    columns = pl.ds(pl.multiple_of(pl.program_id(0) * block, block), block)
    for step in range(len(outs) * part_rows // rows):
        here = slice(step * rows, (step + 1) * rows)
        total = dot(turned[0][here, :], held[0][...], 1, 1)
        for left, right in zip(turned[1:], held[1:]):
            total = total + dot(left[here, :], right[...], 1, 1)
        for part in range(rows // part_rows):
            number = step * (rows // part_rows) + part
            outs[number][:, columns] = total[part * part_rows : (part + 1) * part_rows]


def back_rows(lefts, weights, dots, table, groups, after=()):
    table = table[jnp.array([k for group in groups for k in group], jnp.int32)]
    tokens = lefts[0].shape[0]
    experts, width, hid = weights[0].shape
    count, parts = len(lefts), table.shape[0]
    block = min(256, width)
    part_rows = tokens // parts
    return pl.pallas_call(
        functools.partial(back_rows_kernel, min(512, tokens), count, len(after)),
        grid_spec=pltpu.PrefetchScalarGridSpec(
            num_scalar_prefetch=1,
            grid=(width // block,),
            in_specs=[whole_spec(left.shape) for left in lefts]
            + [pl.BlockSpec((experts, block, hid), lambda d, _: (0, d, 0))] * count
            + [whole_spec(dots.shape)]
            + [ANY] * len(after),
            out_specs=[whole_spec((len(group), part_rows, width + LANES)) for group in groups],
            scratch_shapes=[pltpu.VMEM((block, experts * hid), BF)] * count
            + [pltpu.VMEM(left.shape, BF) for left in lefts],
        ),
        out_shape=[
            jax.ShapeDtypeStruct((len(group), part_rows, width + LANES), F32) for group in groups
        ],
        compiler_params=params(56),
        cost_estimate=cost(
            2 * count * tokens * width * experts * hid, (4 + 4 * count) * tokens * width
        ),
        name="back_rows",
    )(table, *lefts, *weights, dots, *after)


def grads_kernel(rows, chunks, after, *refs):
    lefts = refs[:chunks]
    rest = refs[chunks + after :]
    count = (len(rest) - 2 * chunks) // (chunks + 1)
    rights = [rest[c * count : (c + 1) * count] for c in range(chunks)]
    outs = rest[chunks * count : (chunks + 1) * count]
    held, turned = rest[(chunks + 1) * count : -chunks], rest[-chunks:]
    many, width, hid = outs[0].shape

    @pl.when(pl.program_id(0) == 0)
    def _():
        for chunk in range(chunks):
            wide = 256
            for start in range(0, width, wide):
                turned[chunk][start : start + wide, :] = lefts[chunk][:, start : start + wide].T

    for chunk in range(chunks):
        for index, right in enumerate(rights[chunk]):
            held[chunk][:, index * many * hid : (index + 1) * many * hid] = right[...]

    def body(index, carry):
        here = pl.ds(pl.multiple_of(index * rows, rows), rows)
        total = dot(turned[0][here, :], held[0][...])
        for chunk in range(1, chunks):
            total = total + dot(turned[chunk][here, :], held[chunk][...])
        for which, out in enumerate(outs):
            for part in range(many):
                place = (which * many + part) * hid
                out[part, here, :] = total[:, place : place + hid]
        return carry

    lax.fori_loop(0, width // rows, body, 0)


def expert_grads(lefts, rights, experts, after=()):
    chunks, count = len(rights), len(rights[0])
    tokens = rights[0][0].shape[0]
    width = lefts[0].shape[1]
    hid = rights[0][0].shape[1] // experts
    many = 2
    if len(lefts) == chunks:
        left_specs = [whole_spec(left.shape) for left in lefts]
    else:
        left_specs = [
            pl.BlockSpec(
                (tokens, width),
                lambda e, chunk=chunk: (chunk, 0),
                pipeline_mode=pl.Buffered(buffer_count=1),
            )
            for chunk in range(chunks)
        ]
        lefts = list(lefts) * chunks
    return pl.pallas_call(
        functools.partial(grads_kernel, min(512, width), chunks, len(after)),
        grid=(experts // many,),
        in_specs=left_specs
        + [ANY] * len(after)
        + [pl.BlockSpec((tokens, many * hid), lambda e: (0, e))] * (count * chunks),
        out_specs=[pl.BlockSpec((many, width, hid), lambda e: (e, 0, 0))] * count,
        out_shape=[jax.ShapeDtypeStruct((experts, width, hid), F32)] * count,
        scratch_shapes=[pltpu.VMEM((tokens, count * many * hid), BF)] * chunks
        + [pltpu.VMEM((width, tokens), BF)] * chunks,
        compiler_params=params(58),
        cost_estimate=cost(
            2 * count * chunks * tokens * width * experts * hid, 6 * count * experts * hid * width
        ),
        name="expert_grads",
    )(*lefts, *after, *[item for chunk in rights for item in chunk])


def branch_kernel(count, after, table_ref, *refs):
    pieces = refs[:count]
    w_ref, x_ref, gain_ref, router_ref = refs[count : count + 4]
    mid_ref, mixed_ref, logit_ref, all_ref = refs[count + 4 + after :]
    share = pieces[0].shape[1]
    for index, piece in enumerate(pieces):
        span = pl.ds(pl.multiple_of(table_ref[index] * share, LANES), share)
        all_ref[:, span] = piece[...].astype(BF)
    middle = x_ref[...].astype(F32) + dot(all_ref[...], w_ref[...], 1, 1)
    mid_ref[...] = middle
    mid_hat = middle * norm_scale(middle)
    mixed = (mid_hat * gain_ref[...].astype(F32)).astype(BF)
    mixed_ref[...] = mixed
    logit_ref[...] = dot(mixed, router_ref[...])


def branch(pieces, table, w_out, hidden, chunk, gain, w_router, after=()):
    tokens, share = pieces[0].shape
    width, full = w_out.shape
    rows = min(256, tokens)
    steps = tokens // rows
    experts = w_router.shape[1]
    return pl.pallas_call(
        functools.partial(branch_kernel, len(pieces), len(after)),
        grid_spec=pltpu.PrefetchScalarGridSpec(
            num_scalar_prefetch=1,
            grid=(steps,),
            in_specs=[pl.BlockSpec((rows, share), lambda i, _: (i, 0))] * len(pieces)
            + [
                whole_spec(w_out.shape),
                pl.BlockSpec((rows, width), lambda i, _: (chunk * steps + i, 0)),
                whole_spec((1, width)),
                whole_spec(w_router.shape),
            ]
            + [ANY] * len(after),
            out_specs=[
                pl.BlockSpec((rows, width), lambda i, _: (i, 0)),
                pl.BlockSpec((rows, width), lambda i, _: (i, 0)),
                pl.BlockSpec((rows, experts), lambda i, _: (i, 0)),
                pl.BlockSpec((rows, full), lambda i, _: (i, 0)),
            ],
        ),
        out_shape=[
            jax.ShapeDtypeStruct((tokens, width), F32),
            jax.ShapeDtypeStruct((tokens, width), BF),
            jax.ShapeDtypeStruct((tokens, experts), F32),
            jax.ShapeDtypeStruct((tokens, full), BF),
        ],
        compiler_params=params(56),
        cost_estimate=cost(2 * tokens * width * full, 16 * tokens * width),
        name="branch",
    )(table, *pieces, w_out, hidden, gain.reshape(1, -1), w_router, *after)


def cast_kernel(in_ref, out_ref):
    out_ref[...] = in_ref[...].astype(out_ref.dtype)


def cast(value):
    rows, columns = value.shape
    block = pl.BlockSpec((min(256, rows), columns), lambda i: (i, 0))
    return pl.pallas_call(
        cast_kernel,
        grid=(rows // min(256, rows),),
        in_specs=[block],
        out_specs=block,
        out_shape=jax.ShapeDtypeStruct(value.shape, BF),
        compiler_params=params(32),
        cost_estimate=cost(0, 6 * value.size),
        name="cast",
    )(value)


def send_back_kernel(after, table_ref, low_ref, w_ref, *outs):
    for number, out_ref in enumerate(outs[after:]):

        @pl.when(pl.program_id(0) == number)
        def _(out_ref=out_ref):
            out_ref[...] = dot(low_ref[...], w_ref[...]).astype(BF).astype(F32)


def send_back(low, w_out, table, after=()):
    rows, width = low.shape
    parts = table.shape[0]
    full = w_out.shape[1]
    block = full // parts
    return pl.pallas_call(
        functools.partial(send_back_kernel, len(after)),
        grid_spec=pltpu.PrefetchScalarGridSpec(
            num_scalar_prefetch=1,
            grid=(parts,),
            in_specs=[
                whole_spec(low.shape),
                pl.BlockSpec((width, block), lambda k, table: (0, table[k])),
            ]
            + [ANY] * len(after),
            out_specs=[whole_spec((rows, block))] * parts,
        ),
        out_shape=[jax.ShapeDtypeStruct((rows, block), F32)] * parts,
        compiler_params=params(32),
        cost_estimate=cost(2 * rows * width * full, 2 * width * full + 8 * rows * full),
        name="send_back",
    )(table, low, w_out, *after)


def outer_kernel(after, table_ref, columns_ref, left_ref, right_ref, *outs):
    for number, out_ref in enumerate(outs[after:]):

        @pl.when(pl.program_id(0) == number)
        def _(out_ref=out_ref):
            out_ref[0] = dot(left_ref[...], right_ref[...])


def outer(left, right, table, columns, after=()):
    width, rows = left.shape
    parts, pieces = table.shape[0], columns.shape[0]
    high, wide = width // parts, right.shape[1] // pieces
    out_specs = [
        pl.BlockSpec(
            (1, high, wide),
            lambda k, m, *_, number=number: (
                jnp.where(k < number, 0, jnp.where(k > number, pieces - 1, m)),
                0,
                0,
            ),
        )
        for number in range(parts)
    ]
    return pl.pallas_call(
        functools.partial(outer_kernel, len(after)),
        grid_spec=pltpu.PrefetchScalarGridSpec(
            num_scalar_prefetch=2,
            grid=(parts, pieces),
            in_specs=[
                pl.BlockSpec((high, rows), lambda k, m, table, columns: (table[k], 0)),
                pl.BlockSpec((rows, wide), lambda k, m, table, columns: (0, columns[m])),
            ]
            + [ANY] * len(after),
            out_specs=out_specs,
        ),
        out_shape=[jax.ShapeDtypeStruct((pieces, high, wide), F32)] * parts,
        compiler_params=params(32),
        cost_estimate=cost(2 * width * rows * right.shape[1], 4 * width * right.shape[1]),
        name="outer",
    )(table, columns, left, right, *after)


def plain_acts(mixed, dy, chunk, gates, w_gate, w_up, w_down, after=(), last=False):
    dy = lax.dynamic_slice_in_dim(dy, chunk * mixed.shape[0], mixed.shape[0], 0)
    acts = jnp.einsum("td,edh->teh", mixed, w_gate, preferred_element_type=F32)
    ups = jnp.einsum("td,edh->teh", mixed, w_up, preferred_element_type=F32)
    low = jnp.einsum("td,edh->teh", dy, w_down, preferred_element_type=F32)
    gi, gg, ug, terms = expert_terms(acts, ups, low, gates[:, :, None])
    flat = (mixed.shape[0], -1)
    dots = jnp.pad(jnp.sum(terms, axis=2), ((0, 0), (0, LANES - gates.shape[1])))
    return gi.reshape(flat), gg.reshape(flat), ug.reshape(flat), dots


def plain_back(lefts, weights):
    experts, _, hid = weights[0].shape
    total = 0.0
    for left, weight in zip(lefts, weights):
        total = total + jnp.einsum(
            "teh,edh->td", left.reshape(-1, experts, hid), weight, preferred_element_type=F32
        )
    return total


def plain_columns(
    lefts, weights, table, groups, after=(), last=False, rank=None, added=(), chunk=0
):
    total = plain_back(lefts, weights)
    for item in added:
        own = total.shape[0] // table.shape[0]
        mine = lax.slice_in_dim(item, chunk * own, (chunk + 1) * own, axis=0)
        rows = lax.dynamic_slice_in_dim(total, rank * own, own, 0) + mine
        total = lax.dynamic_update_slice_in_dim(total, rows, rank * own, 0)
    block = total.shape[1] // table.shape[0]
    return [
        jnp.stack([lax.dynamic_slice_in_dim(total, table[k] * block, block, 1) for k in group])
        for group in groups
    ]


def plain_rows(lefts, weights, dots, table, groups, after=()):
    total = jnp.concatenate([plain_back(lefts, weights), dots], axis=1)
    block = total.shape[0] // table.shape[0]
    return [
        jnp.stack([lax.dynamic_slice_in_dim(total, table[k] * block, block, 0) for k in group])
        for group in groups
    ]


def plain_grads(lefts, rights, experts, after=()):
    left = jnp.concatenate(lefts, axis=0)
    return [
        jnp.einsum(
            "td,teh->edh",
            left,
            jnp.concatenate(parts, axis=0).reshape(left.shape[0], experts, -1),
            preferred_element_type=F32,
        )
        for parts in zip(*rights)
    ]


def bits_of(count):
    if count & (count - 1):
        raise ValueError("tensor axis")
    return [1 << bit for bit in range(count.bit_length() - 1)]


def swap(value, axis, step):
    count = lax.axis_size(axis)
    return lax.ppermute(value, axis, [(i, i ^ step) for i in range(count)])


def reduce_blocks(blocks, axis="tensor"):
    blocks = list(blocks)
    live = list(range(len(blocks)))
    for bit in bits_of(len(blocks)):
        for k in sorted((k for k in live if k & bit), reverse=True):
            blocks[k ^ bit] = blocks[k ^ bit] + swap(blocks[k], axis, bit)
        live = [k for k in live if not k & bit]
    return blocks[0]


def stage_kernel(sizes, skip, *refs):
    count = sum(sizes)
    terms = refs[:count]
    outs = list(refs[count + skip :])
    used = 0
    for size in sizes:
        total = terms[used][...]
        for term in terms[used + 1 : used + size]:
            total = total + term[...]
        used += size
        done = 0
        while done < total.shape[0]:
            out = outs.pop(0)
            out[...] = total[done : done + out.shape[0]]
            done += out.shape[0]


def stage(sums, passes=(), after=()):
    steps = 4
    terms = [term for _, group in sums for term in group]
    in_specs, out_specs, out_shape = [], [], []
    for term in terms:
        parts, rows, columns = term.shape
        in_specs.append(pl.BlockSpec((parts, rows // steps, columns), lambda i: (0, i, 0)))
    for cuts, group in sums:
        _, rows, columns = group[0].shape
        for parts in cuts:
            out_specs.append(pl.BlockSpec((parts, rows // steps, columns), lambda i: (0, i, 0)))
            out_shape.append(jax.ShapeDtypeStruct((parts, rows, columns), F32))
    made = len(out_shape)
    out_shape += [jax.ShapeDtypeStruct(item.shape, item.dtype) for item in passes]
    outs = pl.pallas_call(
        functools.partial(
            stage_kernel, tuple(len(group) for _, group in sums), len(passes) + len(after)
        ),
        grid=(steps,),
        in_specs=in_specs + [ANY] * (len(passes) + len(after)),
        out_specs=out_specs + [ANY] * len(passes),
        out_shape=out_shape,
        input_output_aliases={len(terms) + i: made + i for i in range(len(passes))},
        compiler_params=params(32),
        cost_estimate=cost(0, sum(4 * term.size for term in terms) * 4 // 3),
        name="stage",
    )(*terms, *passes, *after)
    return outs[:made], outs[made:]


def tie_kernel(*refs):
    pass


def tie(values, after):
    return pl.pallas_call(
        tie_kernel,
        in_specs=[ANY] * (len(values) + len(after)),
        out_specs=[ANY] * len(values),
        out_shape=[jax.ShapeDtypeStruct(value.shape, value.dtype) for value in values],
        input_output_aliases={i: i for i in range(len(values))},
        compiler_params=params(58),
        name="tie",
    )(*values, *after)


class Chain:
    groups = ((7, 3), (5, 1), (6, 2), (4, 0))

    def __init__(self, parts):
        self.first, self.second, self.six_two, self.four_zero = parts

    def send_first(self):
        self.got_first = swap(self.first, "tensor", 1)

    def send_second(self):
        self.got_second = swap(self.second, "tensor", 1)
        self.got_near = swap(self.six_two, "tensor", 2)

    def send_far(self):
        self.got_far = swap(self.four, "tensor", 4)


def odd_stage(ending, starting, passes=(), after=(), hold=False):
    sums = []
    passes = list(passes)
    if starting is not None:
        sums.append(((2,), (starting.six_two, starting.got_first)))
        passes.append(starting.second)
    if ending is not None:
        sums.append(((1,), (ending.zero, ending.got_far)))
    made, passes = stage(sums, passes, after)
    if ending is not None:
        ending.result = made[-1]
    if starting is not None:
        starting.six_two = made[0]
        starting.second = passes[-1]
        if not hold:
            starting.send_second()
        passes = passes[:-1]
    return passes


def even_stage(middle, coming, passes=(), after=()):
    passes = list(passes)
    if coming is not None:
        passes.append(coming.first)
    made, passes = stage(
        [((1, 1), (middle.four_zero, middle.got_second, middle.got_near))], passes, after
    )
    middle.four, middle.zero = made
    middle.send_far()
    if coming is not None:
        coming.first = passes[-1]
        coming.send_first()
        passes = passes[:-1]
    return passes


def halves_order(count):
    bits = bits_of(count)
    return [
        sum(bit for bit, other in zip(bits, reversed(bits)) if m & other) for m in range(count)
    ]


def reduce_halves(stacked, axis="tensor"):
    for bit in bits_of(stacked.shape[0]):
        half = stacked.shape[0] // 2
        stacked = stacked[:half] + swap(stacked[half:], axis, bit)
    return stacked[0]


def gather_blocks(value):
    count = lax.axis_size("tensor")
    have = {0: value}
    for bit in reversed(bits_of(count)):
        for k in sorted(have):
            have[k ^ bit] = swap(have[k], "tensor", bit)
    return [have[k] for k in range(count)]


def exchange_blocks(blocks):
    return [blocks[0]] + [swap(blocks[k], "tensor", k) for k in range(1, len(blocks))]


def small_sum(value, axis):
    for bit in bits_of(lax.axis_size(axis)):
        value = value + swap(value, axis, bit)
    return value


def on_device(
    hidden_in,
    cotangent,
    routes,
    segments,
    gain_in,
    w_query,
    w_key,
    w_value,
    w_out,
    gain_query,
    gain_key,
    gain_mid,
    w_router,
    w_gate,
    w_up,
    w_down,
):
    count = lax.axis_size("tensor")
    rank = lax.axis_index("tensor")
    dp_count = lax.axis_size("dp")
    dp_rank = lax.axis_index("dp")
    tok_rows, width = hidden_in.shape
    local_width = w_query.shape[1]
    heads_here = local_width // HEAD
    full_width = local_width * count
    share = width // count
    experts = w_gate.shape[0]
    seqs, length = segments.shape
    own = length // count
    scale = 1.0 / math.sqrt(HEAD)
    tiled = w_gate.shape[2] % LANES == 0
    acts_of = expert_acts if tiled else plain_acts
    columns_of = back_columns if tiled else plain_columns
    rows_of = back_rows if tiled else plain_rows
    grads_of = expert_grads if tiled else plain_grads
    table = rank ^ jnp.arange(count, dtype=jnp.int32)
    chunks = range(seqs)

    part = width // dp_count
    w_part = lax.dynamic_slice_in_dim(w_out, dp_rank * part, part, 0).astype(F32)
    w_part = lax.all_gather(w_part, "tensor", axis=1, tiled=True)

    hidden = hidden_in.astype(F32)
    in_scale = norm_scale(hidden)
    in_hat = hidden * in_scale
    normed, query_raw, key_raw, value_low, square_sums = project(
        hidden_in, gain_in, w_query, w_key, w_value
    )
    raws = (query_raw, key_raw)
    square_sums = small_sum(square_sums, "tensor")
    angles = jnp.concatenate(
        rotary_tables(document_positions(segments).reshape(-1), HEAD), axis=1
    )
    gains_here = (gain_query.reshape(1, -1), gain_key.reshape(1, -1))
    expert_ids = jnp.arange(experts, dtype=jnp.int32)
    hits = jnp.any(routes[:, :, None] == expert_ids[None, None, :], axis=1)
    counts = hits.astype(jnp.int32)
    kept_all = hits & (jnp.cumsum(counts, axis=0, dtype=jnp.int32) - counts < CAP)

    pieces, last, query_low, key_low = [], None, [], []
    for c in chunks:
        last, query_c, key_c = attend(
            query_raw, key_raw, value_low, square_sums, gains_here, angles, segments, c, scale,
            full_width,
        )
        query_low.append(query_c)
        key_low.append(key_c)
        pieces.append(gather_blocks(last))
    query_low = jnp.concatenate(query_low, axis=0)
    key_low = jnp.concatenate(key_low, axis=0)
    w_part, _ = lax.optimization_barrier((w_part, last))
    w_whole = cast(lax.all_gather(w_part, "dp", axis=0, tiled=True))

    staged = count == 8 and seqs == 2
    groups = Chain.groups if staged else tuple((k,) for k in range(count))

    def plain_reduce(parts):
        return reduce_blocks([item[0] for item in parts])

    middle, mixed, attended, probs, kept, gates = ([] for _ in range(6))

    def forward(c, after, last=False):
        mid_c, mixed_c, logits_c, attended_c = branch(
            pieces[c], table, w_whole, hidden_in, c, gain_mid, w_router, after
        )
        middle.append(mid_c)
        mixed.append(mixed_c)
        attended.append(attended_c)
        probs.append(jax.nn.softmax(logits_c, axis=-1))
        kept.append(lax.slice_in_dim(kept_all, c * length, (c + 1) * length, axis=0))
        gates.append(jnp.where(kept[c], probs[c], 0.0))
        return acts_of(mixed_c, cotangent, c, gates[c], w_gate, w_up, w_down, (), last)

    def mixed_blocks(c, after=()):
        return rows_of(acts[c][1:3], [w_gate, w_up], acts[c][3], table, groups, after)

    def moe_of(c, after=(), last=False):
        return columns_of([acts[c][0]], [w_down], table, groups, after, last)

    def down_grads(after=()):
        return grads_of([cotangent], [a[:1] for a in acts], experts, after)[0]

    def act_grads(after=()):
        return grads_of(mixed, [a[1:3] for a in acts], experts, after)

    def rows_own(value, start=0):
        return lax.dynamic_slice_in_dim(value, start + rank * own, own, 0)

    def columns_own(value):
        return lax.dynamic_slice_in_dim(value, rank * share, share, 1)

    if staged:
        acts = [forward(0, ())]
        mix = [Chain(mixed_blocks(0))]
        mix[0].send_first()
        acts.append(forward(1, (mix[0].four_zero,), True))
        odd_stage(None, mix[0], after=(acts[1][0],))
        mix.append(Chain(mixed_blocks(1, (mix[0].six_two,))))
        even_stage(mix[0], mix[1])
        moe = [Chain(moe_of(0, (mix[0].zero,)))]
        odd_stage(mix[0], mix[1], after=(moe[0].four_zero,))
    else:
        acts = []
        for c in chunks:
            acts.append(forward(c, ()))
        mixed_share = [plain_reduce(mixed_blocks(c)) for c in chunks]
        moe_share = [plain_reduce(moe_of(c)) for c in chunks]
        grad_down = down_grads()
        grad_gate, grad_up = act_grads()

    def all_own(values):
        return jnp.concatenate([rows_own(value) for value in values], axis=0)

    probs_own, kept_own, mid_own = all_own(probs), all_own(kept), all_own(middle)
    mixed_own, attended_own = all_own(mixed), all_own(attended)
    dy_own = jnp.concatenate([rows_own(cotangent, c * length) for c in chunks], axis=0)

    if staged:
        grad_down = down_grads((mix[1].six_two, probs_own, mid_own, mixed_own, attended_own))
        (grad_down,) = even_stage(mix[1], moe[0], passes=(grad_down,))
        grad_gate, grad_up = act_grads((mix[1].zero,))
        grad_gate, grad_up = odd_stage(mix[1], moe[0], passes=(grad_gate, grad_up))
        mixed_share = [item.result[0] for item in mix]

    mixed_share = jnp.concatenate(mixed_share, axis=0)
    prob_grad = jnp.where(kept_own, mixed_share[:, width : width + experts], 0.0)
    logit_own = (
        probs_own * (prob_grad - jnp.sum(probs_own * prob_grad, axis=-1, keepdims=True))
    ).astype(BF)
    mixed_grad = mixed_share[:, :width] + dot(logit_own, w_router, 1, 1)
    mid_scale = norm_scale(mid_own)
    mid_hat = mid_own * mid_scale
    grad_gain_mid = jnp.sum(mixed_grad * mid_hat, axis=0)
    scaled = mixed_grad * gain_mid.astype(F32)
    mid_grad = dy_own.astype(F32) + mid_scale * (
        scaled - mid_hat * jnp.mean(scaled * mid_hat, axis=1, keepdims=True)
    )
    mid_low = mid_grad.astype(BF)
    if staged:
        moe.append(Chain(moe_of(1, (mid_low,), True)))
        (mid_low,) = even_stage(moe[0], moe[1], passes=(mid_low,))
    blocks = send_back(mid_low, w_whole, table)
    attended_grad = jnp.stack(exchange_blocks(blocks))

    q_scaled, k_scaled, value_grad, totals, gain_parts = attend_back(
        query_low, key_low, value_low, attended_grad, raws, square_sums, gains_here, angles,
        table, segments, scale, full_width,
    )
    if staged:
        (totals,) = odd_stage(moe[0], moe[1], passes=(totals,), hold=True)
    gain_parts = jnp.sum(gain_parts.reshape(seqs, 8, local_width), axis=0)
    totals = small_sum(totals, "tensor")
    query_grad, key_grad = raw_grads((q_scaled, k_scaled), raws, square_sums, totals, full_width)
    in_grads = [query_grad, key_grad, value_grad]
    weights_in = [w[None] for w in (w_query, w_key, w_value)]
    columns_in = back_columns if local_width % LANES == 0 and share % LANES == 0 else plain_columns

    hidden_own = jnp.concatenate([rows_own(hidden_in, c * length) for c in chunks], axis=0)
    hidden_own = hidden_own.astype(F32)
    own_scale = norm_scale(hidden_own)
    own_hat = hidden_own * own_scale
    direct = mid_grad / (own_scale * gain_in.astype(F32))

    def normed_blocks(c):
        part_grads = [grad[c * length : (c + 1) * length] for grad in in_grads]
        return columns_in(
            part_grads, weights_in, table, groups, rank=rank, added=(direct,), chunk=c
        )

    if staged:
        moe[1].second, moe[1].six_two = tie((moe[1].second, moe[1].six_two), (totals,))
        moe[1].send_second()
        norm = [Chain(normed_blocks(c)) for c in chunks]
        even_stage(moe[1], norm[0], after=(norm[1].four_zero,))
        odd_stage(moe[1], norm[0])
        even_stage(norm[0], norm[1])
        odd_stage(norm[0], norm[1])
        even_stage(norm[1], None)
        odd_stage(norm[1], None)
        normed_share = [item.result[0] for item in norm]
        moe_share = [item.result[0] for item in moe]
    else:
        normed_share = [plain_reduce(normed_blocks(c)) for c in chunks]
    output = jnp.concatenate(
        [(columns_own(middle[c]) + moe_share[c]).astype(BF) for c in chunks], axis=0
    )

    def over_dp(grad):
        return lax.psum_scatter(grad, "dp", scatter_dimension=0, tiled=True)

    dp_table = dp_rank ^ jnp.arange(dp_count, dtype=jnp.int32)
    order = rank ^ jnp.array(halves_order(count), jnp.int32)
    out_part = reduce_blocks(outer(mid_low.T, attended_own, dp_table, order, (blocks[0],)), "dp")
    grad_w_out = reduce_halves(out_part)

    grad_in = dot(normed, jnp.concatenate(in_grads, axis=1), 0, 0)
    grad_in = reduce_blocks(
        [lax.dynamic_slice_in_dim(grad_in, dp_table[k] * part, part, 0) for k in range(dp_count)],
        "dp",
    )
    grad_w_query, grad_w_key, grad_w_value = (
        grad_in[:, i * local_width : (i + 1) * local_width] for i in range(3)
    )

    normed_share = jnp.concatenate(normed_share, axis=0)
    in_hat_share = columns_own(in_hat)
    gain_share = lax.dynamic_slice_in_dim(gain_in.astype(F32), rank * share, share, 0)
    in_scaled = normed_share * gain_share
    row_sums = jnp.sum(in_scaled * in_hat_share, axis=1).reshape(seqs, length)
    direct_sums = jnp.sum(mid_grad * own_hat, axis=1) / own_scale[:, 0]
    mine = lax.dynamic_slice_in_dim(row_sums, rank * own, own, 1) - direct_sums.reshape(seqs, own)
    row_sums = lax.dynamic_update_slice_in_dim(row_sums, mine, rank * own, 1)
    row_totals = small_sum(row_sums.reshape(1, tok_rows), "tensor")[0]
    grad_input = (
        in_scale * (in_scaled - in_hat_share * (row_totals / width)[:, None])
    ).astype(BF)
    direct_gain = jnp.sum(direct * own_hat, axis=0)
    grad_router = dot(logit_own, mixed_own, 0, 0)
    wide = jnp.concatenate([grad_router, grad_gain_mid[None], direct_gain[None]], axis=0)
    wide = small_sum(wide, "tensor")
    direct_gain = lax.dynamic_slice_in_dim(wide[experts + 1], rank * share, share, 0)
    grad_gain_in = jnp.sum(normed_share * in_hat_share, axis=0) - direct_gain

    wide = small_sum(wide[: experts + 1], "dp")
    wide = lax.dynamic_slice_in_dim(wide, dp_rank * part, part, 1)
    gains = jnp.concatenate([grad_gain_in, gain_parts[0], gain_parts[1]])
    gains = small_sum(gains[None], "dp")[0]

    return (
        output,
        grad_input,
        grad_w_query,
        grad_w_key,
        grad_w_value,
        grad_w_out,
        gains[:share],
        gains[share : share + local_width],
        gains[share + local_width :],
        wide[experts],
        wide[:experts].T,
        over_dp(grad_gate),
        over_dp(grad_up),
        over_dp(grad_down),
    )


def solution(mesh):
    in_specs = (
        P("dp", None),
        P("dp", None),
        P("dp", None),
        P("dp", None),
        P(),
        P(None, "tensor"),
        P(None, "tensor"),
        P(None, "tensor"),
        P(None, "tensor"),
        P("tensor"),
        P("tensor"),
        P(),
        P(),
        P(None, None, "tensor"),
        P(None, None, "tensor"),
        P(None, None, "tensor"),
    )
    out_specs = (
        P("dp", "tensor"),
        P("dp", "tensor"),
        P("dp", "tensor"),
        P("dp", "tensor"),
        P("dp", "tensor"),
        P("dp", "tensor"),
        P("tensor"),
        P("tensor"),
        P("tensor"),
        P("dp"),
        P("dp", None),
        P("dp", None, "tensor"),
        P("dp", None, "tensor"),
        P("dp", None, "tensor"),
    )
    return jax.shard_map(
        on_device, mesh=mesh, in_specs=in_specs, out_specs=out_specs, check_vma=False
    )
```

time: 2520 us -> 1310 us (0.52)
  waiting for transfers between devices: 1740 us -> 536 us
  Pallas kernels: 272 us -> 522 us
  matrix products: 125 us -> 10.5 us
  blocking collectives: 106 us -> 0 us
  starting transfers between devices: 0.67 us -> 80.6 us
  local copies, waits for them, and re-layouts: 132 us -> 57.9 us
  other arithmetic: 122 us -> 78.2 us
    psum x2 -> x0, waiting for transfers between devices: 973 us -> none  [the longest x1 495 us: on_device(): branch = lax.psum(dot(attended_low, w_out, 1, 1), 'tensor')]
    reduce_scatter x8 -> x3, waiting for transfers between devices: 508 us -> 0.01 us  [over_dp(): return lax.psum_scatter(grad, 'dp', scatter_dimension=0, tiled=True)]
    ppermute x0 -> x70, waiting for transfers between devices: none -> 501 us  [swap(): return lax.ppermute(value, axis, [(i, i ^ step) for i in range(count)])]
    reduce_scatter x2 -> x0, waiting for transfers between devices: 257 us -> none  [the longest x1 257 us: on_device(): lax.psum_scatter(normed_part, 'tensor', scatter_dimension=1, tiled=True)]
    pallas_call x6 -> x33, Pallas kernels: 257 us -> 497 us  [the longest x2 93.4 us: expert_acts(): pl.pallas_call(functools.partial(expert_kernel, min(256, tokens), len(aft...]
    dot_general x15 -> x3, matrix products: 125 us -> 10.5 us  [dot(): lax.dot_general(left, right, (((left_dim,), (right_dim,)), ((), ())), pre...]
    psum x4 -> x0, blocking collectives: 106 us -> none  [the longest x1 39.2 us: on_device(): lax.psum((jnp.sum(query_raw * query_raw, axis=1), jnp.sum(key_raw * key_r...]
    ppermute x0 -> x70, starting transfers between devices: none -> 80 us  [swap(): return lax.ppermute(value, axis, [(i, i ^ step) for i in range(count)])]
  transfers between devices with their start and end apart: 12 -> 75, of which waited for: 10 -> 40; matrix products, arithmetic and copies ran while one was open for 9% -> 10% of each run, Pallas kernels for 5% -> 39%
where the time goes in v2:
time: 1310 us; the launch traced here: 1300 us
  waiting for transfers between devices  536 us (41%)
  Pallas kernels  522 us (40%)
  starting transfers between devices  80.6 us (6%)
  other arithmetic  78.2 us (6%)
  local copies, waits for them, and re-layouts  57.9 us (4%)
  between operations  17.6 us (1%)
    ppermute x70, waiting for transfers between devices, swap(): return lax.ppermute(value, axis, [(i, i ^ step) for i in range(count)])  501 us
    pallas_call x2, Pallas kernels, expert_acts(): pl.pallas_call(functools.partial(expert_kernel, min(256, tokens), len(aft...  93.4 us
    pallas_call x2, Pallas kernels, expert_grads(): pl.pallas_call(functools.partial(grads_kernel, min(512, width), chunks, l...  81.8 us
    ppermute x70, starting transfers between devices, swap(): return lax.ppermute(value, axis, [(i, i ^ step) for i in range(count)])  80 us
    pallas_call x4, Pallas kernels, back_columns(): pl.pallas_call(functools.partial(back_columns_kernel, min(512, tokens), c...  69.9 us
    pallas_call x2, Pallas kernels, back_rows(): pl.pallas_call(functools.partial(back_rows_kernel, min(512, tokens), coun...  65.5 us
    pallas_call x13, Pallas kernels, stage(): pl.pallas_call(functools.partial(stage_kernel, tuple((len(group) for _, g...  61.1 us
    pallas_call x2, Pallas kernels, branch(): pl.pallas_call(functools.partial(branch_kernel, len(pieces), len(after)),...  39 us
  transfers between devices with their start and end apart: 75, of which 40 were waited for; matrix products, arithmetic and copies ran while one was open for 10% of the time, Pallas kernels for 39%

profile of v2, /device:TPU:0, one launch (start us, length us, event | category | flops | bytes accessed | tf_op | source)
XLA Modules:
  0.0 1303.5 jit_solution(12394741671759400168)
XLA Ops:
  10.4 13.6 %project.1 = (bf16[2048,2048]{1,0:T(8,128)(2,1)}, f32[2048,256]{1,0:T(8,128)}, f32[2048,256]{1,0:T(8,128)}, bf16[2048,256]{1,0:T(8,128)(2,1)}, f32[8,2048]{1,0:T(8,128)}) custom-call(bf16[2048,2048]{1,0:T(8,128)(2,1)} %refs_9_.3, bf16[1,2048]{1,0:T(2,128)(2,1)} %reshape.169.gain_ref, bf16[2048,256]{1,0:T(8,128)(2,1)} %wq_ref.1, bf16[2048,256]{1,0:T(8,128)(2,1)} %wk_ref.1, ...), custom_call_target="tpu_custom_call" | custom-call | flops 6442450944 | bytes 16777216 | tf_op jit(solution)/shard_map/project/pallas_call | solution.py:95
  58.8 35.4 %all-gather.3.cloned.1.call-done = f32[512,2048]{1,0:T(8,128)} async-done(((f32[512,256]{1,0:T(8,128)}), f32[512,2048]{1,0:T(8,128)}) %all-gather.3.cloned.1.call-update) | async-done | bytes 4194320 | tf_op jit(solution)/shard_map/all_gather | solution.py:1074
  108.4 65.3 %collective-permute-done.6.refs_4_ = f32[1024,256]{1,0:T(8,128)} collective-permute-done((f32[1024,256]{1,0:T(8,128)}, f32[1024,256]{1,0:T(8,128)}, u32[]{:S(2)}, u32[]{:S(2)}) %collective-permute-start.6) | collective-permute-done | bytes 1048608 | tf_op jit(solution)/shard_map/ppermute | solution.py:871
  180.6 15.5 %collective-permute-done.13.refs_4_ = f32[1024,256]{1,0:T(8,128)} collective-permute-done((f32[1024,256]{1,0:T(8,128)S(1)}, f32[1024,256]{1,0:T(8,128)}, u32[]{:S(2)}, u32[]{:S(2)}) %collective-permute-start.13) | collective-permute-done | bytes 1048608 | tf_op jit(solution)/shard_map/ppermute | solution.py:871
  201.4 20.4 %collective-permute-done.8.refs_6_ = f32[1024,256]{1,0:T(8,128)} collective-permute-done((f32[1024,256]{1,0:T(8,128)}, f32[1024,256]{1,0:T(8,128)}, u32[]{:S(2)}, u32[]{:S(2)}) %collective-permute-start.8) | collective-permute-done | bytes 1048608 | tf_op jit(solution)/shard_map/ppermute | solution.py:871
  251.9 21.6 %collective-permute-done.9.refs_7_ = f32[1024,256]{1,0:T(8,128)} collective-permute-done((f32[1024,256]{1,0:T(8,128)}, f32[1024,256]{1,0:T(8,128)}, u32[]{:S(2)}, u32[]{:S(2)}) %collective-permute-start.9) | collective-permute-done | bytes 1048608 | tf_op jit(solution)/shard_map/ppermute | solution.py:871
  273.5 19.4 %branch.2 = (f32[1024,2048]{1,0:T(8,128)}, bf16[1024,2048]{1,0:T(8,128)(2,1)}, f32[1024,16]{1,0:T(8,128)}, bf16[1024,2048]{1,0:T(8,128)(2,1)}) custom-call(s32[8]{0:T(128)} %copy-done, f32[1024,256]{1,0:T(8,128)} %get-tuple-element.132.refs_0_, f32[1024,256]{1,0:T(8,128)} %collective-permute-done.3.refs_1_, f32[1024,256]{1,0:T(8,128)} %collective-permute-done.4.refs_2_, ...), custom_call_target="tpu_custom_call" | custom-call | flops 8589934592 | bytes 33554432 | tf_op jit(solution)/shard_map/branch/pallas_call | solution.py:679
  298.0 46.6 %expert_acts.2 = (bf16[1024,2048]{1,0:T(8,128)(2,1)}, bf16[1024,2048]{1,0:T(8,128)(2,1)}, bf16[1024,2048]{1,0:T(8,128)(2,1)}, f32[1024,128]{1,0:T(8,128)}) custom-call(bf16[1024,2048]{1,0:T(8,128)(2,1)} %get-tuple-element.136.mixed_ref.refs_0_, bf16[2048,2048]{1,0:T(8,128)(2,1)} %refs_1_.4, f32[1024,16]{1,0:T(8,128)} %get-tuple-element.254.gates_ref, ...), custom_call_target="tpu_custom_call" | custom-call | flops 25769803776 | bytes 25165824 | tf_op jit(solution)/shard_map/expert_acts/pallas_call | solution.py:431
  344.6 32.9 %back_rows.2 = (f32[2,128,2176]{2,1,0:T(8,128)}, f32[2,128,2176]{2,1,0:T(8,128)}, f32[2,128,2176]{2,1,0:T(8,128)}, f32[2,128,2176]{2,1,0:T(8,128)}) custom-call(s32[8]{0:T(128)} %gather_fusion, bf16[1024,2048]{1,0:T(8,128)(2,1)} %get-tuple-element.138.refs_0_.refs_3_, bf16[1024,2048]{1,0:T(8,128)(2,1)} %get-tuple-element.139.refs_1_.refs_4_, ...), custom_call_target="tpu_custom_call" | custom-call | flops 17179869184 | bytes 25165824 | tf_op jit(solution)/shard_map/back_rows/pallas_call | solution.py:563
  379.5 19.5 %branch.3 = (f32[1024,2048]{1,0:T(8,128)}, bf16[1024,2048]{1,0:T(8,128)(2,1)}, f32[1024,16]{1,0:T(8,128)}, bf16[1024,2048]{1,0:T(8,128)(2,1)}) custom-call(s32[8]{0:T(128)} %copy-done, f32[1024,256]{1,0:T(8,128)} %get-tuple-element.133.refs_0_, f32[1024,256]{1,0:T(8,128)} %copy-done.58, f32[1024,256]{1,0:T(8,128)} %collective-permute-done.11.refs_2_, ...), custom_call_target="tpu_custom_call" | custom-call | flops 8589934592 | bytes 33554432 | tf_op jit(solution)/shard_map/branch/pallas_call | solution.py:679
  404.0 46.8 %expert_acts.3 = (bf16[1024,2048]{1,0:T(8,128)(2,1)}, bf16[1024,2048]{1,0:T(8,128)(2,1)}, bf16[1024,2048]{1,0:T(8,128)(2,1)}, f32[1024,128]{1,0:T(8,128)}) custom-call(bf16[1024,2048]{1,0:T(8,128)(2,1)} %get-tuple-element.142.mixed_ref.refs_1_, bf16[2048,2048]{1,0:T(8,128)(2,1)} %refs_1_.4, f32[1024,16]{1,0:T(8,128)} %get-tuple-element.252.gates_ref, ...), custom_call_target="tpu_custom_call" | custom-call | flops 1024 | bytes 1024 | tf_op jit(solution)/shard_map/expert_acts/pallas_call | solution.py:431
  458.1 32.6 %back_rows.3 = (f32[2,128,2176]{2,1,0:T(8,128)}, f32[2,128,2176]{2,1,0:T(8,128)}, f32[2,128,2176]{2,1,0:T(8,128)}, f32[2,128,2176]{2,1,0:T(8,128)}) custom-call(s32[8]{0:T(128)} %gather_fusion, bf16[1024,2048]{1,0:T(8,128)(2,1)} %get-tuple-element.146.refs_0_.refs_5_, bf16[1024,2048]{1,0:T(8,128)(2,1)} %get-tuple-element.147.refs_1_.refs_6_, ...), custom_call_target="tpu_custom_call" | custom-call | flops 17179869184 | bytes 25165824 | tf_op jit(solution)/shard_map/back_rows/pallas_call | solution.py:563
  490.7 11.6 collective-permute-done.18.refs_1_
  519.4 21.2 %back_columns.4 = (f32[2,1024,256]{2,1,0:T(8,128)}, f32[2,1024,256]{2,1,0:T(8,128)}, f32[2,1024,256]{2,1,0:T(8,128)}, f32[2,1024,256]{2,1,0:T(8,128)}) custom-call(s32[8]{0:T(128)} %gather_fusion, s32[1]{0:T(128)} %constant.63.clone.1.rank_ref, bf16[1024,2048]{1,0:T(8,128)(2,1)} %get-tuple-element.160.refs_0_.refs_7_, bf16[16,2048,128]{2,1,0:T(8,128)(2,1)} %refs_1_.5, ...), custom_call_target="tpu_custom_call" | custom-call | flops 8589934592 | bytes 16777216 | tf_op jit(solution)/shard_map/back_columns/pallas_call | solution.py:499
  540.7 20.7 %collective-permute-done.21.refs_3_ = f32[1,128,2176]{2,1,0:T(8,128)S(1)} collective-permute-done((f32[1,128,2176]{2,1,0:T(8,128)S(1)}, f32[1,128,2176]{2,1,0:T(8,128)S(1)}, u32[]{:S(2)}, u32[]{:S(2)}) %collective-permute-start.21) | collective-permute-done | bytes 1114144 | tf_op jit(solution)/shard_map/ppermute | solution.py:871
  573.0 31.0 %expert_grads.2.refs_3_ = f32[16,2048,128]{2,1,0:T(8,128)} custom-call(bf16[2048,2048]{1,0:T(8,128)(2,1)} %refs_1_.4, bf16[2048,2048]{1,0:T(8,128)(2,1)} %refs_1_.4, f32[2,128,2176]{2,1,0:T(8,128)} %get-tuple-element.166.refs_2_, f32[256,16]{1,0:T(8,128)} %pad_maximum_fusion.11.refs_3_, f32[256,2048]{1,0:T(8,128)} %get-tuple-element.263.refs_4_, ...), custom_call_target="tpu_custom_call" | custom-call | flops 17179869184 | bytes 25165824 | tf_op jit(solution)/shard_map/expert_grads/pallas_call | solution.py:639
  604.0 13.1 %collective-permute-done.22.refs_1_ = f32[2,128,2176]{2,1,0:T(8,128)S(1)} collective-permute-done((f32[2,128,2176]{2,1,0:T(8,128)}, f32[2,128,2176]{2,1,0:T(8,128)S(1)}, u32[]{:S(2)}, u32[]{:S(2)}) %collective-permute-start.22) | collective-permute-done | bytes 2228256 | tf_op jit(solution)/shard_map/ppermute | solution.py:871
  624.4 50.8 %expert_grads.3 = (f32[16,2048,128]{2,1,0:T(8,128)}, f32[16,2048,128]{2,1,0:T(8,128)}) custom-call(bf16[1024,2048]{1,0:T(8,128)(2,1)} %get-tuple-element.136.mixed_ref.refs_0_, bf16[1024,2048]{1,0:T(8,128)(2,1)} %get-tuple-element.142.mixed_ref.refs_1_, f32[1,128,2176]{2,1,0:T(8,128)} %get-tuple-element.171.refs_2_, ...), custom_call_target="tpu_custom_call" | custom-call | flops 34359738368 | bytes 50331648 | tf_op jit(solution)/shard_map/expert_grads/pallas_call | solution.py:639
  695.2 21.4 %back_columns.5 = (f32[2,1024,256]{2,1,0:T(8,128)}, f32[2,1024,256]{2,1,0:T(8,128)}, f32[2,1024,256]{2,1,0:T(8,128)}, f32[2,1024,256]{2,1,0:T(8,128)}) custom-call(s32[8]{0:T(128)} %gather_fusion, s32[1]{0:T(128)} %constant.63.clone.1.rank_ref, bf16[1024,2048]{1,0:T(8,128)(2,1)} %get-tuple-element.144.refs_3_.refs_8_.refs_0_, ...), custom_call_target="tpu_custom_call" | custom-call | flops 1024 | bytes 1024 | tf_op jit(solution)/shard_map/back_columns/pallas_call | solution.py:499
  716.5 13.9 %collective-permute-done.26.refs_1_ = f32[2,1024,256]{2,1,0:T(8,128)} collective-permute-done((f32[2,1024,256]{2,1,0:T(8,128)S(1)}, f32[2,1024,256]{2,1,0:T(8,128)}, u32[]{:S(2)}, u32[]{:S(2)}) %collective-permute-start.26) | collective-permute-done | bytes 2097184 | tf_op jit(solution)/shard_map/ppermute | solution.py:871
  771.4 24.9 %collective-permute-done.33 = f32[256,256]{1,0:T(8,128)S(1)} collective-permute-done((f32[256,256]{1,0:T(8,128)}, f32[256,256]{1,0:T(8,128)S(1)}, u32[]{:S(2)}, u32[]{:S(2)}) %collective-permute-start.33) | collective-permute-done | bytes 262176 | tf_op jit(solution)/shard_map/ppermute | solution.py:871
  797.0 16.5 %collective-permute-done.34 = f32[256,256]{1,0:T(8,128)S(1)} collective-permute-done((f32[256,256]{1,0:T(8,128)}, f32[256,256]{1,0:T(8,128)S(1)}, u32[]{:S(2)}, u32[]{:S(2)}) %collective-permute-start.34) | collective-permute-done | bytes 262176 | tf_op jit(solution)/shard_map/ppermute | solution.py:871
  815.7 25.0 %attend_back.1 = (f32[2048,256]{1,0:T(8,128)}, f32[2048,256]{1,0:T(8,128)}, bf16[2048,256]{1,0:T(8,128)(2,1)}, f32[8,2048]{1,0:T(8,128)}, f32[16,256]{1,0:T(8,128)}) custom-call(s32[8]{0:T(128)} %copy-done, bf16[2048,256]{1,0:T(8,128)(2,1)} %get-tuple-element.289.q_ref, bf16[2048,256]{1,0:T(8,128)(2,1)} %get-tuple-element.290.k_ref, ...), custom_call_target="tpu_custom_call" | custom-call | flops 5368709120 | bytes 15728640 | tf_op jit(solution)/shard_map/attend_back/pallas_call | solution.py:289
  850.6 24.7 %outer.1 = (f32[8,512,256]{2,1,0:T(8,128)}, f32[8,512,256]{2,1,0:T(8,128)}, f32[8,512,256]{2,1,0:T(8,128)}, f32[8,512,256]{2,1,0:T(8,128)}) custom-call(s32[4]{0:T(128)} %iota_xor_fusion.table_ref, s32[8]{0:T(128)} %broadcast_xor_fusion.columns_ref, bf16[2048,256]{1,0:T(8,128)(2,1)} %bitcast.109, bf16[256,2048]{1,0:T(8,128)(2,1)} %pad_maximum_fusion.4.refs_6_.right_ref, ...), custom_call_target="tpu_custom_call" | custom-call | flops 2147483648 | bytes 16777216 | tf_op jit(solution)/shard_map/outer/pallas_call | solution.py:785
  908.7 13.7 %back_columns.7 = (f32[2,1024,256]{2,1,0:T(8,128)}, f32[2,1024,256]{2,1,0:T(8,128)}, f32[2,1024,256]{2,1,0:T(8,128)}, f32[2,1024,256]{2,1,0:T(8,128)}) custom-call(s32[8]{0:T(128)} %gather_fusion, s32[1]{0:T(128)} %bitcast.15.rank_ref, bf16[1024,256]{1,0:T(8,128)(2,1)} %get-tuple-element.271.refs_0_, bf16[1024,256]{1,0:T(8,128)(2,1)} %get-tuple-element.269.refs_1_, ...), custom_call_target="tpu_custom_call" | custom-call | flops 3221225472 | bytes 33554432 | tf_op jit(solution)/shard_map/back_columns/pallas_call | solution.py:499
  922.3 13.7 %back_columns.6 = (f32[2,1024,256]{2,1,0:T(8,128)}, f32[2,1024,256]{2,1,0:T(8,128)}, f32[2,1024,256]{2,1,0:T(8,128)}, f32[2,1024,256]{2,1,0:T(8,128)}) custom-call(s32[8]{0:T(128)} %gather_fusion, s32[1]{0:T(128)} %bitcast.15.rank_ref, bf16[1024,256]{1,0:T(8,128)(2,1)} %get-tuple-element.272.refs_0_, bf16[1024,256]{1,0:T(8,128)(2,1)} %get-tuple-element.270.refs_1_, ...), custom_call_target="tpu_custom_call" | custom-call | flops 3221225472 | bytes 33554432 | tf_op jit(solution)/shard_map/back_columns/pallas_call | solution.py:499
  955.6 37.1 %collective-permute-done.43.refs_3_ = f32[1,1024,256]{2,1,0:T(8,128)S(1)} collective-permute-done((f32[1,1024,256]{2,1,0:T(8,128)}, f32[1,1024,256]{2,1,0:T(8,128)S(1)}, u32[]{:S(2)}, u32[]{:S(2)}) %collective-permute-start.43) | collective-permute-done | bytes 1048608 | tf_op jit(solution)/shard_map/ppermute | solution.py:871
  1001.7 48.0 %collective-permute-done.63 = f32[18,2048]{1,0:T(8,128)S(1)} collective-permute-done((f32[18,2048]{1,0:T(8,128)S(1)}, f32[18,2048]{1,0:T(8,128)S(1)}, u32[]{:S(2)}, u32[]{:S(2)}) %collective-permute-start.63) | collective-permute-done | bytes 147488 | tf_op jit(solution)/shard_map/ppermute | solution.py:871
  1123.0 30.3 %collective-permute-done.47.refs_3_ = f32[1,1024,256]{2,1,0:T(8,128)S(1)} collective-permute-done((f32[1,1024,256]{2,1,0:T(8,128)}, f32[1,1024,256]{2,1,0:T(8,128)S(1)}, u32[]{:S(2)}, u32[]{:S(2)}) %collective-permute-start.47) | collective-permute-done | bytes 1048608 | tf_op jit(solution)/shard_map/ppermute | solution.py:871
  1168.8 29.9 %collective-permute-done.56 = f32[512,768]{1,0:T(8,128)S(1)} collective-permute-done((f32[512,768]{1,0:T(8,128)S(1)}, f32[512,768]{1,0:T(8,128)S(1)}, u32[]{:S(2)}, u32[]{:S(2)}) %collective-permute-start.56) | collective-permute-done | bytes 1572896 | tf_op jit(solution)/shard_map/ppermute | solution.py:871
  1218.8 24.6 %collective-permute-done.61 = f32[2,512,256]{2,1,0:T(8,128)} collective-permute-done((f32[2,512,256]{2,1,0:T(8,128)}, f32[2,512,256]{2,1,0:T(8,128)}, u32[]{:S(2)}, u32[]{:S(2)}) %collective-permute-start.61) | collective-permute-done | bytes 1048608 | tf_op jit(solution)/shard_map/ppermute | solution.py:871
  1247.0 28.3 %collective-permute-done.50.refs_1_ = f32[1,1024,256]{2,1,0:T(8,128)} collective-permute-done((f32[1,1024,256]{2,1,0:T(8,128)}, f32[1,1024,256]{2,1,0:T(8,128)}, u32[]{:S(2)}, u32[]{:S(2)}) %collective-permute-start.50) | collective-permute-done | bytes 1048608 | tf_op jit(solution)/shard_map/ppermute | solution.py:871
  (417 shorter events, 415.8 us)
Async XLA Ops:
  7.2 87.0 %all-gather.3.cloned.1.call-start = ((), (), s32[]{:S(2)}) async-start(), calls=%async_computation.3 | async-start | bytes 4718592 | tf_op jit(solution)/shard_map/all_gather | solution.py:1074
  9.0 218.8 %all-gather.5.cloned.1.call-start = ((), (), s32[]{:S(2)}) async-start(), calls=%async_computation.4 | async-start | bytes 20971520 | tf_op jit(solution)/shard_map/all_gather | solution.py:1105
  94.2 1202.5 %reduce-scatter.8.cloned.1.call-start = ((), (), s32[]{:S(2)}) async-start(), calls=%async_computation.7 | async-start | bytes 20971520 | tf_op jit(solution)/shard_map/reduce_scatter | solution.py:1242
  103.4 70.3 %collective-permute-start.6 = (f32[1024,256]{1,0:T(8,128)}, f32[1024,256]{1,0:T(8,128)}, u32[]{:S(2)}, u32[]{:S(2)}) collective-permute-start(f32[1024,256]{1,0:T(8,128)} %get-tuple-element.132.refs_0_), channel_id=1, source_target_pairs={{0,4},{1,5},{2,6},{3,7},{4,0},{5,1},{6,2},{7,3},{8,12},{9,13},{10,... | collective-permute-start | bytes 3145736 | tf_op jit(solution)/shard_map/ppermute | solution.py:871
  105.0 91.1 %collective-permute-start.13 = (f32[1024,256]{1,0:T(8,128)S(1)}, f32[1024,256]{1,0:T(8,128)}, u32[]{:S(2)}, u32[]{:S(2)}) collective-permute-start(f32[1024,256]{1,0:T(8,128)S(1)} %copy-done.56), channel_id=1, source_target_pairs={{0,4},{1,5},{2,6},{3,7},{4,0},{5,1},{6,2},{7,3},{8,12},{9,13},{10,... | collective-permute-start | bytes 3145736 | tf_op jit(solution)/shard_map/ppermute | solution.py:871
  106.4 90.2 %collective-permute-start.11 = (f32[1024,256]{1,0:T(8,128)S(1)}, f32[1024,256]{1,0:T(8,128)}, u32[]{:S(2)}, u32[]{:S(2)}) collective-permute-start(f32[1024,256]{1,0:T(8,128)S(1)} %copy-done.56), channel_id=1, source_target_pairs={{0,2},{1,3},{2,0},{3,1},{4,6},{5,7},{6,4},{7,5},{8,10},{9,11},{10,... | collective-permute-start | bytes 3145736 | tf_op jit(solution)/shard_map/ppermute | solution.py:871
  106.4 92.9 %collective-permute-start.4 = (f32[1024,256]{1,0:T(8,128)}, f32[1024,256]{1,0:T(8,128)}, u32[]{:S(2)}, u32[]{:S(2)}) collective-permute-start(f32[1024,256]{1,0:T(8,128)} %get-tuple-element.132.refs_0_), channel_id=1, source_target_pairs={{0,2},{1,3},{2,0},{3,1},{4,6},{5,7},{6,4},{7,5},{8,10},{9,11},{10,... | collective-permute-start | bytes 3145736 | tf_op jit(solution)/shard_map/ppermute | solution.py:871
  179.7 59.1 %collective-permute-start.3 = (f32[1024,256]{1,0:T(8,128)}, f32[1024,256]{1,0:T(8,128)}, u32[]{:S(2)}, u32[]{:S(2)}) collective-permute-start(f32[1024,256]{1,0:T(8,128)} %get-tuple-element.132.refs_0_), channel_id=1, source_target_pairs={{0,1},{1,0},{2,3},{3,2},{4,5},{5,4},{6,7},{7,6},{8,9},{9,8},{10,11... | collective-permute-start | bytes 3145736 | tf_op jit(solution)/shard_map/ppermute | solution.py:871
  199.3 51.7 %collective-permute-start.5 = (f32[1024,256]{1,0:T(8,128)}, f32[1024,256]{1,0:T(8,128)}, u32[]{:S(2)}, u32[]{:S(2)}) collective-permute-start(f32[1024,256]{1,0:T(8,128)} %collective-permute-done.4.refs_2_), channel_id=1, source_target_pairs={{0,1},{1,0},{2,3},{3,2},{4,5},{5,4},{6,7},{7,6},{8,9},{9,8},{10,11... | collective-permute-start | bytes 3145736 | tf_op jit(solution)/shard_map/ppermute | solution.py:871
  221.8 51.7 %collective-permute-start.9 = (f32[1024,256]{1,0:T(8,128)}, f32[1024,256]{1,0:T(8,128)}, u32[]{:S(2)}, u32[]{:S(2)}) collective-permute-start(f32[1024,256]{1,0:T(8,128)} %collective-permute-done.8.refs_6_), channel_id=1, source_target_pairs={{0,1},{1,0},{2,3},{3,2},{4,5},{5,4},{6,7},{7,6},{8,9},{9,8},{10,11... | collective-permute-start | bytes 3145736 | tf_op jit(solution)/shard_map/ppermute | solution.py:871
  238.8 139.6 %collective-permute-start.10 = (f32[1024,256]{1,0:T(8,128)S(1)}, f32[1024,256]{1,0:T(8,128)S(1)}, u32[]{:S(2)}, u32[]{:S(2)}) collective-permute-start(f32[1024,256]{1,0:T(8,128)S(1)} %copy-done.57), channel_id=1, source_target_pairs={{0,1},{1,0},{2,3},{3,2},{4,5},{5,4},{6,7},{7,6},{8,9},{9,8},{10,11... | collective-permute-start | bytes 3145736 | tf_op jit(solution)/shard_map/ppermute | solution.py:871
  242.7 135.8 %collective-permute-start.14 = (f32[1024,256]{1,0:T(8,128)}, f32[1024,256]{1,0:T(8,128)}, u32[]{:S(2)}, u32[]{:S(2)}) collective-permute-start(f32[1024,256]{1,0:T(8,128)} %collective-permute-done.13.refs_4_), channel_id=1, source_target_pairs={{0,1},{1,0},{2,3},{3,2},{4,5},{5,4},{6,7},{7,6},{8,9},{9,8},{10,11... | collective-permute-start | bytes 3145736 | tf_op jit(solution)/shard_map/ppermute | solution.py:871
  244.8 133.7 %collective-permute-start.12 = (f32[1024,256]{1,0:T(8,128)}, f32[1024,256]{1,0:T(8,128)}, u32[]{:S(2)}, u32[]{:S(2)}) collective-permute-start(f32[1024,256]{1,0:T(8,128)} %collective-permute-done.11.refs_2_), channel_id=1, source_target_pairs={{0,1},{1,0},{2,3},{3,2},{4,5},{5,4},{6,7},{7,6},{8,9},{9,8},{10,11... | collective-permute-start | bytes 3145736 | tf_op jit(solution)/shard_map/ppermute | solution.py:871
  251.0 127.4 %collective-permute-start.16 = (f32[1024,256]{1,0:T(8,128)}, f32[1024,256]{1,0:T(8,128)}, u32[]{:S(2)}, u32[]{:S(2)}) collective-permute-start(f32[1024,256]{1,0:T(8,128)} %collective-permute-done.15.refs_6_), channel_id=1, source_target_pairs={{0,1},{1,0},{2,3},{3,2},{4,5},{5,4},{6,7},{7,6},{8,9},{9,8},{10,11... | collective-permute-start | bytes 3145736 | tf_op jit(solution)/shard_map/ppermute | solution.py:871
  377.6 73.2 %collective-permute-start.17 = (f32[2,128,2176]{2,1,0:T(8,128)}, f32[2,128,2176]{2,1,0:T(8,128)}, u32[]{:S(2)}, u32[]{:S(2)}) collective-permute-start(f32[2,128,2176]{2,1,0:T(8,128)} %get-tuple-element.150), channel_id=1, source_target_pairs={{0,1},{1,0},{2,3},{3,2},{4,5},{5,4},{6,7},{7,6},{8,9},{9,8},{10,11... | collective-permute-start | bytes 6684680 | tf_op jit(solution)/shard_map/ppermute | solution.py:871
  623.3 673.4 %reduce-scatter.4.cloned.1.call-start = ((), (), s32[]{:S(2)}) async-start(), calls=%async_computation.5 | async-start | bytes 20971520 | tf_op jit(solution)/shard_map/reduce_scatter | solution.py:1242
  623.4 51.8 %collective-permute-start.25 = (f32[1,128,2176]{2,1,0:T(8,128)}, f32[1,128,2176]{2,1,0:T(8,128)S(1)}, u32[]{:S(2)}, u32[]{:S(2)}) collective-permute-start(f32[1,128,2176]{2,1,0:T(8,128)} %get-tuple-element.172), channel_id=1, source_target_pairs={{0,4},{1,5},{2,6},{3,7},{4,0},{5,1},{6,2},{7,3},{8,12},{9,13},{10,... | collective-permute-start | bytes 3342344 | tf_op jit(solution)/shard_map/ppermute | solution.py:871
  623.4 51.8 %collective-permute-start.24 = (f32[2,1024,256]{2,1,0:T(8,128)}, f32[2,1024,256]{2,1,0:T(8,128)S(1)}, u32[]{:S(2)}, u32[]{:S(2)}) collective-permute-start(f32[2,1024,256]{2,1,0:T(8,128)} %get-tuple-element.170), channel_id=1, source_target_pairs={{0,1},{1,0},{2,3},{3,2},{4,5},{5,4},{6,7},{7,6},{8,9},{9,8},{10,11... | collective-permute-start | bytes 6291464 | tf_op jit(solution)/shard_map/ppermute | solution.py:871
  681.8 614.9 %reduce-scatter.6.cloned.1.call-start = ((), (), s32[]{:S(2)}) async-start(), calls=%async_computation.6 | async-start | bytes 20971520 | tf_op jit(solution)/shard_map/reduce_scatter | solution.py:1242
  755.6 58.0 %collective-permute-start.34 = (f32[256,256]{1,0:T(8,128)}, f32[256,256]{1,0:T(8,128)S(1)}, u32[]{:S(2)}, u32[]{:S(2)}) collective-permute-start(f32[256,256]{1,0:T(8,128)} %get-tuple-element.194), channel_id=1, source_target_pairs={{0,5},{1,4},{2,7},{3,6},{4,1},{5,0},{6,3},{7,2},{8,13},{9,12},{10,... | collective-permute-start | bytes 786440 | tf_op jit(solution)/shard_map/ppermute | solution.py:871
  756.8 86.5 %collective-permute-start.28 = (f32[2,1024,256]{2,1,0:T(8,128)S(1)}, f32[2,1024,256]{2,1,0:T(8,128)S(1)}, u32[]{:S(2)}, u32[]{:S(2)}) collective-permute-start(f32[2,1024,256]{2,1,0:T(8,128)S(1)} %copy-done.21), channel_id=1, source_target_pairs={{0,1},{1,0},{2,3},{3,2},{4,5},{5,4},{6,7},{7,6},{8,9},{9,8},{10,11... | collective-permute-start | bytes 6291464 | tf_op jit(solution)/shard_map/ppermute | solution.py:871
  875.3 74.1 %collective-permute-start.58 = (f32[8,512,256]{2,1,0:T(8,128)}, f32[8,512,256]{2,1,0:T(8,128)}, u32[]{:S(2)}, u32[]{:S(2)}) collective-permute-start(f32[8,512,256]{2,1,0:T(8,128)} %get-tuple-element.237), channel_id=1, source_target_pairs={{0,8},{8,0},{16,24},{24,16},{1,9},{9,1},{17,25},{25,17},{2,10},{10... | collective-permute-start | bytes 12582920 | tf_op jit(solution)/shard_map/ppermute | solution.py:871
  949.4 138.1 %collective-permute-start.57 = (f32[8,512,256]{2,1,0:T(8,128)}, f32[8,512,256]{2,1,0:T(8,128)}, u32[]{:S(2)}, u32[]{:S(2)}) collective-permute-start(f32[8,512,256]{2,1,0:T(8,128)} %get-tuple-element.235), channel_id=1, source_target_pairs={{0,8},{8,0},{16,24},{24,16},{1,9},{9,1},{17,25},{25,17},{2,10},{10... | collective-permute-start | bytes 12582920 | tf_op jit(solution)/shard_map/ppermute | solution.py:871
  954.1 142.2 %collective-permute-start.59 = (f32[8,512,256]{2,1,0:T(8,128)}, f32[8,512,256]{2,1,0:T(8,128)}, u32[]{:S(2)}, u32[]{:S(2)}) collective-permute-start(f32[8,512,256]{2,1,0:T(8,128)} %add.227), channel_id=1, source_target_pairs={{0,16},{8,24},{16,0},{24,8},{1,17},{9,25},{17,1},{25,9},{2,18},{10... | collective-permute-start | bytes 12582920 | tf_op jit(solution)/shard_map/ppermute | solution.py:871
  999.3 65.9 %collective-permute-start.44 = (f32[2,1024,256]{2,1,0:T(8,128)}, f32[2,1024,256]{2,1,0:T(8,128)S(1)}, u32[]{:S(2)}, u32[]{:S(2)}) collective-permute-start(f32[2,1024,256]{2,1,0:T(8,128)} %get-tuple-element.221), channel_id=1, source_target_pairs={{0,1},{1,0},{2,3},{3,2},{4,5},{5,4},{6,7},{7,6},{8,9},{9,8},{10,11... | collective-permute-start | bytes 6291464 | tf_op jit(solution)/shard_map/ppermute | solution.py:871
  1000.4 64.8 %collective-permute-start.45 = (f32[2,1024,256]{2,1,0:T(8,128)}, f32[2,1024,256]{2,1,0:T(8,128)}, u32[]{:S(2)}, u32[]{:S(2)}) collective-permute-start(f32[2,1024,256]{2,1,0:T(8,128)} %get-tuple-element.222), channel_id=1, source_target_pairs={{0,2},{1,3},{2,0},{3,1},{4,6},{5,7},{6,4},{7,5},{8,10},{9,11},{10,... | collective-permute-start | bytes 6291464 | tf_op jit(solution)/shard_map/ppermute | solution.py:871
  1065.1 57.3 %collective-permute-start.68 = (f32[17,2048]{1,0:T(8,128)S(1)}, f32[17,2048]{1,0:T(8,128)S(1)}, u32[]{:S(2)}, u32[]{:S(2)}) collective-permute-start(f32[17,2048]{1,0:T(8,128)S(1)} %bitcast.110), channel_id=1, source_target_pairs={{0,8},{8,0},{16,24},{24,16},{1,9},{9,1},{17,25},{25,17},{2,10},{10... | collective-permute-start | bytes 417800 | tf_op jit(solution)/shard_map/ppermute | solution.py:871
  1071.3 82.0 %collective-permute-start.46 = (f32[2,1024,256]{2,1,0:T(8,128)}, f32[2,1024,256]{2,1,0:T(8,128)}, u32[]{:S(2)}, u32[]{:S(2)}) collective-permute-start(f32[2,1024,256]{2,1,0:T(8,128)} %get-tuple-element.224), channel_id=1, source_target_pairs={{0,1},{1,0},{2,3},{3,2},{4,5},{5,4},{6,7},{7,6},{8,9},{9,8},{10,11... | collective-permute-start | bytes 6291464 | tf_op jit(solution)/shard_map/ppermute | solution.py:871
  1087.2 72.8 %collective-permute-start.55 = (f32[512,768]{1,0:T(8,128)}, f32[512,768]{1,0:T(8,128)}, u32[]{:S(2)}, u32[]{:S(2)}) collective-permute-start(f32[512,768]{1,0:T(8,128)} %get-tuple-element.261), channel_id=1, source_target_pairs={{0,8},{8,0},{16,24},{24,16},{1,9},{9,1},{17,25},{25,17},{2,10},{10... | collective-permute-start | bytes 4718600 | tf_op jit(solution)/shard_map/ppermute | solution.py:871
  1103.5 62.6 %collective-permute-start.60 = (f32[4,512,256]{2,1,0:T(8,128)}, f32[4,512,256]{2,1,0:T(8,128)S(1)}, u32[]{:S(2)}, u32[]{:S(2)}) collective-permute-start(f32[4,512,256]{2,1,0:T(8,128)} %slice.177), channel_id=1, source_target_pairs={{0,1},{1,0},{2,3},{3,2},{4,5},{5,4},{6,7},{7,6},{8,9},{9,8},{10,11... | collective-permute-start | bytes 6291464 | tf_op jit(solution)/shard_map/ppermute | solution.py:871
  1167.5 75.8 %collective-permute-start.61 = (f32[2,512,256]{2,1,0:T(8,128)}, f32[2,512,256]{2,1,0:T(8,128)}, u32[]{:S(2)}, u32[]{:S(2)}) collective-permute-start(f32[2,512,256]{2,1,0:T(8,128)} %slice.179), channel_id=1, source_target_pairs={{0,2},{1,3},{2,0},{3,1},{4,6},{5,7},{6,4},{7,5},{8,10},{9,11},{10,... | collective-permute-start | bytes 3145736 | tf_op jit(solution)/shard_map/ppermute | solution.py:871
  1214.3 61.0 %collective-permute-start.50 = (f32[1,1024,256]{2,1,0:T(8,128)}, f32[1,1024,256]{2,1,0:T(8,128)}, u32[]{:S(2)}, u32[]{:S(2)}) collective-permute-start(f32[1,1024,256]{2,1,0:T(8,128)} %get-tuple-element.232), channel_id=1, source_target_pairs={{0,4},{1,5},{2,6},{3,7},{4,0},{5,1},{6,2},{7,3},{8,12},{9,13},{10,... | collective-permute-start | bytes 3145736 | tf_op jit(solution)/shard_map/ppermute | solution.py:871
  (107 other events, 2155.5 us)
Sparse Core Ops, SparseCore 0:
  10.6 83.4 all-gather.2
  95.7 104.0 all-gather.4
  623.4 124.6 reduce-scatter.7
  751.3 126.0 reduce-scatter.3
  880.4 176.2 reduce-scatter.5

commit v3 on v2

--- a/solution.py
+++ b/solution.py
@@ -55,7 +55,7 @@
 
 
 def params(mib):
-    return pltpu.CompilerParams(vmem_limit_bytes=max(mib, 58) * MIB)
+    return pltpu.CompilerParams(vmem_limit_bytes=mib * MIB)
 
 
 def cost(flops, moved, last=False):
@@ -111,7 +111,7 @@
             jax.ShapeDtypeStruct((tokens, wide), BF),
             jax.ShapeDtypeStruct((8, tokens), F32),
         ],
-        compiler_params=params(48),
+        compiler_params=params(58),
         cost_estimate=cost(6 * tokens * width * wide, 4 * tokens * width),
         name="project",
     )(hidden, gain.reshape(1, -1), w_query, w_key, w_value)
@@ -147,6 +147,7 @@
     scale,
     block,
     full,
+    after,
     q_ref,
     k_ref,
     v_ref,
@@ -156,10 +157,9 @@
     angle_ref,
     col_ref,
     row_ref,
-    out_ref,
-    ql_ref,
-    kl_ref,
+    *refs,
 ):
+    out_ref, ql_ref, kl_ref = refs[after:]
     length = q_ref.shape[0]
     cosine, sine = both_halves(angle_ref[...])
     for raw, which, gain, low in ((q_ref, 0, gq_ref, ql_ref), (k_ref, 1, gk_ref, kl_ref)):
@@ -182,7 +182,7 @@
         out_ref[rows, :] = dot(weights, v_ref[start:stop, :]).astype(BF).astype(F32)
 
 
-def attend(q, k, v, sums, gains, angles, segments, chunk, scale, full):
+def attend(q, k, v, sums, gains, angles, segments, chunk, scale, full, after=()):
     seqs, length = segments.shape
     heads = q.shape[1] // HEAD
     block = pl.BlockSpec((length, HEAD), lambda head: (chunk, head))
@@ -190,7 +190,7 @@
     gain = pl.BlockSpec((1, HEAD), lambda head: (0, head))
     work = heads * length * length * HEAD
     return pl.pallas_call(
-        functools.partial(attend_kernel, scale, min(256, length), full),
+        functools.partial(attend_kernel, scale, min(256, length), full, len(after)),
         grid=(heads,),
         in_specs=[
             block,
@@ -202,13 +202,14 @@
             pl.BlockSpec((length, HEAD), lambda head: (chunk, 0)),
             pl.BlockSpec((length, 1), lambda head: (chunk, 0)),
             pl.BlockSpec((1, 1, length), lambda head: (chunk, 0, 0)),
-        ],
+        ]
+        + [ANY] * len(after),
         out_specs=[mine] * 3,
         out_shape=[jax.ShapeDtypeStruct((length, q.shape[1]), kind) for kind in (F32, BF, BF)],
-        compiler_params=params(48),
-        cost_estimate=cost(4 * work, length * heads * HEAD * 22),
+        compiler_params=params(58),
+        cost_estimate=cost(64 * work, length * heads * HEAD * 22),
         name="attend",
-    )(q, k, v, sums, *gains, angles, segments.reshape(-1, 1), segments[:, None, :])
+    )(q, k, v, sums, *gains, angles, segments.reshape(-1, 1), segments[:, None, :], *after)
 
 
 def attend_back_kernel(
@@ -326,7 +327,7 @@
             jax.ShapeDtypeStruct((8, q.shape[0]), F32),
             jax.ShapeDtypeStruct((8 * seqs, q.shape[1]), F32),
         ],
-        compiler_params=params(48),
+        compiler_params=params(58),
         cost_estimate=cost(10 * work, q.size * 30),
         name="attend_back",
     )(
@@ -363,18 +364,18 @@
         in_specs=[block] * 4 + [line] * 2,
         out_specs=[block] * 2,
         out_shape=[jax.ShapeDtypeStruct((tokens, wide), BF)] * 2,
-        compiler_params=params(48),
+        compiler_params=params(58),
         cost_estimate=cost(0, 20 * tokens * wide),
         name="raw_grads",
     )(*scaled, *raws, sums, totals)
 
 
 def expert_terms(gate_act, up_act, low_grad, gate):
-    sigmoid = 1.0 / (1.0 + jnp.exp(-gate_act))
+    sigmoid = 0.5 * jnp.tanh(0.5 * gate_act) + 0.5
     silu = gate_act * sigmoid
     inner = (silu * up_act).astype(BF).astype(F32)
     inner_grad = low_grad * gate
-    gate_grad = inner_grad * up_act * sigmoid * (1.0 + gate_act * (1.0 - sigmoid))
+    gate_grad = inner_grad * up_act * (sigmoid + silu * (1.0 - sigmoid))
     return (
         (inner * gate).astype(BF),
         gate_grad.astype(BF),
@@ -383,14 +384,50 @@
     )
 
 
-def expert_kernel(rows, after, mixed_ref, dy_ref, gates_ref, wg_ref, wu_ref, wd_ref, *refs):
-    gi_ref, gg_ref, ug_ref, dots_ref, both, down = refs[after:]
+def low_kernel(rows, after, dy_ref, wd_ref, *refs):
+    out_ref, down = refs[after:]
+    many, _, hid = wd_ref.shape
+    for part in range(many):
+        down[:, part * hid : (part + 1) * hid] = wd_ref[part]
+
+    def body(index, carry):
+        here = pl.ds(pl.multiple_of(index * rows, rows), rows)
+        out_ref[here, :] = dot(dy_ref[here, :], down[...])
+        return carry
+
+    lax.fori_loop(0, dy_ref.shape[0] // rows, body, 0)
+
+
+def low_grads(dy, w_down, chunk, tokens, after=(), last=False):
+    width = dy.shape[1]
+    experts, _, hid = w_down.shape
+    many = 2
+    return pl.pallas_call(
+        functools.partial(low_kernel, min(1024, tokens), len(after)),
+        grid=(experts // many,),
+        in_specs=[
+            pl.BlockSpec(
+                (tokens, width), lambda e: (chunk, 0), pipeline_mode=pl.Buffered(buffer_count=1)
+            ),
+            pl.BlockSpec((many, width, hid), lambda e: (e, 0, 0)),
+        ]
+        + [ANY] * len(after),
+        out_specs=pl.BlockSpec((tokens, many * hid), lambda e: (0, e)),
+        out_shape=jax.ShapeDtypeStruct((tokens, experts * hid), F32),
+        scratch_shapes=[pltpu.VMEM((width, many * hid), BF)],
+        compiler_params=params(58),
+        cost_estimate=cost(8 * tokens * width * experts * hid, 8 * tokens * width, last),
+        name="low_grads",
+    )(dy, w_down, *after)
+
+
+def expert_kernel(rows, after, mixed_ref, low_ref, gates_ref, wg_ref, wu_ref, *refs):
+    gi_ref, gg_ref, ug_ref, dots_ref, both = refs[after:]
     step = pl.program_id(0)
     many, _, hid = wg_ref.shape
     for part in range(many):
         both[:, part * hid : (part + 1) * hid] = wg_ref[part]
         both[:, (many + part) * hid : (many + part + 1) * hid] = wu_ref[part]
-        down[:, part * hid : (part + 1) * hid] = wd_ref[part]
 
     @pl.when(step == 0)
     def _():
@@ -399,7 +436,6 @@
     def body(index, carry):
         here = pl.ds(pl.multiple_of(index * rows, rows), rows)
         acts = dot(mixed_ref[here, :], both[...])
-        low_grads = dot(dy_ref[here, :], down[...])
         gates = gates_ref[here, :]
         totals = dots_ref[here, :]
         lane = lax.broadcasted_iota(jnp.int32, gates.shape, 1)
@@ -409,7 +445,9 @@
             gate = jnp.sum(jnp.where(chosen, gates, 0.0), axis=1, keepdims=True)
             span = slice(part * hid, (part + 1) * hid)
             other = slice((many + part) * hid, (many + part + 1) * hid)
-            gi, gg, ug, terms = expert_terms(acts[:, span], acts[:, other], low_grads[:, span], gate)
+            gi, gg, ug, terms = expert_terms(
+                acts[:, span], acts[:, other], low_ref[here, span], gate
+            )
             gi_ref[here, span] = gi
             gg_ref[here, span] = gg
             ug_ref[here, span] = ug
@@ -418,10 +456,10 @@
         dots_ref[here, :] = totals
         return carry
 
-    lax.fori_loop(0, mixed_ref.shape[0] // rows, body, 0)
-
-
-def expert_acts(mixed, dy, chunk, gates, w_gate, w_up, w_down, after=(), last=False):
+    lax.fori_loop(0, mixed_ref.shape[0] // rows, body, 0, unroll=True)
+
+
+def expert_acts(mixed, low, gates, w_gate, w_up, after=(), last=False):
     tokens, width = mixed.shape
     experts, _, hid = w_gate.shape
     many = 2
@@ -429,29 +467,23 @@
     wide = pl.BlockSpec((tokens, many * hid), lambda e: (0, e))
     wide_shape = jax.ShapeDtypeStruct((tokens, experts * hid), BF)
     return pl.pallas_call(
-        functools.partial(expert_kernel, min(256, tokens), len(after)),
+        functools.partial(expert_kernel, min(512, tokens), len(after)),
         grid=(experts // many,),
         in_specs=[
             whole_spec(mixed.shape),
-            pl.BlockSpec(
-                mixed.shape, lambda e: (chunk, 0), pipeline_mode=pl.Buffered(buffer_count=1)
-            ),
+            wide,
             whole_spec(gates.shape),
-            weight,
             weight,
             weight,
         ]
         + [ANY] * len(after),
         out_specs=[wide, wide, wide, whole_spec((tokens, LANES))],
         out_shape=[wide_shape, wide_shape, wide_shape, jax.ShapeDtypeStruct((tokens, LANES), F32)],
-        scratch_shapes=[
-            pltpu.VMEM((width, 2 * many * hid), BF),
-            pltpu.VMEM((width, many * hid), BF),
-        ],
-        compiler_params=params(58),
-        cost_estimate=cost(6 * tokens * width * experts * hid, 12 * tokens * width, last),
+        scratch_shapes=[pltpu.VMEM((width, 2 * many * hid), BF)],
+        compiler_params=params(58),
+        cost_estimate=cost(4 * tokens * width * experts * hid, 12 * tokens * width, last),
         name="expert_acts",
-    )(mixed, dy, gates, w_gate, w_up, w_down, *after)
+    )(mixed, low, gates, w_gate, w_up, *after)
 
 
 def fill(held, weight):
@@ -514,7 +546,7 @@
             scratch_shapes=[pltpu.VMEM((block, experts * hid), BF)] * count,
         ),
         out_shape=[jax.ShapeDtypeStruct((len(group), tokens, block), F32) for group in groups],
-        compiler_params=params(56),
+        compiler_params=params(58),
         cost_estimate=cost(
             2 * count * tokens * width * experts * hid, (4 + 4 * count) * tokens * width, last
         ),
@@ -525,13 +557,12 @@
 def back_rows_kernel(rows, count, after, table_ref, *refs):
     lefts, weights, dots_ref = refs[:count], refs[count : 2 * count], refs[2 * count]
     refs = refs[2 * count + 1 + after :]
-    outs, held, turned = refs[: -2 * count], refs[-2 * count : -count], refs[-count:]
+    outs, held, turned = refs[:-2], refs[-2], refs[-1]
     outs = [out.at[part] for out in outs for part in range(out.shape[0])]
     part_rows = outs[0].shape[0]
-    block = held[0].shape[0]
-    width = outs[0].shape[1] - LANES
-    for index in range(count):
-        fill(held[index], weights[index])
+    deep = held.shape[1] // count
+    experts, _, hid = weights[0].shape
+    last = pl.num_programs(0) - 1
 
     @pl.when(pl.program_id(0) == 0)
     def _():
@@ -539,18 +570,25 @@
             here = pl.ds(pl.multiple_of(table_ref[number] * part_rows, part_rows), part_rows)
             there = slice(number * part_rows, (number + 1) * part_rows)
             for index in range(count):
-                turned[index][there, :] = lefts[index][here, :]
-            outs[number][:, width:] = dots_ref[here, :]
-
-    columns = pl.ds(pl.multiple_of(pl.program_id(0) * block, block), block)
-    for step in range(len(outs) * part_rows // rows):
-        here = slice(step * rows, (step + 1) * rows)
-        total = dot(turned[0][here, :], held[0][...], 1, 1)
-        for left, right in zip(turned[1:], held[1:]):
-            total = total + dot(left[here, :], right[...], 1, 1)
-        for part in range(rows // part_rows):
-            number = step * (rows // part_rows) + part
-            outs[number][:, columns] = total[part * part_rows : (part + 1) * part_rows]
+                turned[there, index * deep : (index + 1) * deep] = lefts[index][here, :]
+
+    @pl.when(pl.program_id(0) < last)
+    def _():
+        for index in range(count):
+            for expert in range(experts):
+                place = index * deep + expert * hid
+                held[:, place : place + hid] = weights[index][expert]
+        for step in range(len(outs) * part_rows // rows):
+            total = dot(turned[step * rows : (step + 1) * rows, :], held[...], 1, 1)
+            for part in range(rows // part_rows):
+                number = step * (rows // part_rows) + part
+                outs[number][...] = total[part * part_rows : (part + 1) * part_rows]
+
+    @pl.when(pl.program_id(0) == last)
+    def _():
+        for number in range(len(outs)):
+            here = pl.ds(pl.multiple_of(table_ref[number] * part_rows, part_rows), part_rows)
+            outs[number][:, :LANES] = dots_ref[here, :]
 
 
 def back_rows(lefts, weights, dots, table, groups, after=()):
@@ -564,19 +602,30 @@
         functools.partial(back_rows_kernel, min(512, tokens), count, len(after)),
         grid_spec=pltpu.PrefetchScalarGridSpec(
             num_scalar_prefetch=1,
-            grid=(width // block,),
+            grid=(width // block + 1,),
             in_specs=[whole_spec(left.shape) for left in lefts]
-            + [pl.BlockSpec((experts, block, hid), lambda d, _: (0, d, 0))] * count
+            + [
+                pl.BlockSpec(
+                    (experts, block, hid),
+                    lambda d, _: (0, jnp.minimum(d, width // block - 1), 0),
+                )
+            ]
+            * count
             + [whole_spec(dots.shape)]
             + [ANY] * len(after),
-            out_specs=[whole_spec((len(group), part_rows, width + LANES)) for group in groups],
-            scratch_shapes=[pltpu.VMEM((block, experts * hid), BF)] * count
-            + [pltpu.VMEM(left.shape, BF) for left in lefts],
+            out_specs=[
+                pl.BlockSpec((len(group), part_rows, block), lambda d, _: (0, 0, d))
+                for group in groups
+            ],
+            scratch_shapes=[
+                pltpu.VMEM((block, count * experts * hid), BF),
+                pltpu.VMEM((tokens, count * experts * hid), BF),
+            ],
         ),
         out_shape=[
             jax.ShapeDtypeStruct((len(group), part_rows, width + LANES), F32) for group in groups
         ],
-        compiler_params=params(56),
+        compiler_params=params(58),
         cost_estimate=cost(
             2 * count * tokens * width * experts * hid, (4 + 4 * count) * tokens * width
         ),
@@ -654,14 +703,13 @@
     )(*lefts, *after, *[item for chunk in rights for item in chunk])
 
 
-def branch_kernel(count, after, table_ref, *refs):
+def branch_kernel(count, after, *refs):
     pieces = refs[:count]
     w_ref, x_ref, gain_ref, router_ref = refs[count : count + 4]
     mid_ref, mixed_ref, logit_ref, all_ref = refs[count + 4 + after :]
     share = pieces[0].shape[1]
     for index, piece in enumerate(pieces):
-        span = pl.ds(pl.multiple_of(table_ref[index] * share, LANES), share)
-        all_ref[:, span] = piece[...].astype(BF)
+        all_ref[:, index * share : (index + 1) * share] = piece[...].astype(BF)
     middle = x_ref[...].astype(F32) + dot(all_ref[...], w_ref[...], 1, 1)
     mid_ref[...] = middle
     mid_hat = middle * norm_scale(middle)
@@ -670,7 +718,7 @@
     logit_ref[...] = dot(mixed, router_ref[...])
 
 
-def branch(pieces, table, w_out, hidden, chunk, gain, w_router, after=()):
+def branch(pieces, w_out, hidden, chunk, gain, w_router, after=()):
     tokens, share = pieces[0].shape
     width, full = w_out.shape
     rows = min(256, tokens)
@@ -678,56 +726,60 @@
     experts = w_router.shape[1]
     return pl.pallas_call(
         functools.partial(branch_kernel, len(pieces), len(after)),
-        grid_spec=pltpu.PrefetchScalarGridSpec(
-            num_scalar_prefetch=1,
-            grid=(steps,),
-            in_specs=[pl.BlockSpec((rows, share), lambda i, _: (i, 0))] * len(pieces)
-            + [
-                whole_spec(w_out.shape),
-                pl.BlockSpec((rows, width), lambda i, _: (chunk * steps + i, 0)),
-                whole_spec((1, width)),
-                whole_spec(w_router.shape),
-            ]
-            + [ANY] * len(after),
-            out_specs=[
-                pl.BlockSpec((rows, width), lambda i, _: (i, 0)),
-                pl.BlockSpec((rows, width), lambda i, _: (i, 0)),
-                pl.BlockSpec((rows, experts), lambda i, _: (i, 0)),
-                pl.BlockSpec((rows, full), lambda i, _: (i, 0)),
-            ],
-        ),
+        grid=(steps,),
+        in_specs=[pl.BlockSpec((rows, share), lambda i: (i, 0))] * len(pieces)
+        + [
+            whole_spec(w_out.shape),
+            pl.BlockSpec((rows, width), lambda i: (chunk * steps + i, 0)),
+            whole_spec((1, width)),
+            whole_spec(w_router.shape),
+        ]
+        + [ANY] * len(after),
+        out_specs=[
+            pl.BlockSpec((rows, width), lambda i: (i, 0)),
+            pl.BlockSpec((rows, width), lambda i: (i, 0)),
+            pl.BlockSpec((rows, experts), lambda i: (i, 0)),
+            pl.BlockSpec((rows, full), lambda i: (i, 0)),
+        ],
         out_shape=[
             jax.ShapeDtypeStruct((tokens, width), F32),
             jax.ShapeDtypeStruct((tokens, width), BF),
             jax.ShapeDtypeStruct((tokens, experts), F32),
             jax.ShapeDtypeStruct((tokens, full), BF),
         ],
-        compiler_params=params(56),
+        compiler_params=params(58),
         cost_estimate=cost(2 * tokens * width * full, 16 * tokens * width),
         name="branch",
-    )(table, *pieces, w_out, hidden, gain.reshape(1, -1), w_router, *after)
-
-
-def cast_kernel(in_ref, out_ref):
-    out_ref[...] = in_ref[...].astype(out_ref.dtype)
-
-
-def cast(value):
-    rows, columns = value.shape
-    block = pl.BlockSpec((min(256, rows), columns), lambda i: (i, 0))
+    )(*pieces, w_out, hidden, gain.reshape(1, -1), w_router, *after)
+
+
+def cast_kernel(table_ref, in_ref, out_ref):
+    wide = in_ref.shape[3]
+    for index in range(in_ref.shape[1]):
+        span = slice(index * wide, (index + 1) * wide)
+        out_ref[:, span] = in_ref[0, table_ref[index]].astype(out_ref.dtype)
+
+
+def cast(parts, table):
+    count, blocks, rows, wide = parts.shape
+    step = min(256, rows)
+    per = rows // step
     return pl.pallas_call(
         cast_kernel,
-        grid=(rows // min(256, rows),),
-        in_specs=[block],
-        out_specs=block,
-        out_shape=jax.ShapeDtypeStruct(value.shape, BF),
-        compiler_params=params(32),
-        cost_estimate=cost(0, 6 * value.size),
+        grid_spec=pltpu.PrefetchScalarGridSpec(
+            num_scalar_prefetch=1,
+            grid=(count, per),
+            in_specs=[pl.BlockSpec((1, blocks, step, wide), lambda d, i, _: (d, 0, i, 0))],
+            out_specs=pl.BlockSpec((step, blocks * wide), lambda d, i, _: (d * per + i, 0)),
+        ),
+        out_shape=jax.ShapeDtypeStruct((count * rows, blocks * wide), BF),
+        compiler_params=params(58),
+        cost_estimate=cost(0, 6 * parts.size),
         name="cast",
-    )(value)
-
-
-def send_back_kernel(after, table_ref, low_ref, w_ref, *outs):
+    )(table, parts)
+
+
+def send_back_kernel(after, low_ref, w_ref, *outs):
     for number, out_ref in enumerate(outs[after:]):
 
         @pl.when(pl.program_id(0) == number)
@@ -735,78 +787,125 @@
             out_ref[...] = dot(low_ref[...], w_ref[...]).astype(BF).astype(F32)
 
 
-def send_back(low, w_out, table, after=()):
+def send_back(low, w_out, parts, after=()):
     rows, width = low.shape
-    parts = table.shape[0]
     full = w_out.shape[1]
     block = full // parts
     return pl.pallas_call(
         functools.partial(send_back_kernel, len(after)),
-        grid_spec=pltpu.PrefetchScalarGridSpec(
-            num_scalar_prefetch=1,
-            grid=(parts,),
-            in_specs=[
-                whole_spec(low.shape),
-                pl.BlockSpec((width, block), lambda k, table: (0, table[k])),
-            ]
-            + [ANY] * len(after),
-            out_specs=[whole_spec((rows, block))] * parts,
-        ),
+        grid=(parts,),
+        in_specs=[whole_spec(low.shape), pl.BlockSpec((width, block), lambda k: (0, k))]
+        + [ANY] * len(after),
+        out_specs=[whole_spec((rows, block))] * parts,
         out_shape=[jax.ShapeDtypeStruct((rows, block), F32)] * parts,
-        compiler_params=params(32),
+        compiler_params=params(58),
         cost_estimate=cost(2 * rows * width * full, 2 * width * full + 8 * rows * full),
         name="send_back",
-    )(table, low, w_out, *after)
+    )(low, w_out, *after)
 
 
 def outer_kernel(after, table_ref, columns_ref, left_ref, right_ref, *outs):
-    for number, out_ref in enumerate(outs[after:]):
-
-        @pl.when(pl.program_id(0) == number)
+    number = pl.program_id(0) * 2 + pl.program_id(1)
+    for index, out_ref in enumerate(outs[after:]):
+
+        @pl.when(number == index)
         def _(out_ref=out_ref):
-            out_ref[0] = dot(left_ref[...], right_ref[...])
+            for part in range(out_ref.shape[0]):
+                wide = out_ref.shape[2]
+                place = columns_ref[(index % 2) * out_ref.shape[0] + part] * wide
+                right = right_ref[:, pl.ds(pl.multiple_of(place, LANES), wide)]
+                out_ref[part] = dot(left_ref[...], right)
 
 
 def outer(left, right, table, columns, after=()):
     width, rows = left.shape
     parts, pieces = table.shape[0], columns.shape[0]
     high, wide = width // parts, right.shape[1] // pieces
-    out_specs = [
-        pl.BlockSpec(
-            (1, high, wide),
-            lambda k, m, *_, number=number: (
-                jnp.where(k < number, 0, jnp.where(k > number, pieces - 1, m)),
-                0,
-                0,
-            ),
-        )
-        for number in range(parts)
-    ]
+    shape = (pieces // 2, high, wide)
+    steps = 2
     return pl.pallas_call(
         functools.partial(outer_kernel, len(after)),
         grid_spec=pltpu.PrefetchScalarGridSpec(
             num_scalar_prefetch=2,
-            grid=(parts, pieces),
+            grid=(parts, 2, steps),
             in_specs=[
-                pl.BlockSpec((high, rows), lambda k, m, table, columns: (table[k], 0)),
-                pl.BlockSpec((rows, wide), lambda k, m, table, columns: (0, columns[m])),
+                pl.BlockSpec(
+                    (high // steps, rows), lambda k, m, i, table, columns: (table[k] * steps + i, 0)
+                ),
+                whole_spec(right.shape),
             ]
             + [ANY] * len(after),
-            out_specs=out_specs,
+            out_specs=[
+                pl.BlockSpec(
+                    (pieces // 2, high // steps, wide),
+                    lambda k, m, i, *_, index=index: (
+                        0,
+                        jnp.where(
+                            k * 2 + m < index, 0, jnp.where(k * 2 + m > index, steps - 1, i)
+                        ),
+                        0,
+                    ),
+                )
+                for index in range(2 * parts)
+            ],
         ),
-        out_shape=[jax.ShapeDtypeStruct((pieces, high, wide), F32)] * parts,
-        compiler_params=params(32),
+        out_shape=[jax.ShapeDtypeStruct(shape, F32)] * (2 * parts),
+        compiler_params=params(58),
         cost_estimate=cost(2 * width * rows * right.shape[1], 4 * width * right.shape[1]),
         name="outer",
     )(table, columns, left, right, *after)
 
 
-def plain_acts(mixed, dy, chunk, gates, w_gate, w_up, w_down, after=(), last=False):
-    dy = lax.dynamic_slice_in_dim(dy, chunk * mixed.shape[0], mixed.shape[0], 0)
+def in_grads_kernel(count, after, table_ref, left_ref, *refs):
+    rights, refs = refs[:count], refs[count + after :]
+    outs, held = refs[:-1], refs[-1]
+    wide = rights[0].shape[1]
+
+    @pl.when(pl.program_id(0) == 0)
+    def _():
+        for index, right in enumerate(rights):
+            held[:, index * wide : (index + 1) * wide] = right[...]
+
+    for number, out_ref in enumerate(outs):
+
+        @pl.when(pl.program_id(0) == number)
+        def _(out_ref=out_ref):
+            out_ref[...] = dot(left_ref[...].T, held[...])
+
+
+def in_grads_of(left, rights, table, after=()):
+    tokens, width = left.shape
+    parts, count = table.shape[0], len(rights)
+    wide = rights[0].shape[1]
+    high = width // parts
+    return pl.pallas_call(
+        functools.partial(in_grads_kernel, count, len(after)),
+        grid_spec=pltpu.PrefetchScalarGridSpec(
+            num_scalar_prefetch=1,
+            grid=(parts,),
+            in_specs=[pl.BlockSpec((tokens, high), lambda k, table: (0, table[k]))]
+            + [whole_spec(right.shape) for right in rights]
+            + [ANY] * len(after),
+            out_specs=[whole_spec((high, count * wide))] * parts,
+            scratch_shapes=[pltpu.VMEM((tokens, count * wide), BF)],
+        ),
+        out_shape=[jax.ShapeDtypeStruct((high, count * wide), F32)] * parts,
+        compiler_params=params(58),
+        cost_estimate=cost(0, 0, True),
+        name="in_grads",
+    )(table, left, *rights, *after)
+
+
+def plain_low(dy, w_down, chunk, tokens, after=(), last=False):
+    dy = lax.slice_in_dim(dy, chunk * tokens, (chunk + 1) * tokens, axis=0)
+    low = jnp.einsum("td,edh->teh", dy, w_down, preferred_element_type=F32)
+    return low.reshape(tokens, -1)
+
+
+def plain_acts(mixed, low, gates, w_gate, w_up, after=(), last=False):
     acts = jnp.einsum("td,edh->teh", mixed, w_gate, preferred_element_type=F32)
     ups = jnp.einsum("td,edh->teh", mixed, w_up, preferred_element_type=F32)
-    low = jnp.einsum("td,edh->teh", dy, w_down, preferred_element_type=F32)
-    gi, gg, ug, terms = expert_terms(acts, ups, low, gates[:, :, None])
+    gi, gg, ug, terms = expert_terms(acts, ups, low.reshape(acts.shape), gates[:, :, None])
     flat = (mixed.shape[0], -1)
     dots = jnp.pad(jnp.sum(terms, axis=2), ((0, 0), (0, LANES - gates.shape[1])))
     return gi.reshape(flat), gg.reshape(flat), ug.reshape(flat), dots
@@ -871,61 +970,43 @@
     return lax.ppermute(value, axis, [(i, i ^ step) for i in range(count)])
 
 
-def reduce_blocks(blocks, axis="tensor"):
+def reduce_blocks(blocks, axis="tensor", start=1):
     blocks = list(blocks)
-    live = list(range(len(blocks)))
+    live = [k for k in range(len(blocks)) if not k % start]
     for bit in bits_of(len(blocks)):
+        if bit < start:
+            continue
         for k in sorted((k for k in live if k & bit), reverse=True):
             blocks[k ^ bit] = blocks[k ^ bit] + swap(blocks[k], axis, bit)
         live = [k for k in live if not k & bit]
     return blocks[0]
 
 
-def stage_kernel(sizes, skip, *refs):
-    count = sum(sizes)
-    terms = refs[:count]
-    outs = list(refs[count + skip :])
-    used = 0
-    for size in sizes:
-        total = terms[used][...]
-        for term in terms[used + 1 : used + size]:
-            total = total + term[...]
-        used += size
-        done = 0
-        while done < total.shape[0]:
-            out = outs.pop(0)
-            out[...] = total[done : done + out.shape[0]]
-            done += out.shape[0]
-
-
-def stage(sums, passes=(), after=()):
+def stage_kernel(count, parts, skip, *refs):
+    terms, out = refs[:count], refs[count + skip]
+    total = terms[0][...]
+    for term in terms[1:]:
+        total = total + term[...]
+    out[...] = total
+
+
+def stage(parts, terms, passes=(), after=()):
     steps = 4
-    terms = [term for _, group in sums for term in group]
-    in_specs, out_specs, out_shape = [], [], []
-    for term in terms:
-        parts, rows, columns = term.shape
-        in_specs.append(pl.BlockSpec((parts, rows // steps, columns), lambda i: (0, i, 0)))
-    for cuts, group in sums:
-        _, rows, columns = group[0].shape
-        for parts in cuts:
-            out_specs.append(pl.BlockSpec((parts, rows // steps, columns), lambda i: (0, i, 0)))
-            out_shape.append(jax.ShapeDtypeStruct((parts, rows, columns), F32))
-    made = len(out_shape)
-    out_shape += [jax.ShapeDtypeStruct(item.shape, item.dtype) for item in passes]
+    _, rows, columns = terms[0].shape
+    block = pl.BlockSpec((parts, rows // steps, columns), lambda i: (0, i, 0))
     outs = pl.pallas_call(
-        functools.partial(
-            stage_kernel, tuple(len(group) for _, group in sums), len(passes) + len(after)
-        ),
+        functools.partial(stage_kernel, len(terms), parts, len(passes) + len(after)),
         grid=(steps,),
-        in_specs=in_specs + [ANY] * (len(passes) + len(after)),
-        out_specs=out_specs + [ANY] * len(passes),
-        out_shape=out_shape,
-        input_output_aliases={len(terms) + i: made + i for i in range(len(passes))},
-        compiler_params=params(32),
-        cost_estimate=cost(0, sum(4 * term.size for term in terms) * 4 // 3),
+        in_specs=[block] * len(terms) + [ANY] * (len(passes) + len(after)),
+        out_specs=[block] + [ANY] * len(passes),
+        out_shape=[jax.ShapeDtypeStruct((parts, rows, columns), F32)]
+        + [jax.ShapeDtypeStruct(item.shape, item.dtype) for item in passes],
+        input_output_aliases={len(terms) + i: 1 + i for i in range(len(passes))},
+        compiler_params=params(58),
+        cost_estimate=cost(0, 4 * parts * rows * columns * (len(terms) + 1)),
         name="stage",
     )(*terms, *passes, *after)
-    return outs[:made], outs[made:]
+    return outs[0], outs[1:]
 
 
 def tie_kernel(*refs):
@@ -940,6 +1021,7 @@
         out_shape=[jax.ShapeDtypeStruct(value.shape, value.dtype) for value in values],
         input_output_aliases={i: i for i in range(len(values))},
         compiler_params=params(58),
+        cost_estimate=cost(0, 0, True),
         name="tie",
     )(*values, *after)
 
@@ -960,35 +1042,29 @@
     def send_far(self):
         self.got_far = swap(self.four, "tensor", 4)
 
+    def result(self):
+        return self.four_zero[1] + self.got_second[1] + self.got_near[1] + self.got_far[0]
+
 
 def odd_stage(ending, starting, passes=(), after=(), hold=False):
-    sums = []
-    passes = list(passes)
-    if starting is not None:
-        sums.append(((2,), (starting.six_two, starting.got_first)))
-        passes.append(starting.second)
     if ending is not None:
-        sums.append(((1,), (ending.zero, ending.got_far)))
-    made, passes = stage(sums, passes, after)
-    if ending is not None:
-        ending.result = made[-1]
-    if starting is not None:
-        starting.six_two = made[0]
-        starting.second = passes[-1]
-        if not hold:
-            starting.send_second()
-        passes = passes[:-1]
-    return passes
+        after = (*after, ending.got_far)
+    passes = (*passes, starting.second)
+    starting.six_two, passes = stage(
+        2, (starting.six_two, starting.got_first), passes, after
+    )
+    starting.second = passes[-1]
+    if not hold:
+        starting.send_second()
+    return passes[:-1]
 
 
 def even_stage(middle, coming, passes=(), after=()):
-    passes = list(passes)
     if coming is not None:
-        passes.append(coming.first)
-    made, passes = stage(
-        [((1, 1), (middle.four_zero, middle.got_second, middle.got_near))], passes, after
-    )
-    middle.four, middle.zero = made
+        passes = (*passes, coming.first)
+    middle.four, passes = stage(
+        1, (middle.four_zero, middle.got_second, middle.got_near), passes, after
+    )
     middle.send_far()
     if coming is not None:
         coming.first = passes[-1]
@@ -997,6 +1073,12 @@
     return passes
 
 
+def reduce_first(blocks, axis):
+    return [
+        item + swap(blocks[k + 1], axis, 1) if not k & 1 else item for k, item in enumerate(blocks)
+    ]
+
+
 def halves_order(count):
     bits = bits_of(count)
     return [
@@ -1004,11 +1086,14 @@
     ]
 
 
-def reduce_halves(stacked, axis="tensor"):
-    for bit in bits_of(stacked.shape[0]):
-        half = stacked.shape[0] // 2
-        stacked = stacked[:half] + swap(stacked[half:], axis, bit)
-    return stacked[0]
+def reduce_halves(low, high, axis="tensor", start=1):
+    for bit in bits_of(2 * start * low.shape[0]):
+        if bit < start:
+            continue
+        total = low + swap(high, axis, bit)
+        half = total.shape[0] // 2
+        low, high = total[:half], total[half:]
+    return total[0]
 
 
 def gather_blocks(value):
@@ -1063,6 +1148,7 @@
     scale = 1.0 / math.sqrt(HEAD)
     tiled = w_gate.shape[2] % LANES == 0
     acts_of = expert_acts if tiled else plain_acts
+    low_of = low_grads if tiled else plain_low
     columns_of = back_columns if tiled else plain_columns
     rows_of = back_rows if tiled else plain_rows
     grads_of = expert_grads if tiled else plain_grads
@@ -1071,11 +1157,11 @@
 
     part = width // dp_count
     w_part = lax.dynamic_slice_in_dim(w_out, dp_rank * part, part, 0).astype(F32)
-    w_part = lax.all_gather(w_part, "tensor", axis=1, tiled=True)
-
-    hidden = hidden_in.astype(F32)
-    in_scale = norm_scale(hidden)
-    in_hat = hidden * in_scale
+    if count == 8:
+        w_part = lax.all_gather(w_part, "tensor", axis=0, tiled=False)
+    staged = count == 8 and seqs == 2
+
+    in_scale = norm_scale(hidden_in.astype(F32))
     normed, query_raw, key_raw, value_low, square_sums = project(
         hidden_in, gain_in, w_query, w_key, w_value
     )
@@ -1090,21 +1176,52 @@
     counts = hits.astype(jnp.int32)
     kept_all = hits & (jnp.cumsum(counts, axis=0, dtype=jnp.int32) - counts < CAP)
 
-    pieces, last, query_low, key_low = [], None, [], []
-    for c in chunks:
-        last, query_c, key_c = attend(
+    query_low, key_low = [], []
+
+    def attend_of(c, after=()):
+        attended_c, query_c, key_c = attend(
             query_raw, key_raw, value_low, square_sums, gains_here, angles, segments, c, scale,
-            full_width,
+            full_width, after,
         )
         query_low.append(query_c)
         key_low.append(key_c)
-        pieces.append(gather_blocks(last))
+        return attended_c
+
+    pieces, low = [], []
+    if staged:
+        first = attend_of(0)
+        near = swap(first, "tensor", 2)
+        odd = [swap(first, "tensor", 1)]
+        second = attend_of(1, (first,))
+        near, again = tie((near, first), (odd[0], second))
+        far = swap(again, "tensor", 4)
+        odd.append(swap(near, "tensor", 1))
+        (w_part,) = tie((w_part,), (near,))
+        low.append(low_of(cotangent, w_down, 0, length, (near,)))
+        low.append(low_of(cotangent, w_down, 1, length, (low[0],), True))
+        w_whole = cast(lax.all_gather(w_part, "dp", axis=0, tiled=False), table)
+        (far,) = tie((far,), (odd[1], low[1]))
+        both = swap(far, "tensor", 2)
+        odd.append(swap(far, "tensor", 1))
+        both, second = tie((both, second), (odd[2],))
+        odd.append(swap(both, "tensor", 1))
+        even = [again, near, far, both]
+        pieces.append([item for pair in zip(even, odd) for item in pair])
+        near = swap(second, "tensor", 2)
+        near, again = tie((near, second), (odd[3],))
+        far = swap(again, "tensor", 4)
+        odd = [swap(again, "tensor", 1), swap(near, "tensor", 1)]
+    else:
+        for c in chunks:
+            pieces.append(gather_blocks(attend_of(c)))
+            low.append(low_of(cotangent, w_down, c, length))
     query_low = jnp.concatenate(query_low, axis=0)
     key_low = jnp.concatenate(key_low, axis=0)
-    w_part, _ = lax.optimization_barrier((w_part, last))
-    w_whole = cast(lax.all_gather(w_part, "dp", axis=0, tiled=True))
-
-    staged = count == 8 and seqs == 2
+    if not staged:
+        w_part = jnp.stack(gather_blocks(w_part)) if count != 8 else w_part
+        w_table = jnp.arange(count, dtype=jnp.int32) if count != 8 else table
+        w_whole = cast(lax.all_gather(w_part, "dp", axis=0, tiled=False), w_table)
+
     groups = Chain.groups if staged else tuple((k,) for k in range(count))
 
     def plain_reduce(parts):
@@ -1114,7 +1231,7 @@
 
     def forward(c, after, last=False):
         mid_c, mixed_c, logits_c, attended_c = branch(
-            pieces[c], table, w_whole, hidden_in, c, gain_mid, w_router, after
+            pieces[c], w_whole, hidden_in, c, gain_mid, w_router, after
         )
         middle.append(mid_c)
         mixed.append(mixed_c)
@@ -1122,7 +1239,7 @@
         probs.append(jax.nn.softmax(logits_c, axis=-1))
         kept.append(lax.slice_in_dim(kept_all, c * length, (c + 1) * length, axis=0))
         gates.append(jnp.where(kept[c], probs[c], 0.0))
-        return acts_of(mixed_c, cotangent, c, gates[c], w_gate, w_up, w_down, (), last)
+        return acts_of(mixed_c, low[c], gates[c], w_gate, w_up, (), last)
 
     def mixed_blocks(c, after=()):
         return rows_of(acts[c][1:3], [w_gate, w_up], acts[c][3], table, groups, after)
@@ -1144,13 +1261,20 @@
 
     if staged:
         acts = [forward(0, ())]
+        (far,) = tie((far,), (middle[0],))
+        both = swap(far, "tensor", 2)
+        odd.append(swap(far, "tensor", 1))
+        (both,) = tie((both,), (acts[0][0],))
+        odd.append(swap(both, "tensor", 1))
+        even = [again, near, far, both]
+        pieces.append([item for pair in zip(even, odd) for item in pair])
         mix = [Chain(mixed_blocks(0))]
         mix[0].send_first()
         acts.append(forward(1, (mix[0].four_zero,), True))
         odd_stage(None, mix[0], after=(acts[1][0],))
         mix.append(Chain(mixed_blocks(1, (mix[0].six_two,))))
         even_stage(mix[0], mix[1])
-        moe = [Chain(moe_of(0, (mix[0].zero,)))]
+        moe = [Chain(moe_of(0, (mix[0].four,)))]
         odd_stage(mix[0], mix[1], after=(moe[0].four_zero,))
     else:
         acts = []
@@ -1171,9 +1295,9 @@
     if staged:
         grad_down = down_grads((mix[1].six_two, probs_own, mid_own, mixed_own, attended_own))
         (grad_down,) = even_stage(mix[1], moe[0], passes=(grad_down,))
-        grad_gate, grad_up = act_grads((mix[1].zero,))
+        grad_gate, grad_up = act_grads((mix[1].four,))
         grad_gate, grad_up = odd_stage(mix[1], moe[0], passes=(grad_gate, grad_up))
-        mixed_share = [item.result[0] for item in mix]
+        mixed_share = [item.result() for item in mix]
 
     mixed_share = jnp.concatenate(mixed_share, axis=0)
     prob_grad = jnp.where(kept_own, mixed_share[:, width : width + experts], 0.0)
@@ -1192,12 +1316,16 @@
     if staged:
         moe.append(Chain(moe_of(1, (mid_low,), True)))
         (mid_low,) = even_stage(moe[0], moe[1], passes=(mid_low,))
-    blocks = send_back(mid_low, w_whole, table)
+    blocks = send_back(mid_low, w_whole, count)
     attended_grad = jnp.stack(exchange_blocks(blocks))
+
+    dp_table = dp_rank ^ jnp.arange(dp_count, dtype=jnp.int32)
+    order = jnp.array(halves_order(count), jnp.int32)
+    out_parts = outer(mid_low.T, attended_own, dp_table, order, (blocks[0],))
 
     q_scaled, k_scaled, value_grad, totals, gain_parts = attend_back(
         query_low, key_low, value_low, attended_grad, raws, square_sums, gains_here, angles,
-        table, segments, scale, full_width,
+        table, segments, scale, full_width, (out_parts[0],),
     )
     if staged:
         (totals,) = odd_stage(moe[0], moe[1], passes=(totals,), hold=True)
@@ -1225,15 +1353,30 @@
         moe[1].send_second()
         norm = [Chain(normed_blocks(c)) for c in chunks]
         even_stage(moe[1], norm[0], after=(norm[1].four_zero,))
-        odd_stage(moe[1], norm[0])
+        grad_in = in_grads_of(normed, in_grads, dp_table, (moe[1].four,))
+        odd_stage(moe[1], norm[0], after=(grad_in[0],))
         even_stage(norm[0], norm[1])
-        odd_stage(norm[0], norm[1])
-        even_stage(norm[1], None)
-        odd_stage(norm[1], None)
-        normed_share = [item.result[0] for item in norm]
-        moe_share = [item.result[0] for item in moe]
+        out_high = reduce_blocks(out_parts[1::2], "dp")
+        odd_stage(norm[0], norm[1], after=(out_high,))
+        out_low = reduce_blocks(out_parts[::2], "dp")
+        grad_in = reduce_blocks(grad_in, "dp")
+        (out_high,) = even_stage(norm[1], None, passes=(out_high,), after=(out_low, grad_in))
+        grad_w_out = reduce_halves(out_low, out_high)
+        normed_share = [item.result() for item in norm]
+        moe_share = [item.result() for item in moe]
     else:
         normed_share = [plain_reduce(normed_blocks(c)) for c in chunks]
+        out_low = reduce_blocks(out_parts[::2], "dp")
+        out_high = reduce_blocks(out_parts[1::2], "dp")
+        grad_in = dot(normed, jnp.concatenate(in_grads, axis=1), 0, 0)
+        grad_in = reduce_blocks(
+            [
+                lax.dynamic_slice_in_dim(grad_in, dp_table[k] * part, part, 0)
+                for k in range(dp_count)
+            ],
+            "dp",
+        )
+        grad_w_out = reduce_halves(out_low, out_high)
     output = jnp.concatenate(
         [(columns_own(middle[c]) + moe_share[c]).astype(BF) for c in chunks], axis=0
     )
@@ -1241,41 +1384,33 @@
     def over_dp(grad):
         return lax.psum_scatter(grad, "dp", scatter_dimension=0, tiled=True)
 
-    dp_table = dp_rank ^ jnp.arange(dp_count, dtype=jnp.int32)
-    order = rank ^ jnp.array(halves_order(count), jnp.int32)
-    out_part = reduce_blocks(outer(mid_low.T, attended_own, dp_table, order, (blocks[0],)), "dp")
-    grad_w_out = reduce_halves(out_part)
-
-    grad_in = dot(normed, jnp.concatenate(in_grads, axis=1), 0, 0)
-    grad_in = reduce_blocks(
-        [lax.dynamic_slice_in_dim(grad_in, dp_table[k] * part, part, 0) for k in range(dp_count)],
-        "dp",
-    )
     grad_w_query, grad_w_key, grad_w_value = (
         grad_in[:, i * local_width : (i + 1) * local_width] for i in range(3)
     )
 
     normed_share = jnp.concatenate(normed_share, axis=0)
-    in_hat_share = columns_own(in_hat)
+    in_hat_share = columns_own(hidden_in).astype(F32) * in_scale
     gain_share = lax.dynamic_slice_in_dim(gain_in.astype(F32), rank * share, share, 0)
     in_scaled = normed_share * gain_share
     row_sums = jnp.sum(in_scaled * in_hat_share, axis=1).reshape(seqs, length)
     direct_sums = jnp.sum(mid_grad * own_hat, axis=1) / own_scale[:, 0]
     mine = lax.dynamic_slice_in_dim(row_sums, rank * own, own, 1) - direct_sums.reshape(seqs, own)
     row_sums = lax.dynamic_update_slice_in_dim(row_sums, mine, rank * own, 1)
-    row_totals = small_sum(row_sums.reshape(1, tok_rows), "tensor")[0]
+    grad_router = dot(logit_own, mixed_own, 0, 0)
+    direct_gain = jnp.sum(direct * own_hat, axis=0)
+    wide = jnp.concatenate([grad_router, grad_gain_mid[None], direct_gain[None]], axis=0)
+    wide = small_sum(wide, "dp")
+    direct_gain = wide[experts + 1]
+    wide = lax.dynamic_slice_in_dim(wide[: experts + 1], dp_rank * part, part, 1)
+    flat = [row_sums.reshape(-1), wide.reshape(-1), direct_gain]
+    flat = small_sum(jnp.concatenate(flat)[None], "tensor")[0]
+    row_totals = flat[:tok_rows]
+    wide = flat[tok_rows : tok_rows + wide.size].reshape(wide.shape)
+    direct_gain = lax.dynamic_slice_in_dim(flat[-width:], rank * share, share, 0)
     grad_input = (
         in_scale * (in_scaled - in_hat_share * (row_totals / width)[:, None])
     ).astype(BF)
-    direct_gain = jnp.sum(direct * own_hat, axis=0)
-    grad_router = dot(logit_own, mixed_own, 0, 0)
-    wide = jnp.concatenate([grad_router, grad_gain_mid[None], direct_gain[None]], axis=0)
-    wide = small_sum(wide, "tensor")
-    direct_gain = lax.dynamic_slice_in_dim(wide[experts + 1], rank * share, share, 0)
-    grad_gain_in = jnp.sum(normed_share * in_hat_share, axis=0) - direct_gain
-
-    wide = small_sum(wide[: experts + 1], "dp")
-    wide = lax.dynamic_slice_in_dim(wide, dp_rank * part, part, 1)
+    grad_gain_in = jnp.sum(normed_share * in_hat_share, axis=0)
     gains = jnp.concatenate([grad_gain_in, gain_parts[0], gain_parts[1]])
     gains = small_sum(gains[None], "dp")[0]
 
@@ -1286,7 +1421,7 @@
         grad_w_key,
         grad_w_value,
         grad_w_out,
-        gains[:share],
+        gains[:share] - direct_gain,
         gains[share : share + local_width],
         gains[share + local_width :],
         wide[experts],

time: 1310 us -> 1220 us (0.931)
  waiting for transfers between devices: 536 us -> 454 us
  Pallas kernels: 522 us -> 505 us
    ppermute x70, waiting for transfers between devices: 501 us -> 454 us  [swap(): return lax.ppermute(value, axis, [(i, i ^ step) for i in range(count)])]
    all_gather x2, waiting for transfers between devices: 35.4 us -> 0.01 us  [the longest x1 0.01 us: on_device(): w_part = lax.all_gather(w_part, 'tensor', axis=0, tiled=False)]
    convert_element_type x2 -> x0, other arithmetic: 13.1 us -> none  [the longest x1 11.3 us: on_device(): hidden = hidden_in.astype(F32)]
    unnamed x142 -> x180, local copies, waits for them, and re-layouts: 26.5 us -> 38.7 us
    pallas_call x17 -> x19, Pallas kernels: 176 us -> 177 us  [the longest x2 62.3 us: expert_acts(): pl.pallas_call(functools.partial(expert_kernel, min(512, tokens), len(aft...]
  transfers between devices with their start and end apart: 75 -> 75, of which waited for: 40 -> 37; matrix products, arithmetic and copies ran while one was open for 10% -> 10% of each run, Pallas kernels for 39% -> 41%
where the time goes in v3:
time: 1220 us; the launch traced here: 1210 us
  Pallas kernels  505 us (41%)
  waiting for transfers between devices  454 us (37%)
  starting transfers between devices  82.7 us (7%)
  other arithmetic  80.6 us (7%)
  local copies, waits for them, and re-layouts  66.9 us (5%)
  between operations  15.2 us (1%)
    ppermute x70, waiting for transfers between devices, swap(): return lax.ppermute(value, axis, [(i, i ^ step) for i in range(count)])  454 us
    pallas_call x2, Pallas kernels, expert_grads(): pl.pallas_call(functools.partial(grads_kernel, min(512, width), chunks, l...  81.9 us
    ppermute x70, starting transfers between devices, swap(): return lax.ppermute(value, axis, [(i, i ^ step) for i in range(count)])  81.8 us
    pallas_call x4, Pallas kernels, back_columns(): pl.pallas_call(functools.partial(back_columns_kernel, min(512, tokens), c...  71.4 us
    pallas_call x2, Pallas kernels, expert_acts(): pl.pallas_call(functools.partial(expert_kernel, min(512, tokens), len(aft...  62.3 us
    pallas_call x2, Pallas kernels, back_rows(): pl.pallas_call(functools.partial(back_rows_kernel, min(512, tokens), coun...  55 us
    pallas_call x12, Pallas kernels, stage(): pl.pallas_call(functools.partial(stage_kernel, len(terms), parts, len(pas...  48.6 us
    unnamed x180, local copies, waits for them, and re-layouts  38.7 us
  transfers between devices with their start and end apart: 75, of which 37 were waited for; matrix products, arithmetic and copies ran while one was open for 10% of the time, Pallas kernels for 41%

profile of v3, /device:TPU:0, one launch (start us, length us, event | category | flops | bytes accessed | tf_op | source)
XLA Modules:
  0.0 1206.0 jit_solution(328399084970352476)
XLA Ops:
  68.2 28.2 %collective-permute-done.4.refs_2_.refs_1_ = f32[1024,256]{1,0:T(8,128)S(1)} collective-permute-done((f32[1024,256]{1,0:T(8,128)}, f32[1024,256]{1,0:T(8,128)S(1)}, u32[]{:S(2)}, u32[]{:S(2)}) %collective-permute-start.4) | collective-permute-done | bytes 1048608 | tf_op jit(solution)/shard_map/ppermute | solution.py:970
  113.3 16.1 %low_grads.2.refs_0_.low_ref = f32[1024,2048]{1,0:T(8,128)} custom-call(bf16[2048,2048]{1,0:T(8,128)(2,1)} %refs_1_.4, bf16[16,2048,128]{2,1,0:T(8,128)(2,1)} %refs_1_.5, f32[1024,256]{1,0:T(8,128)} %get-tuple-element.138.refs_0_.refs_1_.refs_2_), custom_call_target="tpu_custom_call" | custom-call | flops 34359738368 | bytes 16777216 | tf_op jit(solution)/shard_map/low_grads/pallas_call | solution.py:405
  129.4 15.4 %low_grads.3.refs_2_.low_ref = f32[1024,2048]{1,0:T(8,128)} custom-call(bf16[2048,2048]{1,0:T(8,128)(2,1)} %refs_1_.4, bf16[16,2048,128]{2,1,0:T(8,128)(2,1)} %refs_1_.5, f32[1024,2048]{1,0:T(8,128)} %low_grads.2.refs_0_.low_ref), custom_call_target="tpu_custom_call" | custom-call | flops 1024 | bytes 1024 | tf_op jit(solution)/shard_map/low_grads/pallas_call | solution.py:405
  144.7 14.5 %collective-permute-done.6.refs_0_ = f32[1024,256]{1,0:T(8,128)S(1)} collective-permute-done((f32[1024,256]{1,0:T(8,128)S(1)}, f32[1024,256]{1,0:T(8,128)S(1)}, u32[]{:S(2)}, u32[]{:S(2)}) %collective-permute-start.6) | collective-permute-done | bytes 1048608 | tf_op jit(solution)/shard_map/ppermute | solution.py:970
  161.8 24.7 %collective-permute-done.8.refs_0_ = f32[1024,256]{1,0:T(8,128)S(1)} collective-permute-done((f32[1024,256]{1,0:T(8,128)}, f32[1024,256]{1,0:T(8,128)S(1)}, u32[]{:S(2)}, u32[]{:S(2)}) %collective-permute-start.8) | collective-permute-done | bytes 1048608 | tf_op jit(solution)/shard_map/ppermute | solution.py:970
  197.1 16.1 %collective-permute-done.9.refs_7_.refs_2_ = f32[1024,256]{1,0:T(8,128)} collective-permute-done((f32[1024,256]{1,0:T(8,128)}, f32[1024,256]{1,0:T(8,128)}, u32[]{:S(2)}, u32[]{:S(2)}) %collective-permute-start.9) | collective-permute-done | bytes 1048608 | tf_op jit(solution)/shard_map/ppermute | solution.py:970
  231.1 18.5 %branch.2 = (f32[1024,2048]{1,0:T(8,128)}, bf16[1024,2048]{1,0:T(8,128)(2,1)}, f32[1024,16]{1,0:T(8,128)}, bf16[1024,2048]{1,0:T(8,128)(2,1)}) custom-call(f32[1024,256]{1,0:T(8,128)} %get-tuple-element.137.refs_0_, f32[1024,256]{1,0:T(8,128)} %copy-done.61, f32[1024,256]{1,0:T(8,128)} %get-tuple-element.138.refs_0_.refs_1_.refs_2_, f32[1024,256]{1,0:T(8,128)} %copy-done.64, ...), custom_call_target="tpu_custom_call" | custom-call | flops 8589934592 | bytes 33554432 | tf_op jit(solution)/shard_map/branch/pallas_call | solution.py:727
  263.6 31.1 %expert_acts.2 = (bf16[1024,2048]{1,0:T(8,128)(2,1)}, bf16[1024,2048]{1,0:T(8,128)(2,1)}, bf16[1024,2048]{1,0:T(8,128)(2,1)}, f32[1024,128]{1,0:T(8,128)}) custom-call(bf16[1024,2048]{1,0:T(8,128)(2,1)} %get-tuple-element.141.mixed_ref.refs_0_, f32[1024,2048]{1,0:T(8,128)} %low_grads.2.refs_0_.low_ref, f32[1024,16]{1,0:T(8,128)} %get-tuple-element.261.gates_ref, ...), custom_call_target="tpu_custom_call" | custom-call | flops 17179869184 | bytes 25165824 | tf_op jit(solution)/shard_map/expert_acts/pallas_call | solution.py:469
  296.8 27.7 %back_rows.2 = (f32[2,128,2176]{2,1,0:T(8,128)}, f32[2,128,2176]{2,1,0:T(8,128)}, f32[2,128,2176]{2,1,0:T(8,128)}, f32[2,128,2176]{2,1,0:T(8,128)}) custom-call(s32[8]{0:T(128)} %gather_fusion, bf16[1024,2048]{1,0:T(8,128)(2,1)} %get-tuple-element.144.refs_0_.refs_3_, bf16[1024,2048]{1,0:T(8,128)(2,1)} %get-tuple-element.145.refs_1_.refs_4_, ...), custom_call_target="tpu_custom_call" | custom-call | flops 17179869184 | bytes 25165824 | tf_op jit(solution)/shard_map/back_rows/pallas_call | solution.py:601
  326.5 18.7 %branch.3 = (f32[1024,2048]{1,0:T(8,128)}, bf16[1024,2048]{1,0:T(8,128)(2,1)}, f32[1024,16]{1,0:T(8,128)}, bf16[1024,2048]{1,0:T(8,128)(2,1)}) custom-call(f32[1024,256]{1,0:T(8,128)} %get-tuple-element.152.refs_0_, f32[1024,256]{1,0:T(8,128)} %collective-permute-done.12.refs_1_, f32[1024,256]{1,0:T(8,128)} %get-tuple-element.153.refs_2_, ...), custom_call_target="tpu_custom_call" | custom-call | flops 8589934592 | bytes 33554432 | tf_op jit(solution)/shard_map/branch/pallas_call | solution.py:727
  350.2 31.2 %expert_acts.3 = (bf16[1024,2048]{1,0:T(8,128)(2,1)}, bf16[1024,2048]{1,0:T(8,128)(2,1)}, bf16[1024,2048]{1,0:T(8,128)(2,1)}, f32[1024,128]{1,0:T(8,128)}) custom-call(bf16[1024,2048]{1,0:T(8,128)(2,1)} %get-tuple-element.154.mixed_ref.refs_1_, f32[1024,2048]{1,0:T(8,128)} %low_grads.3.refs_2_.low_ref, f32[1024,16]{1,0:T(8,128)} %get-tuple-element.259.gates_ref, ...), custom_call_target="tpu_custom_call" | custom-call | flops 1024 | bytes 1024 | tf_op jit(solution)/shard_map/expert_acts/pallas_call | solution.py:469
  388.4 27.3 %back_rows.3 = (f32[2,128,2176]{2,1,0:T(8,128)}, f32[2,128,2176]{2,1,0:T(8,128)}, f32[2,128,2176]{2,1,0:T(8,128)}, f32[2,128,2176]{2,1,0:T(8,128)}) custom-call(s32[8]{0:T(128)} %gather_fusion, bf16[1024,2048]{1,0:T(8,128)(2,1)} %get-tuple-element.159.refs_0_.refs_5_, bf16[1024,2048]{1,0:T(8,128)(2,1)} %get-tuple-element.160.refs_1_.refs_6_, ...), custom_call_target="tpu_custom_call" | custom-call | flops 17179869184 | bytes 25165824 | tf_op jit(solution)/shard_map/back_rows/pallas_call | solution.py:601
  415.7 19.8 %collective-permute-done.18.refs_1_ = f32[2,128,2176]{2,1,0:T(8,128)S(1)} collective-permute-done((f32[2,128,2176]{2,1,0:T(8,128)}, f32[2,128,2176]{2,1,0:T(8,128)S(1)}, u32[]{:S(2)}, u32[]{:S(2)}) %collective-permute-start.18) | collective-permute-done | bytes 2228256 | tf_op jit(solution)/shard_map/ppermute | solution.py:970
  452.6 21.1 %back_columns.4 = (f32[2,1024,256]{2,1,0:T(8,128)}, f32[2,1024,256]{2,1,0:T(8,128)}, f32[2,1024,256]{2,1,0:T(8,128)}, f32[2,1024,256]{2,1,0:T(8,128)}) custom-call(s32[8]{0:T(128)} %gather_fusion, s32[1]{0:T(128)} %constant.22.clone.1.rank_ref, bf16[1024,2048]{1,0:T(8,128)(2,1)} %get-tuple-element.143.refs_1_.refs_0_.refs_7_, ...), custom_call_target="tpu_custom_call" | custom-call | flops 8589934592 | bytes 16777216 | tf_op jit(solution)/shard_map/back_columns/pallas_call | solution.py:531
  473.8 23.7 %collective-permute-done.21.refs_4_ = f32[1,128,2176]{2,1,0:T(8,128)S(1)} collective-permute-done((f32[1,128,2176]{2,1,0:T(8,128)S(1)}, f32[1,128,2176]{2,1,0:T(8,128)S(1)}, u32[]{:S(2)}, u32[]{:S(2)}) %collective-permute-start.21) | collective-permute-done | bytes 1114144 | tf_op jit(solution)/shard_map/ppermute | solution.py:970
  508.5 31.0 %expert_grads.2.refs_3_ = f32[16,2048,128]{2,1,0:T(8,128)} custom-call(bf16[2048,2048]{1,0:T(8,128)(2,1)} %refs_1_.4, bf16[2048,2048]{1,0:T(8,128)(2,1)} %refs_1_.4, f32[2,128,2176]{2,1,0:T(8,128)} %get-tuple-element.171.refs_2_, f32[256,16]{1,0:T(8,128)} %pad_maximum_fusion.11.refs_3_, f32[256,2048]{1,0:T(8,128)} %get-tuple-element.267.refs_4_, ...), custom_call_target="tpu_custom_call" | custom-call | flops 17179869184 | bytes 25165824 | tf_op jit(solution)/shard_map/expert_grads/pallas_call | solution.py:688
  559.1 50.8 %expert_grads.3 = (f32[16,2048,128]{2,1,0:T(8,128)}, f32[16,2048,128]{2,1,0:T(8,128)}) custom-call(bf16[1024,2048]{1,0:T(8,128)(2,1)} %get-tuple-element.141.mixed_ref.refs_0_, bf16[1024,2048]{1,0:T(8,128)(2,1)} %get-tuple-element.154.mixed_ref.refs_1_, f32[1,128,2176]{2,1,0:T(8,128)} %get-tuple-element.177.refs_2_, ...), custom_call_target="tpu_custom_call" | custom-call | flops 34359738368 | bytes 50331648 | tf_op jit(solution)/shard_map/expert_grads/pallas_call | solution.py:688
  633.0 21.2 %back_columns.5 = (f32[2,1024,256]{2,1,0:T(8,128)}, f32[2,1024,256]{2,1,0:T(8,128)}, f32[2,1024,256]{2,1,0:T(8,128)}, f32[2,1024,256]{2,1,0:T(8,128)}) custom-call(s32[8]{0:T(128)} %gather_fusion, s32[1]{0:T(128)} %constant.22.clone.1.rank_ref, bf16[1024,2048]{1,0:T(8,128)(2,1)} %get-tuple-element.156.refs_3_.refs_8_.refs_0_, ...), custom_call_target="tpu_custom_call" | custom-call | flops 1024 | bytes 1024 | tf_op jit(solution)/shard_map/back_columns/pallas_call | solution.py:531
  654.2 15.6 %collective-permute-done.26.refs_1_ = f32[2,1024,256]{2,1,0:T(8,128)S(1)} collective-permute-done((f32[2,1024,256]{2,1,0:T(8,128)}, f32[2,1024,256]{2,1,0:T(8,128)S(1)}, u32[]{:S(2)}, u32[]{:S(2)}) %collective-permute-start.26) | collective-permute-done | bytes 2097184 | tf_op jit(solution)/shard_map/ppermute | solution.py:970
  694.8 18.6 %outer.1 = (f32[4,512,256]{2,1,0:T(8,128)}, f32[4,512,256]{2,1,0:T(8,128)}, f32[4,512,256]{2,1,0:T(8,128)}, f32[4,512,256]{2,1,0:T(8,128)}, f32[4,512,256]{2,1,0...) custom-call(s32[4]{0:T(128)} %iota_xor_fusion.table_ref, ...), custom_call_target="tpu_custom_call" | custom-call | flops 2147483648 | bytes 16777216 | tf_op jit(solution)/shard_map/outer/pallas_call | solution.py:826
  734.1 24.8 %attend_back.1 = (f32[2048,256]{1,0:T(8,128)}, f32[2048,256]{1,0:T(8,128)}, bf16[2048,256]{1,0:T(8,128)(2,1)}, f32[8,2048]{1,0:T(8,128)}, f32[16,256]{1,0:T(8,128)}) custom-call(s32[8]{0:T(128)} %copy-done, bf16[2048,256]{1,0:T(8,128)(2,1)} %get-tuple-element.291.q_ref, bf16[2048,256]{1,0:T(8,128)(2,1)} %get-tuple-element.292.k_ref, ...), custom_call_target="tpu_custom_call" | custom-call | flops 5368709120 | bytes 15728640 | tf_op jit(solution)/shard_map/attend_back/pallas_call | solution.py:290
  759.0 24.2 %collective-permute-done.28.refs_4_ = f32[1,1024,256]{2,1,0:T(8,128)S(1)} collective-permute-done((f32[1,1024,256]{2,1,0:T(8,128)}, f32[1,1024,256]{2,1,0:T(8,128)S(1)}, u32[]{:S(2)}, u32[]{:S(2)}) %collective-permute-start.28) | collective-permute-done | bytes 1048608 | tf_op jit(solution)/shard_map/ppermute | solution.py:970
  824.7 15.1 %back_columns.7 = (f32[2,1024,256]{2,1,0:T(8,128)}, f32[2,1024,256]{2,1,0:T(8,128)}, f32[2,1024,256]{2,1,0:T(8,128)}, f32[2,1024,256]{2,1,0:T(8,128)}) custom-call(s32[8]{0:T(128)} %gather_fusion, s32[1]{0:T(128)} %bitcast.18.rank_ref, bf16[1024,256]{1,0:T(8,128)(2,1)} %get-tuple-element.276.refs_0_, bf16[1024,256]{1,0:T(8,128)(2,1)} %get-tuple-element.274.refs_1_, ...), custom_call_target="tpu_custom_call" | custom-call | flops 3221225472 | bytes 33554432 | tf_op jit(solution)/shard_map/back_columns/pallas_call | solution.py:531
  876.0 26.7 %collective-permute-done.42.refs_4_ = f32[1,1024,256]{2,1,0:T(8,128)S(1)} collective-permute-done((f32[1,1024,256]{2,1,0:T(8,128)}, f32[1,1024,256]{2,1,0:T(8,128)S(1)}, u32[]{:S(2)}, u32[]{:S(2)}) %collective-permute-start.42) | collective-permute-done | bytes 1048608 | tf_op jit(solution)/shard_map/ppermute | solution.py:970
  916.3 39.8 %collective-permute-done.44.refs_1_ = f32[2,1024,256]{2,1,0:T(8,128)S(1)} collective-permute-done((f32[2,1024,256]{2,1,0:T(8,128)}, f32[2,1024,256]{2,1,0:T(8,128)S(1)}, u32[]{:S(2)}, u32[]{:S(2)}) %collective-permute-start.44) | collective-permute-done | bytes 2097184 | tf_op jit(solution)/shard_map/ppermute | solution.py:970
  970.0 14.4 %collective-permute-done.50 = f32[4,512,256]{2,1,0:T(8,128)} collective-permute-done((f32[4,512,256]{2,1,0:T(8,128)}, f32[4,512,256]{2,1,0:T(8,128)}, u32[]{:S(2)}, u32[]{:S(2)}) %collective-permute-start.50) | collective-permute-done | bytes 2097184 | tf_op jit(solution)/shard_map/ppermute | solution.py:970
  993.4 19.5 %collective-permute-done.46.refs_4_ = f32[1,1024,256]{2,1,0:T(8,128)S(1)} collective-permute-done((f32[1,1024,256]{2,1,0:T(8,128)}, f32[1,1024,256]{2,1,0:T(8,128)S(1)}, u32[]{:S(2)}, u32[]{:S(2)}) %collective-permute-start.46) | collective-permute-done | bytes 1048608 | tf_op jit(solution)/shard_map/ppermute | solution.py:970
  1018.8 18.6 %collective-permute-done.61 = f32[18,2048]{1,0:T(8,128)S(1)} collective-permute-done((f32[18,2048]{1,0:T(8,128)S(1)}, f32[18,2048]{1,0:T(8,128)S(1)}, u32[]{:S(2)}, u32[]{:S(2)}) %collective-permute-start.61) | collective-permute-done | bytes 147488 | tf_op jit(solution)/shard_map/ppermute | solution.py:970
  1050.2 19.7 %collective-permute-done.58 = f32[512,768]{1,0:T(8,128)} collective-permute-done((f32[512,768]{1,0:T(8,128)}, f32[512,768]{1,0:T(8,128)}, u32[]{:S(2)}, u32[]{:S(2)}) %collective-permute-start.58) | collective-permute-done | bytes 1572896 | tf_op jit(solution)/shard_map/ppermute | solution.py:970
  1098.9 35.2 %collective-permute-done.59 = f32[1,1024,256]{2,1,0:T(8,128)S(1)} collective-permute-done((f32[1,1024,256]{2,1,0:T(8,128)}, f32[1,1024,256]{2,1,0:T(8,128)S(1)}, u32[]{:S(2)}, u32[]{:S(2)}) %collective-permute-start.59) | collective-permute-done | bytes 1048608 | tf_op jit(solution)/shard_map/ppermute | solution.py:970
  1151.0 18.8 %collective-permute-done.64 = f32[1,12800]{1,0:T(1,128)S(1)} collective-permute-done((f32[1,12800]{1,0:T(1,128)S(1)}, f32[1,12800]{1,0:T(1,128)S(1)}, u32[]{:S(2)}, u32[]{:S(2)}) %collective-permute-start.64) | collective-permute-done | bytes 51232 | tf_op jit(solution)/shard_map/ppermute | solution.py:970
  1178.9 18.3 %collective-permute-done.67 = f32[1,512,256]{2,1,0:T(8,128)} collective-permute-done((f32[1,512,256]{2,1,0:T(8,128)}, f32[1,512,256]{2,1,0:T(8,128)}, u32[]{:S(2)}, u32[]{:S(2)}) %collective-permute-start.67) | collective-permute-done | bytes 524320 | tf_op jit(solution)/shard_map/ppermute | solution.py:970
  (464 shorter events, 444.5 us)
Async XLA Ops:
  7.2 101.4 %all-gather.5.cloned.1.call-start = ((), (), s32[]{:S(2)}) async-start(), calls=%async_computation.6 | async-start | bytes 4718592 | tf_op jit(solution)/shard_map/all_gather | solution.py:1161
  9.0 210.2 %all-gather.7.cloned.1.call-start = ((), (), s32[]{:S(2)}) async-start(), calls=%async_computation.7 | async-start | bytes 20971520 | tf_op jit(solution)/shard_map/all_gather | solution.py:1202
  57.4 50.2 %collective-permute-start.3 = (f32[1024,256]{1,0:T(8,128)}, f32[1024,256]{1,0:T(8,128)S(1)}, u32[]{:S(2)}, u32[]{:S(2)}) collective-permute-start(f32[1024,256]{1,0:T(8,128)} %get-tuple-element.135.refs_0_.refs_1_), channel_id=1, source_target_pairs={{0,2},{1,3},{2,0},{3,1},{4,6},{5,7},{6,4},{7,5},{8,10},{9,11},{10,... | collective-permute-start | bytes 3145736 | tf_op jit(solution)/shard_map/ppermute | solution.py:970
  108.6 1090.5 %reduce-scatter.8.cloned.1.call-start = ((), (), s32[]{:S(2)}) async-start(), calls=%async_computation.5 | async-start | bytes 20971520 | tf_op jit(solution)/shard_map/reduce_scatter | solution.py:1385
  109.8 49.5 %collective-permute-start.5 = (f32[1024,256]{1,0:T(8,128)S(1)}, f32[1024,256]{1,0:T(8,128)S(1)}, u32[]{:S(2)}, u32[]{:S(2)}) collective-permute-start(f32[1024,256]{1,0:T(8,128)S(1)} %copy-done.46), channel_id=1, source_target_pairs={{0,1},{1,0},{2,3},{3,2},{4,5},{5,4},{6,7},{7,6},{8,9},{9,8},{10,11... | collective-permute-start | bytes 3145736 | tf_op jit(solution)/shard_map/ppermute | solution.py:970
  111.3 47.9 %collective-permute-start.6 = (f32[1024,256]{1,0:T(8,128)S(1)}, f32[1024,256]{1,0:T(8,128)S(1)}, u32[]{:S(2)}, u32[]{:S(2)}) collective-permute-start(f32[1024,256]{1,0:T(8,128)S(1)} %copy-done.62), channel_id=1, source_target_pairs={{0,4},{1,5},{2,6},{3,7},{4,0},{5,1},{6,2},{7,3},{8,12},{9,13},{10,... | collective-permute-start | bytes 3145736 | tf_op jit(solution)/shard_map/ppermute | solution.py:970
  217.2 108.3 %collective-permute-start.12 = (f32[1024,256]{1,0:T(8,128)S(1)}, f32[1024,256]{1,0:T(8,128)}, u32[]{:S(2)}, u32[]{:S(2)}) collective-permute-start(f32[1024,256]{1,0:T(8,128)S(1)} %copy-done.8), channel_id=1, source_target_pairs={{0,1},{1,0},{2,3},{3,2},{4,5},{5,4},{6,7},{7,6},{8,9},{9,8},{10,11... | collective-permute-start | bytes 3145736 | tf_op jit(solution)/shard_map/ppermute | solution.py:970
  218.7 106.8 %collective-permute-start.13 = (f32[1024,256]{1,0:T(8,128)}, f32[1024,256]{1,0:T(8,128)}, u32[]{:S(2)}, u32[]{:S(2)}) collective-permute-start(f32[1024,256]{1,0:T(8,128)} %get-tuple-element.153.refs_2_), channel_id=1, source_target_pairs={{0,1},{1,0},{2,3},{3,2},{4,5},{5,4},{6,7},{7,6},{8,9},{9,8},{10,11... | collective-permute-start | bytes 3145736 | tf_op jit(solution)/shard_map/ppermute | solution.py:970
  260.2 65.3 %collective-permute-start.15 = (f32[1024,256]{1,0:T(8,128)}, f32[1024,256]{1,0:T(8,128)}, u32[]{:S(2)}, u32[]{:S(2)}) collective-permute-start(f32[1024,256]{1,0:T(8,128)} %tie.13.refs_4_), channel_id=1, source_target_pairs={{0,1},{1,0},{2,3},{3,2},{4,5},{5,4},{6,7},{7,6},{8,9},{9,8},{10,11... | collective-permute-start | bytes 3145736 | tf_op jit(solution)/shard_map/ppermute | solution.py:970
  324.5 57.0 %collective-permute-start.10 = (f32[2,128,2176]{2,1,0:T(8,128)}, f32[2,128,2176]{2,1,0:T(8,128)}, u32[]{:S(2)}, u32[]{:S(2)}) collective-permute-start(f32[2,128,2176]{2,1,0:T(8,128)} %get-tuple-element.149), channel_id=1, source_target_pairs={{0,1},{1,0},{2,3},{3,2},{4,5},{5,4},{6,7},{7,6},{8,9},{9,8},{10,11... | collective-permute-start | bytes 6684680 | tf_op jit(solution)/shard_map/ppermute | solution.py:970
  385.8 49.7 %collective-permute-start.18 = (f32[2,128,2176]{2,1,0:T(8,128)}, f32[2,128,2176]{2,1,0:T(8,128)S(1)}, u32[]{:S(2)}, u32[]{:S(2)}) collective-permute-start(f32[2,128,2176]{2,1,0:T(8,128)} %get-tuple-element.157), channel_id=1, source_target_pairs={{0,1},{1,0},{2,3},{3,2},{4,5},{5,4},{6,7},{7,6},{8,9},{9,8},{10,11... | collective-permute-start | bytes 6684680 | tf_op jit(solution)/shard_map/ppermute | solution.py:970
  386.8 49.7 %collective-permute-start.19 = (f32[2,128,2176]{2,1,0:T(8,128)}, f32[2,128,2176]{2,1,0:T(8,128)S(1)}, u32[]{:S(2)}, u32[]{:S(2)}) collective-permute-start(f32[2,128,2176]{2,1,0:T(8,128)} %get-tuple-element.158.refs_5_), channel_id=1, source_target_pairs={{0,2},{1,3},{2,0},{3,1},{4,6},{5,7},{6,4},{7,5},{8,10},{9,11},{10,... | collective-permute-start | bytes 6684680 | tf_op jit(solution)/shard_map/ppermute | solution.py:970
  441.9 55.6 %collective-permute-start.20 = (f32[2,128,2176]{2,1,0:T(8,128)}, f32[2,128,2176]{2,1,0:T(8,128)}, u32[]{:S(2)}, u32[]{:S(2)}) collective-permute-start(f32[2,128,2176]{2,1,0:T(8,128)} %get-tuple-element.168), channel_id=1, source_target_pairs={{0,1},{1,0},{2,3},{3,2},{4,5},{5,4},{6,7},{7,6},{8,9},{9,8},{10,11... | collective-permute-start | bytes 6684680 | tf_op jit(solution)/shard_map/ppermute | solution.py:970
  447.9 49.6 %collective-permute-start.21 = (f32[1,128,2176]{2,1,0:T(8,128)S(1)}, f32[1,128,2176]{2,1,0:T(8,128)S(1)}, u32[]{:S(2)}, u32[]{:S(2)}) collective-permute-start(f32[1,128,2176]{2,1,0:T(8,128)S(1)} %copy-done.79), channel_id=1, source_target_pairs={{0,4},{1,5},{2,6},{3,7},{4,0},{5,1},{6,2},{7,3},{8,12},{9,13},{10,... | collective-permute-start | bytes 3342344 | tf_op jit(solution)/shard_map/ppermute | solution.py:970
  502.7 50.5 %collective-permute-start.22 = (f32[2,128,2176]{2,1,0:T(8,128)}, f32[2,128,2176]{2,1,0:T(8,128)S(1)}, u32[]{:S(2)}, u32[]{:S(2)}) collective-permute-start(f32[2,128,2176]{2,1,0:T(8,128)} %get-tuple-element.170), channel_id=1, source_target_pairs={{0,1},{1,0},{2,3},{3,2},{4,5},{5,4},{6,7},{7,6},{8,9},{9,8},{10,11... | collective-permute-start | bytes 6684680 | tf_op jit(solution)/shard_map/ppermute | solution.py:970
  503.5 49.9 %collective-permute-start.23 = (f32[2,128,2176]{2,1,0:T(8,128)}, f32[2,128,2176]{2,1,0:T(8,128)}, u32[]{:S(2)}, u32[]{:S(2)}) collective-permute-start(f32[2,128,2176]{2,1,0:T(8,128)} %get-tuple-element.171.refs_2_), channel_id=1, source_target_pairs={{0,2},{1,3},{2,0},{3,1},{4,6},{5,7},{6,4},{7,5},{8,10},{9,11},{10,... | collective-permute-start | bytes 6684680 | tf_op jit(solution)/shard_map/ppermute | solution.py:970
  558.4 640.7 %reduce-scatter.4.cloned.1.call-start = ((), (), s32[]{:S(2)}) async-start(), calls=%async_computation.3 | async-start | bytes 20971520 | tf_op jit(solution)/shard_map/reduce_scatter | solution.py:1385
  558.4 51.5 %collective-permute-start.25 = (f32[1,128,2176]{2,1,0:T(8,128)}, f32[1,128,2176]{2,1,0:T(8,128)S(1)}, u32[]{:S(2)}, u32[]{:S(2)}) collective-permute-start(f32[1,128,2176]{2,1,0:T(8,128)} %get-tuple-element.177.refs_2_), channel_id=1, source_target_pairs={{0,4},{1,5},{2,6},{3,7},{4,0},{5,1},{6,2},{7,3},{8,12},{9,13},{10,... | collective-permute-start | bytes 3342344 | tf_op jit(solution)/shard_map/ppermute | solution.py:970
  558.5 51.4 %collective-permute-start.24 = (f32[2,1024,256]{2,1,0:T(8,128)}, f32[2,1024,256]{2,1,0:T(8,128)S(1)}, u32[]{:S(2)}, u32[]{:S(2)}) collective-permute-start(f32[2,1024,256]{2,1,0:T(8,128)} %get-tuple-element.176), channel_id=1, source_target_pairs={{0,1},{1,0},{2,3},{3,2},{4,5},{5,4},{6,7},{7,6},{8,9},{9,8},{10,11... | collective-permute-start | bytes 6291464 | tf_op jit(solution)/shard_map/ppermute | solution.py:970
  615.8 583.2 %reduce-scatter.6.cloned.1.call-start = ((), (), s32[]{:S(2)}) async-start(), calls=%async_computation.4 | async-start | bytes 20971520 | tf_op jit(solution)/shard_map/reduce_scatter | solution.py:1385
  713.3 69.9 %collective-permute-start.29 = (f32[2,1024,256]{2,1,0:T(8,128)S(1)}, f32[2,1024,256]{2,1,0:T(8,128)S(1)}, u32[]{:S(2)}, u32[]{:S(2)}) collective-permute-start(f32[2,1024,256]{2,1,0:T(8,128)S(1)} %copy-done.54), channel_id=1, source_target_pairs={{0,1},{1,0},{2,3},{3,2},{4,5},{5,4},{6,7},{7,6},{8,9},{9,8},{10,11... | collective-permute-start | bytes 6291464 | tf_op jit(solution)/shard_map/ppermute | solution.py:970
  723.7 59.5 %collective-permute-start.28 = (f32[1,1024,256]{2,1,0:T(8,128)}, f32[1,1024,256]{2,1,0:T(8,128)S(1)}, u32[]{:S(2)}, u32[]{:S(2)}) collective-permute-start(f32[1,1024,256]{2,1,0:T(8,128)} %get-tuple-element.184), channel_id=1, source_target_pairs={{0,4},{1,5},{2,6},{3,7},{4,0},{5,1},{6,2},{7,3},{8,12},{9,13},{10,... | collective-permute-start | bytes 3145736 | tf_op jit(solution)/shard_map/ppermute | solution.py:970
  862.4 48.2 %collective-permute-start.49 = (f32[4,512,256]{2,1,0:T(8,128)}, f32[4,512,256]{2,1,0:T(8,128)}, u32[]{:S(2)}, u32[]{:S(2)}) collective-permute-start(f32[4,512,256]{2,1,0:T(8,128)} %get-tuple-element.233), channel_id=1, source_target_pairs={{0,8},{8,0},{16,24},{24,16},{1,9},{9,1},{17,25},{25,17},{2,10},{10... | collective-permute-start | bytes 6291464 | tf_op jit(solution)/shard_map/ppermute | solution.py:970
  910.1 53.5 %collective-permute-start.48 = (f32[4,512,256]{2,1,0:T(8,128)}, f32[4,512,256]{2,1,0:T(8,128)}, u32[]{:S(2)}, u32[]{:S(2)}) collective-permute-start(f32[4,512,256]{2,1,0:T(8,128)} %get-tuple-element.231), channel_id=1, source_target_pairs={{0,8},{8,0},{16,24},{24,16},{1,9},{9,1},{17,25},{25,17},{2,10},{10... | collective-permute-start | bytes 6291464 | tf_op jit(solution)/shard_map/ppermute | solution.py:970
  910.1 54.0 %collective-permute-start.54 = (f32[4,512,256]{2,1,0:T(8,128)}, f32[4,512,256]{2,1,0:T(8,128)}, u32[]{:S(2)}, u32[]{:S(2)}) collective-permute-start(f32[4,512,256]{2,1,0:T(8,128)} %get-tuple-element.238), channel_id=1, source_target_pairs={{0,8},{8,0},{16,24},{24,16},{1,9},{9,1},{17,25},{25,17},{2,10},{10... | collective-permute-start | bytes 6291464 | tf_op jit(solution)/shard_map/ppermute | solution.py:970
  914.6 69.8 %collective-permute-start.50 = (f32[4,512,256]{2,1,0:T(8,128)}, f32[4,512,256]{2,1,0:T(8,128)}, u32[]{:S(2)}, u32[]{:S(2)}) collective-permute-start(f32[4,512,256]{2,1,0:T(8,128)} %add.309), channel_id=1, source_target_pairs={{0,16},{8,24},{16,0},{24,8},{1,17},{9,25},{17,1},{25,9},{2,18},{10... | collective-permute-start | bytes 6291464 | tf_op jit(solution)/shard_map/ppermute | solution.py:970
  962.7 50.1 %collective-permute-start.47 = (f32[2,1024,256]{2,1,0:T(8,128)}, f32[2,1024,256]{2,1,0:T(8,128)S(1)}, u32[]{:S(2)}, u32[]{:S(2)}) collective-permute-start(f32[2,1024,256]{2,1,0:T(8,128)} %get-tuple-element.228), channel_id=1, source_target_pairs={{0,1},{1,0},{2,3},{3,2},{4,5},{5,4},{6,7},{7,6},{8,9},{9,8},{10,11... | collective-permute-start | bytes 6291464 | tf_op jit(solution)/shard_map/ppermute | solution.py:970
  963.6 75.2 %collective-permute-start.53 = (f32[4,512,256]{2,1,0:T(8,128)}, f32[4,512,256]{2,1,0:T(8,128)}, u32[]{:S(2)}, u32[]{:S(2)}) collective-permute-start(f32[4,512,256]{2,1,0:T(8,128)} %get-tuple-element.236), channel_id=1, source_target_pairs={{0,8},{8,0},{16,24},{24,16},{1,9},{9,1},{17,25},{25,17},{2,10},{10... | collective-permute-start | bytes 6291464 | tf_op jit(solution)/shard_map/ppermute | solution.py:970
  964.1 48.7 %collective-permute-start.46 = (f32[1,1024,256]{2,1,0:T(8,128)}, f32[1,1024,256]{2,1,0:T(8,128)S(1)}, u32[]{:S(2)}, u32[]{:S(2)}) collective-permute-start(f32[1,1024,256]{2,1,0:T(8,128)} %get-tuple-element.226), channel_id=1, source_target_pairs={{0,4},{1,5},{2,6},{3,7},{4,0},{5,1},{6,2},{7,3},{8,12},{9,13},{10,... | collective-permute-start | bytes 3145736 | tf_op jit(solution)/shard_map/ppermute | solution.py:970
  984.4 61.1 %collective-permute-start.55 = (f32[4,512,256]{2,1,0:T(8,128)}, f32[4,512,256]{2,1,0:T(8,128)}, u32[]{:S(2)}, u32[]{:S(2)}) collective-permute-start(f32[4,512,256]{2,1,0:T(8,128)} %add.314), channel_id=1, source_target_pairs={{0,16},{8,24},{16,0},{24,8},{1,17},{9,25},{17,1},{25,9},{2,18},{10... | collective-permute-start | bytes 6291464 | tf_op jit(solution)/shard_map/ppermute | solution.py:970
  984.7 52.6 %collective-permute-start.61 = (f32[18,2048]{1,0:T(8,128)S(1)}, f32[18,2048]{1,0:T(8,128)S(1)}, u32[]{:S(2)}, u32[]{:S(2)}) collective-permute-start(f32[18,2048]{1,0:T(8,128)S(1)} %fusion.37), channel_id=1, source_target_pairs={{0,16},{8,24},{16,0},{24,8},{1,17},{9,25},{17,1},{25,9},{2,18},{10... | collective-permute-start | bytes 442376 | tf_op jit(solution)/shard_map/ppermute | solution.py:970
  1012.9 57.1 %collective-permute-start.58 = (f32[512,768]{1,0:T(8,128)}, f32[512,768]{1,0:T(8,128)}, u32[]{:S(2)}, u32[]{:S(2)}) collective-permute-start(f32[512,768]{1,0:T(8,128)} %add.317), channel_id=1, source_target_pairs={{0,16},{8,24},{16,0},{24,8},{1,17},{9,25},{17,1},{25,9},{2,18},{10... | collective-permute-start | bytes 4718600 | tf_op jit(solution)/shard_map/ppermute | solution.py:970
  (126 other events, 1635.4 us)
Sparse Core Ops, SparseCore 0:
  10.7 97.4 all-gather.4
  109.7 105.9 all-gather.6
  558.5 123.6 reduce-scatter.7
  685.4 126.0 reduce-scatter.3
  814.6 147.8 reduce-scatter.5

commit v4 on v3

--- a/solution.py
+++ b/solution.py
@@ -705,8 +705,8 @@
 
 def branch_kernel(count, after, *refs):
     pieces = refs[:count]
-    w_ref, x_ref, gain_ref, router_ref = refs[count : count + 4]
-    mid_ref, mixed_ref, logit_ref, all_ref = refs[count + 4 + after :]
+    w_ref, x_ref, gain_ref, router_ref, kept_ref = refs[count : count + 5]
+    mid_ref, mixed_ref, probs_ref, gates_ref, all_ref = refs[count + 5 + after :]
     share = pieces[0].shape[1]
     for index, piece in enumerate(pieces):
         all_ref[:, index * share : (index + 1) * share] = piece[...].astype(BF)
@@ -715,10 +715,14 @@
     mid_hat = middle * norm_scale(middle)
     mixed = (mid_hat * gain_ref[...].astype(F32)).astype(BF)
     mixed_ref[...] = mixed
-    logit_ref[...] = dot(mixed, router_ref[...])
-
-
-def branch(pieces, w_out, hidden, chunk, gain, w_router, after=()):
+    logits = dot(mixed, router_ref[...])
+    expo = jnp.exp(logits - jnp.max(logits, axis=1, keepdims=True))
+    probs = expo / jnp.sum(expo, axis=1, keepdims=True)
+    probs_ref[...] = probs
+    gates_ref[...] = probs * kept_ref[...]
+
+
+def branch(pieces, w_out, hidden, chunk, gain, w_router, kept, after=()):
     tokens, share = pieces[0].shape
     width, full = w_out.shape
     rows = min(256, tokens)
@@ -733,11 +737,13 @@
             pl.BlockSpec((rows, width), lambda i: (chunk * steps + i, 0)),
             whole_spec((1, width)),
             whole_spec(w_router.shape),
+            pl.BlockSpec((rows, experts), lambda i: (chunk * steps + i, 0)),
         ]
         + [ANY] * len(after),
         out_specs=[
             pl.BlockSpec((rows, width), lambda i: (i, 0)),
             pl.BlockSpec((rows, width), lambda i: (i, 0)),
+            pl.BlockSpec((rows, experts), lambda i: (i, 0)),
             pl.BlockSpec((rows, experts), lambda i: (i, 0)),
             pl.BlockSpec((rows, full), lambda i: (i, 0)),
         ],
@@ -745,12 +751,13 @@
             jax.ShapeDtypeStruct((tokens, width), F32),
             jax.ShapeDtypeStruct((tokens, width), BF),
             jax.ShapeDtypeStruct((tokens, experts), F32),
+            jax.ShapeDtypeStruct((tokens, experts), F32),
             jax.ShapeDtypeStruct((tokens, full), BF),
         ],
         compiler_params=params(58),
         cost_estimate=cost(2 * tokens * width * full, 16 * tokens * width),
         name="branch",
-    )(*pieces, w_out, hidden, gain.reshape(1, -1), w_router, *after)
+    )(*pieces, w_out, hidden, gain.reshape(1, -1), w_router, kept, *after)
 
 
 def cast_kernel(table_ref, in_ref, out_ref):
@@ -804,36 +811,143 @@
     )(low, w_out, *after)
 
 
-def outer_kernel(after, table_ref, columns_ref, left_ref, right_ref, *outs):
+def mid_back_kernel(counts, rank_ref, *refs):
+    chunks = len(counts)
+    terms, refs = refs[: sum(counts)], refs[sum(counts) :]
+    by_chunk = [refs[c * 6 : (c + 1) * 6] for c in range(chunks)]
+    gain_ref, in_ref, router_ref = refs[6 * chunks : 6 * chunks + 3]
+    low_ref, direct_ref, sums_ref, vectors_ref = refs[6 * chunks + 3 :]
+    experts = router_ref.shape[1]
+    own, width = by_chunk[0][0].shape
+    gain, gain_in = gain_ref[...].astype(F32), in_ref[...].astype(F32)
+    gain_mid, direct_gain, router = 0.0, 0.0, 0.0
+    used = 0
+    for chunk in range(chunks):
+        mid_ref, dy_ref, x_ref, probs_ref, kept_ref, mixed_ref = by_chunk[chunk]
+        total = terms[used][0]
+        for term in terms[used + 1 : used + counts[chunk]]:
+            total = total + term[0]
+        used += counts[chunk]
+        probs = probs_ref[...]
+        prob_grad = total[:, width : width + experts] * kept_ref[...]
+        logit_grad = (
+            probs * (prob_grad - jnp.sum(probs * prob_grad, axis=1, keepdims=True))
+        ).astype(BF)
+        mixed_grad = total[:, :width] + dot(logit_grad, router_ref[...], 1, 1)
+        middle = mid_ref[...]
+        scale = norm_scale(middle)
+        hat = middle * scale
+        gain_mid = gain_mid + jnp.sum(mixed_grad * hat, axis=0, keepdims=True)
+        scaled = mixed_grad * gain
+        grad = dy_ref[...].astype(F32) + scale * (
+            scaled - hat * jnp.mean(scaled * hat, axis=1, keepdims=True)
+        )
+        here = slice(chunk * own, (chunk + 1) * own)
+        low_ref[here, :] = grad.astype(BF)
+        hidden = x_ref[...].astype(F32)
+        in_scale = norm_scale(hidden)
+        in_hat = hidden * in_scale
+        direct = grad / (in_scale * gain_in)
+        direct_ref[here, :] = direct
+        sums_ref[here, :] = jnp.broadcast_to(
+            jnp.sum(grad * in_hat, axis=1, keepdims=True) / in_scale, (own, LANES)
+        )
+        direct_gain = direct_gain + jnp.sum(direct * in_hat, axis=0, keepdims=True)
+        router = router + dot(logit_grad, mixed_ref[...], 0, 0)
+    vectors_ref[:experts, :] = router
+    row = lax.broadcasted_iota(jnp.int32, (8, width), 0)
+    vectors_ref[experts:, :] = jnp.where(
+        row == 0, gain_mid, jnp.where(row == 1, direct_gain, 0.0)
+    )
+
+
+def mid_back(rank, shares, middle, dy, hidden, probs, kept, mixed, gain, gain_in, w_router):
+    chunks = len(shares)
+    own, width = shares[0][0][0].shape[1], middle[0].shape[1]
+    experts = w_router.shape[1]
+    parts = middle[0].shape[0] // own
+    specs, arrays = [], []
+    for chunk in shares:
+        for array, block in chunk:
+            specs.append(
+                pl.BlockSpec((1,) + array.shape[1:], lambda i, _, block=block: (block, 0, 0))
+            )
+            arrays.append(array)
+    for c in range(chunks):
+        mine = pl.BlockSpec((own, width), lambda i, rank: (rank[0], 0))
+        far = pl.BlockSpec((own, width), lambda i, rank, c=c: (c * parts + rank[0], 0))
+        few = pl.BlockSpec((own, experts), lambda i, rank: (rank[0], 0))
+        some = pl.BlockSpec((own, experts), lambda i, rank, c=c: (c * parts + rank[0], 0))
+        specs += [mine, far, far, few, some, mine]
+        arrays += [middle[c], dy, hidden, probs[c], kept, mixed[c]]
+    rows = chunks * own
+    return pl.pallas_call(
+        functools.partial(mid_back_kernel, tuple(len(chunk) for chunk in shares)),
+        grid_spec=pltpu.PrefetchScalarGridSpec(
+            num_scalar_prefetch=1,
+            grid=(1,),
+            in_specs=specs
+            + [whole_spec((1, width)), whole_spec((1, width)), whole_spec(w_router.shape)],
+            out_specs=[
+                whole_spec((rows, width)),
+                whole_spec((rows, width)),
+                whole_spec((rows, LANES)),
+                whole_spec((experts + 8, width)),
+            ],
+        ),
+        out_shape=[
+            jax.ShapeDtypeStruct((rows, width), BF),
+            jax.ShapeDtypeStruct((rows, width), F32),
+            jax.ShapeDtypeStruct((rows, LANES), F32),
+            jax.ShapeDtypeStruct((experts + 8, width), F32),
+        ],
+        compiler_params=params(58),
+        cost_estimate=cost(0, 0, True),
+        name="mid_back",
+    )(rank.reshape(1), *arrays, gain.reshape(1, -1), gain_in.reshape(1, -1), w_router)
+
+
+def outer_kernel(count, after, table_ref, columns_ref, rank_ref, left_ref, *refs):
+    rights, refs = refs[:count], refs[count + after :]
+    outs, held = refs[:-1], refs[-1]
+    own = rights[0].shape[0]
     number = pl.program_id(0) * 2 + pl.program_id(1)
-    for index, out_ref in enumerate(outs[after:]):
+
+    @pl.when((number == 0) & (pl.program_id(2) == 0))
+    def _():
+        for index, right in enumerate(rights):
+            held[index * own : (index + 1) * own, :] = right[...]
+
+    left = left_ref[...].T
+    for index, out_ref in enumerate(outs):
 
         @pl.when(number == index)
         def _(out_ref=out_ref):
             for part in range(out_ref.shape[0]):
                 wide = out_ref.shape[2]
                 place = columns_ref[(index % 2) * out_ref.shape[0] + part] * wide
-                right = right_ref[:, pl.ds(pl.multiple_of(place, LANES), wide)]
-                out_ref[part] = dot(left_ref[...], right)
-
-
-def outer(left, right, table, columns, after=()):
-    width, rows = left.shape
+                right = held[:, pl.ds(pl.multiple_of(place, LANES), wide)]
+                out_ref[part] = dot(left, right)
+
+
+def outer(left, rights, rank, table, columns, after=()):
+    rows, width = left.shape
+    count = len(rights)
+    own, full = rows // count, rights[0].shape[1]
     parts, pieces = table.shape[0], columns.shape[0]
-    high, wide = width // parts, right.shape[1] // pieces
-    shape = (pieces // 2, high, wide)
-    steps = 2
+    high, wide = width // parts, full // pieces
+    steps = 2 if high % (2 * LANES) == 0 else 1
     return pl.pallas_call(
-        functools.partial(outer_kernel, len(after)),
+        functools.partial(outer_kernel, count, len(after)),
         grid_spec=pltpu.PrefetchScalarGridSpec(
-            num_scalar_prefetch=2,
+            num_scalar_prefetch=3,
             grid=(parts, 2, steps),
             in_specs=[
                 pl.BlockSpec(
-                    (high // steps, rows), lambda k, m, i, table, columns: (table[k] * steps + i, 0)
+                    (rows, high // steps), lambda k, m, i, table, *_: (0, table[k] * steps + i)
                 ),
-                whole_spec(right.shape),
             ]
+            + [pl.BlockSpec((own, full), lambda k, m, i, t, c, rank: (rank[0], 0))] * count
             + [ANY] * len(after),
             out_specs=[
                 pl.BlockSpec(
@@ -848,12 +962,13 @@
                 )
                 for index in range(2 * parts)
             ],
+            scratch_shapes=[pltpu.VMEM((rows, full), BF)],
         ),
-        out_shape=[jax.ShapeDtypeStruct(shape, F32)] * (2 * parts),
-        compiler_params=params(58),
-        cost_estimate=cost(2 * width * rows * right.shape[1], 4 * width * right.shape[1]),
+        out_shape=[jax.ShapeDtypeStruct((pieces // 2, high, wide), F32)] * (2 * parts),
+        compiler_params=params(58),
+        cost_estimate=cost(2 * width * rows * full, 4 * width * full),
         name="outer",
-    )(table, columns, left, right, *after)
+    )(table, columns, rank.reshape(1), left, *rights, *after)
 
 
 def in_grads_kernel(count, after, table_ref, left_ref, *refs):
@@ -1042,8 +1157,16 @@
     def send_far(self):
         self.got_far = swap(self.four, "tensor", 4)
 
+    def terms(self):
+        return [
+            (self.four_zero, 1),
+            (self.got_second, 1),
+            (self.got_near, 1),
+            (self.got_far, 0),
+        ]
+
     def result(self):
-        return self.four_zero[1] + self.got_second[1] + self.got_near[1] + self.got_far[0]
+        return sum(array[block] for array, block in self.terms())
 
 
 def odd_stage(ending, starting, passes=(), after=(), hold=False):
@@ -1175,6 +1298,7 @@
     hits = jnp.any(routes[:, :, None] == expert_ids[None, None, :], axis=1)
     counts = hits.astype(jnp.int32)
     kept_all = hits & (jnp.cumsum(counts, axis=0, dtype=jnp.int32) - counts < CAP)
+    kept_all = kept_all.astype(F32)
 
     query_low, key_low = [], []
 
@@ -1227,18 +1351,17 @@
     def plain_reduce(parts):
         return reduce_blocks([item[0] for item in parts])
 
-    middle, mixed, attended, probs, kept, gates = ([] for _ in range(6))
+    middle, mixed, attended, probs, gates = ([] for _ in range(5))
 
     def forward(c, after, last=False):
-        mid_c, mixed_c, logits_c, attended_c = branch(
-            pieces[c], w_whole, hidden_in, c, gain_mid, w_router, after
+        mid_c, mixed_c, probs_c, gates_c, attended_c = branch(
+            pieces[c], w_whole, hidden_in, c, gain_mid, w_router, kept_all, after
         )
         middle.append(mid_c)
         mixed.append(mixed_c)
         attended.append(attended_c)
-        probs.append(jax.nn.softmax(logits_c, axis=-1))
-        kept.append(lax.slice_in_dim(kept_all, c * length, (c + 1) * length, axis=0))
-        gates.append(jnp.where(kept[c], probs[c], 0.0))
+        probs.append(probs_c)
+        gates.append(gates_c)
         return acts_of(mixed_c, low[c], gates[c], w_gate, w_up, (), last)
 
     def mixed_blocks(c, after=()):
@@ -1261,21 +1384,22 @@
 
     if staged:
         acts = [forward(0, ())]
-        (far,) = tie((far,), (middle[0],))
+        (far,) = tie((far,), (middle[0], odd[0], odd[1]))
         both = swap(far, "tensor", 2)
         odd.append(swap(far, "tensor", 1))
-        (both,) = tie((both,), (acts[0][0],))
+        (both,) = tie((both,), (acts[0][0], odd[2]))
         odd.append(swap(both, "tensor", 1))
         even = [again, near, far, both]
         pieces.append([item for pair in zip(even, odd) for item in pair])
         mix = [Chain(mixed_blocks(0))]
+        (mix[0].first,) = tie((mix[0].first,), (odd[3],))
         mix[0].send_first()
         acts.append(forward(1, (mix[0].four_zero,), True))
         odd_stage(None, mix[0], after=(acts[1][0],))
         mix.append(Chain(mixed_blocks(1, (mix[0].six_two,))))
         even_stage(mix[0], mix[1])
-        moe = [Chain(moe_of(0, (mix[0].four,)))]
-        odd_stage(mix[0], mix[1], after=(moe[0].four_zero,))
+        grad_down = down_grads((mix[0].four,))
+        (grad_down,) = odd_stage(mix[0], mix[1], passes=(grad_down,))
     else:
         acts = []
         for c in chunks:
@@ -1285,34 +1409,19 @@
         grad_down = down_grads()
         grad_gate, grad_up = act_grads()
 
-    def all_own(values):
-        return jnp.concatenate([rows_own(value) for value in values], axis=0)
-
-    probs_own, kept_own, mid_own = all_own(probs), all_own(kept), all_own(middle)
-    mixed_own, attended_own = all_own(mixed), all_own(attended)
-    dy_own = jnp.concatenate([rows_own(cotangent, c * length) for c in chunks], axis=0)
-
     if staged:
-        grad_down = down_grads((mix[1].six_two, probs_own, mid_own, mixed_own, attended_own))
-        (grad_down,) = even_stage(mix[1], moe[0], passes=(grad_down,))
+        moe = [Chain(moe_of(0, (mix[1].six_two,)))]
+        even_stage(mix[1], moe[0])
         grad_gate, grad_up = act_grads((mix[1].four,))
         grad_gate, grad_up = odd_stage(mix[1], moe[0], passes=(grad_gate, grad_up))
-        mixed_share = [item.result() for item in mix]
-
-    mixed_share = jnp.concatenate(mixed_share, axis=0)
-    prob_grad = jnp.where(kept_own, mixed_share[:, width : width + experts], 0.0)
-    logit_own = (
-        probs_own * (prob_grad - jnp.sum(probs_own * prob_grad, axis=-1, keepdims=True))
-    ).astype(BF)
-    mixed_grad = mixed_share[:, :width] + dot(logit_own, w_router, 1, 1)
-    mid_scale = norm_scale(mid_own)
-    mid_hat = mid_own * mid_scale
-    grad_gain_mid = jnp.sum(mixed_grad * mid_hat, axis=0)
-    scaled = mixed_grad * gain_mid.astype(F32)
-    mid_grad = dy_own.astype(F32) + mid_scale * (
-        scaled - mid_hat * jnp.mean(scaled * mid_hat, axis=1, keepdims=True)
-    )
-    mid_low = mid_grad.astype(BF)
+        mixed_terms = [item.terms() for item in mix]
+    else:
+        mixed_terms = [[(item[None], 0)] for item in mixed_share]
+
+    mid_low, direct, direct_sums, vectors = mid_back(
+        rank, mixed_terms, middle, cotangent, hidden_in, probs, kept_all, mixed, gain_mid,
+        gain_in, w_router,
+    )
     if staged:
         moe.append(Chain(moe_of(1, (mid_low,), True)))
         (mid_low,) = even_stage(moe[0], moe[1], passes=(mid_low,))
@@ -1321,26 +1430,20 @@
 
     dp_table = dp_rank ^ jnp.arange(dp_count, dtype=jnp.int32)
     order = jnp.array(halves_order(count), jnp.int32)
-    out_parts = outer(mid_low.T, attended_own, dp_table, order, (blocks[0],))
+    out_parts = outer(mid_low, attended, rank, dp_table, order, (blocks[0],))
 
     q_scaled, k_scaled, value_grad, totals, gain_parts = attend_back(
         query_low, key_low, value_low, attended_grad, raws, square_sums, gains_here, angles,
         table, segments, scale, full_width, (out_parts[0],),
     )
     if staged:
-        (totals,) = odd_stage(moe[0], moe[1], passes=(totals,), hold=True)
+        odd_stage(moe[0], moe[1], after=(q_scaled,), hold=True)
     gain_parts = jnp.sum(gain_parts.reshape(seqs, 8, local_width), axis=0)
     totals = small_sum(totals, "tensor")
     query_grad, key_grad = raw_grads((q_scaled, k_scaled), raws, square_sums, totals, full_width)
     in_grads = [query_grad, key_grad, value_grad]
     weights_in = [w[None] for w in (w_query, w_key, w_value)]
     columns_in = back_columns if local_width % LANES == 0 and share % LANES == 0 else plain_columns
-
-    hidden_own = jnp.concatenate([rows_own(hidden_in, c * length) for c in chunks], axis=0)
-    hidden_own = hidden_own.astype(F32)
-    own_scale = norm_scale(hidden_own)
-    own_hat = hidden_own * own_scale
-    direct = mid_grad / (own_scale * gain_in.astype(F32))
 
     def normed_blocks(c):
         part_grads = [grad[c * length : (c + 1) * length] for grad in in_grads]
@@ -1393,13 +1496,10 @@
     gain_share = lax.dynamic_slice_in_dim(gain_in.astype(F32), rank * share, share, 0)
     in_scaled = normed_share * gain_share
     row_sums = jnp.sum(in_scaled * in_hat_share, axis=1).reshape(seqs, length)
-    direct_sums = jnp.sum(mid_grad * own_hat, axis=1) / own_scale[:, 0]
-    mine = lax.dynamic_slice_in_dim(row_sums, rank * own, own, 1) - direct_sums.reshape(seqs, own)
+    mine = lax.dynamic_slice_in_dim(row_sums, rank * own, own, 1)
+    mine = mine - direct_sums[:, 0].reshape(seqs, own)
     row_sums = lax.dynamic_update_slice_in_dim(row_sums, mine, rank * own, 1)
-    grad_router = dot(logit_own, mixed_own, 0, 0)
-    direct_gain = jnp.sum(direct * own_hat, axis=0)
-    wide = jnp.concatenate([grad_router, grad_gain_mid[None], direct_gain[None]], axis=0)
-    wide = small_sum(wide, "dp")
+    wide = small_sum(vectors, "dp")
     direct_gain = wide[experts + 1]
     wide = lax.dynamic_slice_in_dim(wide[: experts + 1], dp_rank * part, part, 1)
     flat = [row_sums.reshape(-1), wide.reshape(-1), direct_gain]

time: 1220 us -> 1180 us (0.967)
  waiting for transfers between devices: 454 us -> 424 us
  other arithmetic: 80.6 us -> 64 us
  local copies, waits for them, and re-layouts: 66.9 us -> 52.1 us
  starting transfers between devices: 82.7 us -> 97.5 us
    ppermute x70, waiting for transfers between devices: 454 us -> 424 us  [swap(): return lax.ppermute(value, axis, [(i, i ^ step) for i in range(count)])]
    ppermute x70, starting transfers between devices: 81.8 us -> 96.4 us  [swap(): return lax.ppermute(value, axis, [(i, i ^ step) for i in range(count)])]
    pallas_call x1 -> x2, Pallas kernels: 18.6 us -> 28.2 us  [the longest x1 18.6 us: outer(): pl.pallas_call(functools.partial(outer_kernel, count, len(after)), grid_s...]
    unnamed x180 -> x156, local copies, waits for them, and re-layouts: 38.7 us -> 36.9 us
  transfers between devices with their start and end apart: 75 -> 75, of which waited for: 37 -> 37; matrix products, arithmetic and copies ran while one was open for 10% -> 7% of each run, Pallas kernels for 41% -> 43%
where the time goes in v4:
time: 1180 us; the launch traced here: 1170 us
  Pallas kernels  514 us (44%)
  waiting for transfers between devices  424 us (36%)
  starting transfers between devices  97.5 us (8%)
  other arithmetic  64 us (5%)
  local copies, waits for them, and re-layouts  52.1 us (4%)
  between operations  15 us (1%)
    ppermute x70, waiting for transfers between devices, swap(): return lax.ppermute(value, axis, [(i, i ^ step) for i in range(count)])  424 us
    ppermute x70, starting transfers between devices, swap(): return lax.ppermute(value, axis, [(i, i ^ step) for i in range(count)])  96.4 us
    pallas_call x2, Pallas kernels, expert_grads(): pl.pallas_call(functools.partial(grads_kernel, min(512, width), chunks, l...  81.3 us
    pallas_call x4, Pallas kernels, back_columns(): pl.pallas_call(functools.partial(back_columns_kernel, min(512, tokens), c...  71.7 us
    pallas_call x2, Pallas kernels, expert_acts(): pl.pallas_call(functools.partial(expert_kernel, min(512, tokens), len(aft...  62.5 us
    pallas_call x2, Pallas kernels, back_rows(): pl.pallas_call(functools.partial(back_rows_kernel, min(512, tokens), coun...  54.4 us
    pallas_call x12, Pallas kernels, stage(): pl.pallas_call(functools.partial(stage_kernel, len(terms), parts, len(pas...  48.3 us
    pallas_call x2, Pallas kernels, branch(): pl.pallas_call(functools.partial(branch_kernel, len(pieces), len(after)),...  37.5 us
  transfers between devices with their start and end apart: 75, of which 37 were waited for; matrix products, arithmetic and copies ran while one was open for 7% of the time, Pallas kernels for 43%

profile of v4, /device:TPU:0, one launch (start us, length us, event | category | flops | bytes accessed | tf_op | source)
XLA Modules:
  0.0 1167.2 jit_solution(8666103861714576624)
XLA Ops:
  10.4 13.7 %project.1 = (bf16[2048,2048]{1,0:T(8,128)(2,1)}, f32[2048,256]{1,0:T(8,128)}, f32[2048,256]{1,0:T(8,128)}, bf16[2048,256]{1,0:T(8,128)(2,1)}, f32[8,2048]{1,0:T(8,128)}) custom-call(bf16[2048,2048]{1,0:T(8,128)(2,1)} %refs_16_.1, bf16[1,2048]{1,0:T(2,128)(2,1)} %reshape.153.gain_ref.refs_21_, bf16[2048,256]{1,0:T(8,128)(2,1)} %wq_ref.1, ...), custom_call_target="tpu_custom_call" | custom-call | flops 6442450944 | bytes 16777216 | tf_op jit(solution)/shard_map/project/pallas_call | solution.py:95
  67.8 27.9 %collective-permute-done.4.refs_2_.refs_1_ = f32[1024,256]{1,0:T(8,128)S(1)} collective-permute-done((f32[1024,256]{1,0:T(8,128)}, f32[1024,256]{1,0:T(8,128)S(1)}, u32[]{:S(2)}, u32[]{:S(2)}) %collective-permute-start.4) | collective-permute-done | bytes 1048608 | tf_op jit(solution)/shard_map/ppermute | solution.py:1085
  112.6 16.1 %low_grads.2.refs_0_.low_ref = f32[1024,2048]{1,0:T(8,128)} custom-call(bf16[2048,2048]{1,0:T(8,128)(2,1)} %refs_15_.1, bf16[16,2048,128]{2,1,0:T(8,128)(2,1)} %refs_1_.5, f32[1024,256]{1,0:T(8,128)} %get-tuple-element.143.refs_0_.refs_1_.refs_2_), custom_call_target="tpu_custom_call" | custom-call | flops 34359738368 | bytes 16777216 | tf_op jit(solution)/shard_map/low_grads/pallas_call | solution.py:405
  128.7 15.4 %low_grads.3.refs_2_.low_ref = f32[1024,2048]{1,0:T(8,128)} custom-call(bf16[2048,2048]{1,0:T(8,128)(2,1)} %refs_15_.1, bf16[16,2048,128]{2,1,0:T(8,128)(2,1)} %refs_1_.5, f32[1024,2048]{1,0:T(8,128)} %low_grads.2.refs_0_.low_ref), custom_call_target="tpu_custom_call" | custom-call | flops 1024 | bytes 1024 | tf_op jit(solution)/shard_map/low_grads/pallas_call | solution.py:405
  144.1 14.5 %collective-permute-done.6.refs_0_ = f32[1024,256]{1,0:T(8,128)S(1)} collective-permute-done((f32[1024,256]{1,0:T(8,128)S(1)}, f32[1024,256]{1,0:T(8,128)S(1)}, u32[]{:S(2)}, u32[]{:S(2)}) %collective-permute-start.6) | collective-permute-done | bytes 1048608 | tf_op jit(solution)/shard_map/ppermute | solution.py:1085
  161.1 24.7 %collective-permute-done.8.refs_0_ = f32[1024,256]{1,0:T(8,128)S(1)} collective-permute-done((f32[1024,256]{1,0:T(8,128)}, f32[1024,256]{1,0:T(8,128)S(1)}, u32[]{:S(2)}, u32[]{:S(2)}) %collective-permute-start.8) | collective-permute-done | bytes 1048608 | tf_op jit(solution)/shard_map/ppermute | solution.py:1085
  195.8 16.6 %collective-permute-done.9.refs_7_.refs_2_ = f32[1024,256]{1,0:T(8,128)S(1)} collective-permute-done((f32[1024,256]{1,0:T(8,128)}, f32[1024,256]{1,0:T(8,128)S(1)}, u32[]{:S(2)}, u32[]{:S(2)}) %collective-permute-start.9) | collective-permute-done | bytes 1048608 | tf_op jit(solution)/shard_map/ppermute | solution.py:1085
  231.6 18.8 %branch.2 = (f32[1024,2048]{1,0:T(8,128)}, bf16[1024,2048]{1,0:T(8,128)(2,1)}, f32[1024,16]{1,0:T(8,128)}, f32[1024,16]{1,0:T(8,128)}, bf16[1024,2048]{1,0:T(8,128)(2,1)}) custom-call(f32[1024,256]{1,0:T(8,128)} %get-tuple-element.142.refs_0_, f32[1024,256]{1,0:T(8,128)} %copy-done.52, f32[1024,256]{1,0:T(8,128)} %get-tuple-element.143.refs_0_.refs_1_.refs_2_, ...), custom_call_target="tpu_custom_call" | custom-call | flops 8589934592 | bytes 33554432 | tf_op jit(solution)/shard_map/branch/pallas_call | solution.py:731
  262.2 31.3 %expert_acts.2 = (bf16[1024,2048]{1,0:T(8,128)(2,1)}, bf16[1024,2048]{1,0:T(8,128)(2,1)}, bf16[1024,2048]{1,0:T(8,128)(2,1)}, f32[1024,128]{1,0:T(8,128)}) custom-call(bf16[1024,2048]{1,0:T(8,128)(2,1)} %get-tuple-element.146.mixed_ref.refs_0_.refs_13_, f32[1024,2048]{1,0:T(8,128)} %low_grads.2.refs_0_.low_ref, f32[1024,16]{1,0:T(8,128)} %get-tuple-element.147.gates_ref, ...), custom_call_target="tpu_custom_call" | custom-call | flops 17179869184 | bytes 25165824 | tf_op jit(solution)/shard_map/expert_acts/pallas_call | solution.py:469
  296.2 27.3 %back_rows.2 = (f32[2,128,2176]{2,1,0:T(8,128)}, f32[2,128,2176]{2,1,0:T(8,128)}, f32[2,128,2176]{2,1,0:T(8,128)}, f32[2,128,2176]{2,1,0:T(8,128)}) custom-call(s32[8]{0:T(128)} %gather_fusion, bf16[1024,2048]{1,0:T(8,128)(2,1)} %get-tuple-element.152.refs_0_.refs_3_, bf16[1024,2048]{1,0:T(8,128)(2,1)} %get-tuple-element.153.refs_1_.refs_4_, ...), custom_call_target="tpu_custom_call" | custom-call | flops 17179869184 | bytes 25165824 | tf_op jit(solution)/shard_map/back_rows/pallas_call | solution.py:601
  325.2 18.7 %branch.3 = (f32[1024,2048]{1,0:T(8,128)}, bf16[1024,2048]{1,0:T(8,128)(2,1)}, f32[1024,16]{1,0:T(8,128)}, f32[1024,16]{1,0:T(8,128)}, bf16[1024,2048]{1,0:T(8,128)(2,1)}) custom-call(f32[1024,256]{1,0:T(8,128)} %get-tuple-element.150.refs_0_, f32[1024,256]{1,0:T(8,128)} %copy-done.46, f32[1024,256]{1,0:T(8,128)} %get-tuple-element.151.refs_2_, ...), custom_call_target="tpu_custom_call" | custom-call | flops 8589934592 | bytes 33554432 | tf_op jit(solution)/shard_map/branch/pallas_call | solution.py:731
  343.9 31.2 %expert_acts.3 = (bf16[1024,2048]{1,0:T(8,128)(2,1)}, bf16[1024,2048]{1,0:T(8,128)(2,1)}, bf16[1024,2048]{1,0:T(8,128)(2,1)}, f32[1024,128]{1,0:T(8,128)}) custom-call(bf16[1024,2048]{1,0:T(8,128)(2,1)} %get-tuple-element.156.mixed_ref.refs_1_.refs_19_, f32[1024,2048]{1,0:T(8,128)} %low_grads.3.refs_2_.low_ref, f32[1024,16]{1,0:T(8,128)} %get-tuple-element.157.gates_ref, ...), custom_call_target="tpu_custom_call" | custom-call | flops 1024 | bytes 1024 | tf_op jit(solution)/shard_map/expert_acts/pallas_call | solution.py:469
  384.0 27.1 %back_rows.3 = (f32[2,128,2176]{2,1,0:T(8,128)}, f32[2,128,2176]{2,1,0:T(8,128)}, f32[2,128,2176]{2,1,0:T(8,128)}, f32[2,128,2176]{2,1,0:T(8,128)}) custom-call(s32[8]{0:T(128)} %gather_fusion, bf16[1024,2048]{1,0:T(8,128)(2,1)} %get-tuple-element.158.refs_0_.refs_5_, bf16[1024,2048]{1,0:T(8,128)(2,1)} %get-tuple-element.159.refs_1_.refs_6_, ...), custom_call_target="tpu_custom_call" | custom-call | flops 17179869184 | bytes 25165824 | tf_op jit(solution)/shard_map/back_rows/pallas_call | solution.py:601
  411.1 19.2 %collective-permute-done.18.refs_1_ = f32[2,128,2176]{2,1,0:T(8,128)S(1)} collective-permute-done((f32[2,128,2176]{2,1,0:T(8,128)}, f32[2,128,2176]{2,1,0:T(8,128)S(1)}, u32[]{:S(2)}, u32[]{:S(2)}) %collective-permute-start.18) | collective-permute-done | bytes 2228256 | tf_op jit(solution)/shard_map/ppermute | solution.py:1085
  437.9 31.2 %expert_grads.2.refs_2_ = f32[16,2048,128]{2,1,0:T(8,128)} custom-call(bf16[2048,2048]{1,0:T(8,128)(2,1)} %refs_15_.1, bf16[2048,2048]{1,0:T(8,128)(2,1)} %refs_15_.1, f32[1,128,2176]{2,1,0:T(8,128)} %get-tuple-element.170.refs_2_, bf16[1024,2048]{1,0:T(8,128)(2,1)} %get-tuple-element.148.refs_1_.refs_3_.refs_0_, ...), custom_call_target="tpu_custom_call" | custom-call | flops 17179869184 | bytes 25165824 | tf_op jit(solution)/shard_map/expert_grads/pallas_call | solution.py:688
  469.1 17.8 %collective-permute-done.21.refs_4_.refs_3_ = f32[1,128,2176]{2,1,0:T(8,128)S(1)} collective-permute-done((f32[1,128,2176]{2,1,0:T(8,128)}, f32[1,128,2176]{2,1,0:T(8,128)S(1)}, u32[]{:S(2)}, u32[]{:S(2)}) %collective-permute-start.21) | collective-permute-done | bytes 1114144 | tf_op jit(solution)/shard_map/ppermute | solution.py:1085
  493.7 22.3 %back_columns.4 = (f32[2,1024,256]{2,1,0:T(8,128)}, f32[2,1024,256]{2,1,0:T(8,128)}, f32[2,1024,256]{2,1,0:T(8,128)}, f32[2,1024,256]{2,1,0:T(8,128)}) custom-call(s32[8]{0:T(128)} %gather_fusion, s32[1]{0:T(128)} %constant.53.clone.1.rank_ref, bf16[1024,2048]{1,0:T(8,128)(2,1)} %get-tuple-element.148.refs_1_.refs_3_.refs_0_, ...), custom_call_target="tpu_custom_call" | custom-call | flops 8589934592 | bytes 16777216 | tf_op jit(solution)/shard_map/back_columns/pallas_call | solution.py:531
  516.0 26.4 %collective-permute-done.22.refs_1_.refs_5_ = f32[2,128,2176]{2,1,0:T(8,128)S(1)} collective-permute-done((f32[2,128,2176]{2,1,0:T(8,128)}, f32[2,128,2176]{2,1,0:T(8,128)S(1)}, u32[]{:S(2)}, u32[]{:S(2)}) %collective-permute-start.22) | collective-permute-done | bytes 2228256 | tf_op jit(solution)/shard_map/ppermute | solution.py:1085
  550.5 50.0 %expert_grads.3 = (f32[16,2048,128]{2,1,0:T(8,128)}, f32[16,2048,128]{2,1,0:T(8,128)}) custom-call(bf16[1024,2048]{1,0:T(8,128)(2,1)} %get-tuple-element.146.mixed_ref.refs_0_.refs_13_, bf16[1024,2048]{1,0:T(8,128)(2,1)} %get-tuple-element.156.mixed_ref.refs_1_.refs_19_, f32[1,128,2176]{2,1,0:T(8,128)} %get-tuple-element.179.refs_2_, ...), custom_call_target="tpu_custom_call" | custom-call | flops 34359738368 | bytes 50331648 | tf_op jit(solution)/shard_map/expert_grads/pallas_call | solution.py:688
  622.6 22.2 %back_columns.5 = (f32[2,1024,256]{2,1,0:T(8,128)}, f32[2,1024,256]{2,1,0:T(8,128)}, f32[2,1024,256]{2,1,0:T(8,128)}, f32[2,1024,256]{2,1,0:T(8,128)}) custom-call(s32[8]{0:T(128)} %gather_fusion, s32[1]{0:T(128)} %constant.53.clone.1.rank_ref, bf16[1024,2048]{1,0:T(8,128)(2,1)} %get-tuple-element.164.refs_3_.refs_4_.refs_0_, ...), custom_call_target="tpu_custom_call" | custom-call | flops 1024 | bytes 1024 | tf_op jit(solution)/shard_map/back_columns/pallas_call | solution.py:531
  677.3 18.6 %outer.1 = (f32[4,512,256]{2,1,0:T(8,128)}, f32[4,512,256]{2,1,0:T(8,128)}, f32[4,512,256]{2,1,0:T(8,128)}, f32[4,512,256]{2,1,0:T(8,128)}, f32[4,512,256]{2,1,0...) custom-call(s32[4]{0:T(128)} %iota_xor_fusion.table_ref, ...), custom_call_target="tpu_custom_call" | custom-call | flops 2147483648 | bytes 16777216 | tf_op jit(solution)/shard_map/outer/pallas_call | solution.py:940
  714.0 24.8 %attend_back.1 = (f32[2048,256]{1,0:T(8,128)}, f32[2048,256]{1,0:T(8,128)}, bf16[2048,256]{1,0:T(8,128)(2,1)}, f32[8,2048]{1,0:T(8,128)}, f32[16,256]{1,0:T(8,128)}) custom-call(s32[8]{0:T(128)} %copy-done, bf16[2048,256]{1,0:T(8,128)(2,1)} %get-tuple-element.280.q_ref, bf16[2048,256]{1,0:T(8,128)(2,1)} %get-tuple-element.281.k_ref, ...), custom_call_target="tpu_custom_call" | custom-call | flops 5368709120 | bytes 15728640 | tf_op jit(solution)/shard_map/attend_back/pallas_call | solution.py:290
  750.4 24.7 %collective-permute-start.38 = (f32[8,2048]{1,0:T(8,128)S(1)}, f32[8,2048]{1,0:T(8,128)S(1)}, u32[]{:S(2)}, u32[]{:S(2)}) collective-permute-start(f32[8,2048]{1,0:T(8,128)S(1)} %add.202), channel_id=1, source_target_pairs={{0,2},{1,3},{2,0},{3,1},{4,6},{5,7},{6,4},{7,5},{8,10},{9,11},{10,... | collective-permute-start | bytes 196616 | tf_op jit(solution)/shard_map/ppermute | solution.py:1085
  818.2 13.7 %back_columns.6 = (f32[2,1024,256]{2,1,0:T(8,128)}, f32[2,1024,256]{2,1,0:T(8,128)}, f32[2,1024,256]{2,1,0:T(8,128)}, f32[2,1024,256]{2,1,0:T(8,128)}) custom-call(s32[8]{0:T(128)} %gather_fusion, s32[1]{0:T(128)} %bitcast.6.rank_ref, bf16[1024,256]{1,0:T(8,128)(2,1)} %get-tuple-element.268.refs_0_, bf16[1024,256]{1,0:T(8,128)(2,1)} %get-tuple-element.266.refs_1_, ...), custom_call_target="tpu_custom_call" | custom-call | flops 3221225472 | bytes 33554432 | tf_op jit(solution)/shard_map/back_columns/pallas_call | solution.py:531
  839.2 13.7 %in_grads.1 = (f32[512,768]{1,0:T(8,128)}, f32[512,768]{1,0:T(8,128)}, f32[512,768]{1,0:T(8,128)}, f32[512,768]{1,0:T(8,128)}) custom-call(s32[4]{0:T(128)} %iota_xor_fusion.table_ref, bf16[2048,2048]{1,0:T(8,128)(2,1)} %get-tuple-element.229.left_ref, bf16[2048,256]{1,0:T(8,128)(2,1)} %get-tuple-element.218.refs_0_, ...), custom_call_target="tpu_custom_call" | custom-call | flops 1024 | bytes 1024 | tf_op jit(solution)/shard_map/in_grads/pallas_call | solution.py:996
  852.9 26.7 %collective-permute-done.42.refs_4_ = f32[1,1024,256]{2,1,0:T(8,128)S(1)} collective-permute-done((f32[1,1024,256]{2,1,0:T(8,128)}, f32[1,1024,256]{2,1,0:T(8,128)S(1)}, u32[]{:S(2)}, u32[]{:S(2)}) %collective-permute-start.42) | collective-permute-done | bytes 1048608 | tf_op jit(solution)/shard_map/ppermute | solution.py:1085
  892.2 40.7 %collective-permute-done.44.refs_1_ = f32[2,1024,256]{2,1,0:T(8,128)S(1)} collective-permute-done((f32[2,1024,256]{2,1,0:T(8,128)}, f32[2,1024,256]{2,1,0:T(8,128)S(1)}, u32[]{:S(2)}, u32[]{:S(2)}) %collective-permute-start.44) | collective-permute-done | bytes 2097184 | tf_op jit(solution)/shard_map/ppermute | solution.py:1085
  953.5 35.2 %collective-permute-done.46.refs_4_ = f32[1,1024,256]{2,1,0:T(8,128)S(1)} collective-permute-done((f32[1,1024,256]{2,1,0:T(8,128)}, f32[1,1024,256]{2,1,0:T(8,128)S(1)}, u32[]{:S(2)}, u32[]{:S(2)}) %collective-permute-start.46) | collective-permute-done | bytes 1048608 | tf_op jit(solution)/shard_map/ppermute | solution.py:1085
  1011.1 19.7 %collective-permute-done.58 = f32[512,768]{1,0:T(8,128)} collective-permute-done((f32[512,768]{1,0:T(8,128)}, f32[512,768]{1,0:T(8,128)}, u32[]{:S(2)}, u32[]{:S(2)}) %collective-permute-start.58) | collective-permute-done | bytes 1572896 | tf_op jit(solution)/shard_map/ppermute | solution.py:1085
  1059.8 35.4 %collective-permute-done.59 = f32[1,1024,256]{2,1,0:T(8,128)S(1)} collective-permute-done((f32[1,1024,256]{2,1,0:T(8,128)}, f32[1,1024,256]{2,1,0:T(8,128)S(1)}, u32[]{:S(2)}, u32[]{:S(2)}) %collective-permute-start.59) | collective-permute-done | bytes 1048608 | tf_op jit(solution)/shard_map/ppermute | solution.py:1085
  1112.5 19.0 %collective-permute-done.64 = f32[1,12800]{1,0:T(1,128)S(1)} collective-permute-done((f32[1,12800]{1,0:T(1,128)S(1)}, f32[1,12800]{1,0:T(1,128)S(1)}, u32[]{:S(2)}, u32[]{:S(2)}) %collective-permute-start.64) | collective-permute-done | bytes 51232 | tf_op jit(solution)/shard_map/ppermute | solution.py:1085
  1140.7 17.7 %collective-permute-done.67 = f32[1,512,256]{2,1,0:T(8,128)} collective-permute-done((f32[1,512,256]{2,1,0:T(8,128)}, f32[1,512,256]{2,1,0:T(8,128)}, u32[]{:S(2)}, u32[]{:S(2)}) %collective-permute-start.67) | collective-permute-done | bytes 524320 | tf_op jit(solution)/shard_map/ppermute | solution.py:1085
  (410 shorter events, 390.2 us)
Async XLA Ops:
  7.2 100.7 %all-gather.5.cloned.1.call-start = ((), (), s32[]{:S(2)}) async-start(), calls=%async_computation.6 | async-start | bytes 4718592 | tf_op jit(solution)/shard_map/all_gather | solution.py:1284
  9.1 210.7 %all-gather.7.cloned.1.call-start = ((), (), s32[]{:S(2)}) async-start(), calls=%async_computation.7 | async-start | bytes 20971520 | tf_op jit(solution)/shard_map/all_gather | solution.py:1326
  57.0 49.9 %collective-permute-start.3 = (f32[1024,256]{1,0:T(8,128)}, f32[1024,256]{1,0:T(8,128)S(1)}, u32[]{:S(2)}, u32[]{:S(2)}) collective-permute-start(f32[1024,256]{1,0:T(8,128)} %get-tuple-element.140.refs_0_.refs_1_), channel_id=1, source_target_pairs={{0,2},{1,3},{2,0},{3,1},{4,6},{5,7},{6,4},{7,5},{8,10},{9,11},{10,... | collective-permute-start | bytes 3145736 | tf_op jit(solution)/shard_map/ppermute | solution.py:1085
  107.9 1052.4 %reduce-scatter.8.cloned.1.call-start = ((), (), s32[]{:S(2)}) async-start(), calls=%async_computation.5 | async-start | bytes 20971520 | tf_op jit(solution)/shard_map/reduce_scatter | solution.py:1488
  109.1 49.5 %collective-permute-start.5 = (f32[1024,256]{1,0:T(8,128)S(1)}, f32[1024,256]{1,0:T(8,128)S(1)}, u32[]{:S(2)}, u32[]{:S(2)}) collective-permute-start(f32[1024,256]{1,0:T(8,128)S(1)} %copy-done.36), channel_id=1, source_target_pairs={{0,1},{1,0},{2,3},{3,2},{4,5},{5,4},{6,7},{7,6},{8,9},{9,8},{10,11... | collective-permute-start | bytes 3145736 | tf_op jit(solution)/shard_map/ppermute | solution.py:1085
  110.6 48.0 %collective-permute-start.6 = (f32[1024,256]{1,0:T(8,128)S(1)}, f32[1024,256]{1,0:T(8,128)S(1)}, u32[]{:S(2)}, u32[]{:S(2)}) collective-permute-start(f32[1024,256]{1,0:T(8,128)S(1)} %copy-done.54), channel_id=1, source_target_pairs={{0,4},{1,5},{2,6},{3,7},{4,0},{5,1},{6,2},{7,3},{8,12},{9,13},{10,... | collective-permute-start | bytes 3145736 | tf_op jit(solution)/shard_map/ppermute | solution.py:1085
  213.4 47.1 %collective-permute-start.13 = (f32[1024,256]{1,0:T(8,128)}, f32[1024,256]{1,0:T(8,128)}, u32[]{:S(2)}, u32[]{:S(2)}) collective-permute-start(f32[1024,256]{1,0:T(8,128)} %get-tuple-element.150.refs_0_), channel_id=1, source_target_pairs={{0,4},{1,5},{2,6},{3,7},{4,0},{5,1},{6,2},{7,3},{8,12},{9,13},{10,... | collective-permute-start | bytes 3145736 | tf_op jit(solution)/shard_map/ppermute | solution.py:1085
  213.8 46.7 %collective-permute-start.11 = (f32[1024,256]{1,0:T(8,128)}, f32[1024,256]{1,0:T(8,128)S(1)}, u32[]{:S(2)}, u32[]{:S(2)}) collective-permute-start(f32[1024,256]{1,0:T(8,128)} %get-tuple-element.150.refs_0_), channel_id=1, source_target_pairs={{0,1},{1,0},{2,3},{3,2},{4,5},{5,4},{6,7},{7,6},{8,9},{9,8},{10,11... | collective-permute-start | bytes 3145736 | tf_op jit(solution)/shard_map/ppermute | solution.py:1085
  324.5 50.5 %collective-permute-start.17 = (f32[2,128,2176]{2,1,0:T(8,128)}, f32[2,128,2176]{2,1,0:T(8,128)S(1)}, u32[]{:S(2)}, u32[]{:S(2)}) collective-permute-start(f32[2,128,2176]{2,1,0:T(8,128)} %tie.16), channel_id=1, source_target_pairs={{0,1},{1,0},{2,3},{3,2},{4,5},{5,4},{6,7},{7,6},{8,9},{9,8},{10,11... | collective-permute-start | bytes 6684680 | tf_op jit(solution)/shard_map/ppermute | solution.py:1085
  380.7 49.6 %collective-permute-start.18 = (f32[2,128,2176]{2,1,0:T(8,128)}, f32[2,128,2176]{2,1,0:T(8,128)S(1)}, u32[]{:S(2)}, u32[]{:S(2)}) collective-permute-start(f32[2,128,2176]{2,1,0:T(8,128)} %get-tuple-element.167), channel_id=1, source_target_pairs={{0,1},{1,0},{2,3},{3,2},{4,5},{5,4},{6,7},{7,6},{8,9},{9,8},{10,11... | collective-permute-start | bytes 6684680 | tf_op jit(solution)/shard_map/ppermute | solution.py:1085
  382.1 49.3 %collective-permute-start.19 = (f32[2,128,2176]{2,1,0:T(8,128)}, f32[2,128,2176]{2,1,0:T(8,128)S(1)}, u32[]{:S(2)}, u32[]{:S(2)}) collective-permute-start(f32[2,128,2176]{2,1,0:T(8,128)} %get-tuple-element.165.refs_5_), channel_id=1, source_target_pairs={{0,2},{1,3},{2,0},{3,1},{4,6},{5,7},{6,4},{7,5},{8,10},{9,11},{10,... | collective-permute-start | bytes 6684680 | tf_op jit(solution)/shard_map/ppermute | solution.py:1085
  436.6 50.3 %collective-permute-start.20 = (f32[2,128,2176]{2,1,0:T(8,128)}, f32[2,128,2176]{2,1,0:T(8,128)S(1)}, u32[]{:S(2)}, u32[]{:S(2)}) collective-permute-start(f32[2,128,2176]{2,1,0:T(8,128)} %get-tuple-element.169), channel_id=1, source_target_pairs={{0,1},{1,0},{2,3},{3,2},{4,5},{5,4},{6,7},{7,6},{8,9},{9,8},{10,11... | collective-permute-start | bytes 6684680 | tf_op jit(solution)/shard_map/ppermute | solution.py:1085
  437.6 49.3 %collective-permute-start.21 = (f32[1,128,2176]{2,1,0:T(8,128)}, f32[1,128,2176]{2,1,0:T(8,128)S(1)}, u32[]{:S(2)}, u32[]{:S(2)}) collective-permute-start(f32[1,128,2176]{2,1,0:T(8,128)} %get-tuple-element.170.refs_2_), channel_id=1, source_target_pairs={{0,4},{1,5},{2,6},{3,7},{4,0},{5,1},{6,2},{7,3},{8,12},{9,13},{10,... | collective-permute-start | bytes 3342344 | tf_op jit(solution)/shard_map/ppermute | solution.py:1085
  492.8 667.4 %reduce-scatter.4.cloned.1.call-start = ((), (), s32[]{:S(2)}) async-start(), calls=%async_computation.3 | async-start | bytes 20971520 | tf_op jit(solution)/shard_map/reduce_scatter | solution.py:1488
  492.9 49.6 %collective-permute-start.22 = (f32[2,128,2176]{2,1,0:T(8,128)}, f32[2,128,2176]{2,1,0:T(8,128)S(1)}, u32[]{:S(2)}, u32[]{:S(2)}) collective-permute-start(f32[2,128,2176]{2,1,0:T(8,128)} %get-tuple-element.176), channel_id=1, source_target_pairs={{0,1},{1,0},{2,3},{3,2},{4,5},{5,4},{6,7},{7,6},{8,9},{9,8},{10,11... | collective-permute-start | bytes 6684680 | tf_op jit(solution)/shard_map/ppermute | solution.py:1085
  493.7 49.2 %collective-permute-start.23 = (f32[2,128,2176]{2,1,0:T(8,128)}, f32[2,128,2176]{2,1,0:T(8,128)S(1)}, u32[]{:S(2)}, u32[]{:S(2)}) collective-permute-start(f32[2,128,2176]{2,1,0:T(8,128)} %get-tuple-element.172.refs_2_), channel_id=1, source_target_pairs={{0,2},{1,3},{2,0},{3,1},{4,6},{5,7},{6,4},{7,5},{8,10},{9,11},{10,... | collective-permute-start | bytes 6684680 | tf_op jit(solution)/shard_map/ppermute | solution.py:1085
  548.4 52.1 %collective-permute-start.25 = (f32[1,128,2176]{2,1,0:T(8,128)}, f32[1,128,2176]{2,1,0:T(8,128)S(1)}, u32[]{:S(2)}, u32[]{:S(2)}) collective-permute-start(f32[1,128,2176]{2,1,0:T(8,128)} %get-tuple-element.179.refs_2_), channel_id=1, source_target_pairs={{0,4},{1,5},{2,6},{3,7},{4,0},{5,1},{6,2},{7,3},{8,12},{9,13},{10,... | collective-permute-start | bytes 3342344 | tf_op jit(solution)/shard_map/ppermute | solution.py:1085
  549.2 51.3 %collective-permute-start.24 = (f32[2,1024,256]{2,1,0:T(8,128)}, f32[2,1024,256]{2,1,0:T(8,128)S(1)}, u32[]{:S(2)}, u32[]{:S(2)}) collective-permute-start(f32[2,1024,256]{2,1,0:T(8,128)} %get-tuple-element.178), channel_id=1, source_target_pairs={{0,1},{1,0},{2,3},{3,2},{4,5},{5,4},{6,7},{7,6},{8,9},{9,8},{10,11... | collective-permute-start | bytes 6291464 | tf_op jit(solution)/shard_map/ppermute | solution.py:1085
  606.4 553.8 %reduce-scatter.6.cloned.1.call-start = ((), (), s32[]{:S(2)}) async-start(), calls=%async_computation.4 | async-start | bytes 20971520 | tf_op jit(solution)/shard_map/reduce_scatter | solution.py:1488
  698.6 84.6 %collective-permute-start.29 = (f32[2,1024,256]{2,1,0:T(8,128)S(1)}, f32[2,1024,256]{2,1,0:T(8,128)S(1)}, u32[]{:S(2)}, u32[]{:S(2)}) collective-permute-start(f32[2,1024,256]{2,1,0:T(8,128)S(1)} %copy-done.44), channel_id=1, source_target_pairs={{0,1},{1,0},{2,3},{3,2},{4,5},{5,4},{6,7},{7,6},{8,9},{9,8},{10,11... | collective-permute-start | bytes 6291464 | tf_op jit(solution)/shard_map/ppermute | solution.py:1085
  703.4 79.8 %collective-permute-start.28 = (f32[1,1024,256]{2,1,0:T(8,128)}, f32[1,1024,256]{2,1,0:T(8,128)S(1)}, u32[]{:S(2)}, u32[]{:S(2)}) collective-permute-start(f32[1,1024,256]{2,1,0:T(8,128)} %get-tuple-element.190), channel_id=1, source_target_pairs={{0,4},{1,5},{2,6},{3,7},{4,0},{5,1},{6,2},{7,3},{8,12},{9,13},{10,... | collective-permute-start | bytes 3145736 | tf_op jit(solution)/shard_map/ppermute | solution.py:1085
  839.2 48.4 %collective-permute-start.49 = (f32[4,512,256]{2,1,0:T(8,128)}, f32[4,512,256]{2,1,0:T(8,128)}, u32[]{:S(2)}, u32[]{:S(2)}) collective-permute-start(f32[4,512,256]{2,1,0:T(8,128)} %get-tuple-element.241), channel_id=1, source_target_pairs={{0,8},{8,0},{16,24},{24,16},{1,9},{9,1},{17,25},{25,17},{2,10},{10... | collective-permute-start | bytes 6291464 | tf_op jit(solution)/shard_map/ppermute | solution.py:1085
  885.4 47.5 %collective-permute-start.44 = (f32[2,1024,256]{2,1,0:T(8,128)}, f32[2,1024,256]{2,1,0:T(8,128)S(1)}, u32[]{:S(2)}, u32[]{:S(2)}) collective-permute-start(f32[2,1024,256]{2,1,0:T(8,128)} %get-tuple-element.231), channel_id=1, source_target_pairs={{0,1},{1,0},{2,3},{3,2},{4,5},{5,4},{6,7},{7,6},{8,9},{9,8},{10,11... | collective-permute-start | bytes 6291464 | tf_op jit(solution)/shard_map/ppermute | solution.py:1085
  887.1 47.3 %collective-permute-start.45 = (f32[2,1024,256]{2,1,0:T(8,128)}, f32[2,1024,256]{2,1,0:T(8,128)S(1)}, u32[]{:S(2)}, u32[]{:S(2)}) collective-permute-start(f32[2,1024,256]{2,1,0:T(8,128)} %get-tuple-element.232), channel_id=1, source_target_pairs={{0,2},{1,3},{2,0},{3,1},{4,6},{5,7},{6,4},{7,5},{8,10},{9,11},{10,... | collective-permute-start | bytes 6291464 | tf_op jit(solution)/shard_map/ppermute | solution.py:1085
  887.1 53.4 %collective-permute-start.48 = (f32[4,512,256]{2,1,0:T(8,128)}, f32[4,512,256]{2,1,0:T(8,128)}, u32[]{:S(2)}, u32[]{:S(2)}) collective-permute-start(f32[4,512,256]{2,1,0:T(8,128)} %get-tuple-element.239), channel_id=1, source_target_pairs={{0,8},{8,0},{16,24},{24,16},{1,9},{9,1},{17,25},{25,17},{2,10},{10... | collective-permute-start | bytes 6291464 | tf_op jit(solution)/shard_map/ppermute | solution.py:1085
  887.1 53.9 %collective-permute-start.54 = (f32[4,512,256]{2,1,0:T(8,128)}, f32[4,512,256]{2,1,0:T(8,128)}, u32[]{:S(2)}, u32[]{:S(2)}) collective-permute-start(f32[4,512,256]{2,1,0:T(8,128)} %get-tuple-element.246), channel_id=1, source_target_pairs={{0,8},{8,0},{16,24},{24,16},{1,9},{9,1},{17,25},{25,17},{2,10},{10... | collective-permute-start | bytes 6291464 | tf_op jit(solution)/shard_map/ppermute | solution.py:1085
  891.4 53.5 %collective-permute-start.50 = (f32[4,512,256]{2,1,0:T(8,128)}, f32[4,512,256]{2,1,0:T(8,128)}, u32[]{:S(2)}, u32[]{:S(2)}) collective-permute-start(f32[4,512,256]{2,1,0:T(8,128)} %add.219), channel_id=1, source_target_pairs={{0,16},{8,24},{16,0},{24,8},{1,17},{9,25},{17,1},{25,9},{2,18},{10... | collective-permute-start | bytes 6291464 | tf_op jit(solution)/shard_map/ppermute | solution.py:1085
  939.5 49.3 %collective-permute-start.47 = (f32[2,1024,256]{2,1,0:T(8,128)}, f32[2,1024,256]{2,1,0:T(8,128)S(1)}, u32[]{:S(2)}, u32[]{:S(2)}) collective-permute-start(f32[2,1024,256]{2,1,0:T(8,128)} %get-tuple-element.236), channel_id=1, source_target_pairs={{0,1},{1,0},{2,3},{3,2},{4,5},{5,4},{6,7},{7,6},{8,9},{9,8},{10,11... | collective-permute-start | bytes 6291464 | tf_op jit(solution)/shard_map/ppermute | solution.py:1085
  940.4 58.4 %collective-permute-start.53 = (f32[4,512,256]{2,1,0:T(8,128)}, f32[4,512,256]{2,1,0:T(8,128)}, u32[]{:S(2)}, u32[]{:S(2)}) collective-permute-start(f32[4,512,256]{2,1,0:T(8,128)} %get-tuple-element.244), channel_id=1, source_target_pairs={{0,8},{8,0},{16,24},{24,16},{1,9},{9,1},{17,25},{25,17},{2,10},{10... | collective-permute-start | bytes 6291464 | tf_op jit(solution)/shard_map/ppermute | solution.py:1085
  941.0 47.7 %collective-permute-start.46 = (f32[1,1024,256]{2,1,0:T(8,128)}, f32[1,1024,256]{2,1,0:T(8,128)S(1)}, u32[]{:S(2)}, u32[]{:S(2)}) collective-permute-start(f32[1,1024,256]{2,1,0:T(8,128)} %get-tuple-element.234), channel_id=1, source_target_pairs={{0,4},{1,5},{2,6},{3,7},{4,0},{5,1},{6,2},{7,3},{8,12},{9,13},{10,... | collective-permute-start | bytes 3145736 | tf_op jit(solution)/shard_map/ppermute | solution.py:1085
  944.9 61.4 %collective-permute-start.55 = (f32[4,512,256]{2,1,0:T(8,128)}, f32[4,512,256]{2,1,0:T(8,128)}, u32[]{:S(2)}, u32[]{:S(2)}) collective-permute-start(f32[4,512,256]{2,1,0:T(8,128)} %add.224), channel_id=1, source_target_pairs={{0,16},{8,24},{16,0},{24,8},{1,17},{9,25},{17,1},{25,9},{2,18},{10... | collective-permute-start | bytes 6291464 | tf_op jit(solution)/shard_map/ppermute | solution.py:1085
  947.1 50.8 %collective-permute-start.61 = (f32[24,2048]{1,0:T(8,128)S(1)}, f32[24,2048]{1,0:T(8,128)S(1)}, u32[]{:S(2)}, u32[]{:S(2)}) collective-permute-start(f32[24,2048]{1,0:T(8,128)S(1)} %add.232), channel_id=1, source_target_pairs={{0,16},{8,24},{16,0},{24,8},{1,17},{9,25},{17,1},{25,9},{2,18},{10... | collective-permute-start | bytes 589832 | tf_op jit(solution)/shard_map/ppermute | solution.py:1085
  (114 other events, 1557.3 us)
Sparse Core Ops, SparseCore 0:
  10.1 97.1 all-gather.4
  108.9 106.0 all-gather.6
  493.0 124.2 reduce-scatter.7
  620.4 126.0 reduce-scatter.3
  749.6 126.0 reduce-scatter.5

commit v5 on v4

--- a/solution.py
+++ b/solution.py
@@ -1437,7 +1437,10 @@
         table, segments, scale, full_width, (out_parts[0],),
     )
     if staged:
-        odd_stage(moe[0], moe[1], after=(q_scaled,), hold=True)
+        out_high = reduce_first(out_parts[1::2], "dp")
+        out_low = reduce_first(out_parts[::2], "dp")
+        after = (q_scaled, out_high[0], out_high[2], out_low[0], out_low[2])
+        odd_stage(moe[0], moe[1], after=after, hold=True)
     gain_parts = jnp.sum(gain_parts.reshape(seqs, 8, local_width), axis=0)
     totals = small_sum(totals, "tensor")
     query_grad, key_grad = raw_grads((q_scaled, k_scaled), raws, square_sums, totals, full_width)
@@ -1457,12 +1460,13 @@
         norm = [Chain(normed_blocks(c)) for c in chunks]
         even_stage(moe[1], norm[0], after=(norm[1].four_zero,))
         grad_in = in_grads_of(normed, in_grads, dp_table, (moe[1].four,))
-        odd_stage(moe[1], norm[0], after=(grad_in[0],))
+        grad_in = reduce_first(grad_in, "dp")
+        odd_stage(moe[1], norm[0], after=(grad_in[0], grad_in[2]))
         even_stage(norm[0], norm[1])
-        out_high = reduce_blocks(out_parts[1::2], "dp")
+        out_high = reduce_blocks(out_high, "dp", 2)
         odd_stage(norm[0], norm[1], after=(out_high,))
-        out_low = reduce_blocks(out_parts[::2], "dp")
-        grad_in = reduce_blocks(grad_in, "dp")
+        out_low = reduce_blocks(out_low, "dp", 2)
+        grad_in = reduce_blocks(grad_in, "dp", 2)
         (out_high,) = even_stage(norm[1], None, passes=(out_high,), after=(out_low, grad_in))
         grad_w_out = reduce_halves(out_low, out_high)
         normed_share = [item.result() for item in norm]

time: 1180 us -> 1300 us (1.10)
  waiting for transfers between devices: 424 us -> 568 us
    ppermute x70, waiting for transfers between devices: 424 us -> 568 us  [swap(): return lax.ppermute(value, axis, [(i, i ^ step) for i in range(count)])]
    unnamed x156 -> x182, local copies, waits for them, and re-layouts: 36.9 us -> 32.7 us
  transfers between devices with their start and end apart: 75 -> 75, of which waited for: 37 -> 46; matrix products, arithmetic and copies ran while one was open for 7% -> 6% of each run, Pallas kernels for 43% -> 39%
where the time goes in v5:
time: 1300 us; the launch traced here: 1290 us
  waiting for transfers between devices  568 us (44%)
  Pallas kernels  515 us (40%)
  starting transfers between devices  90.4 us (7%)
  other arithmetic  56.8 us (4%)
  local copies, waits for them, and re-layouts  47.2 us (4%)
  between operations  15.1 us (1%)
    ppermute x70, waiting for transfers between devices, swap(): return lax.ppermute(value, axis, [(i, i ^ step) for i in range(count)])  568 us
    ppermute x70, starting transfers between devices, swap(): return lax.ppermute(value, axis, [(i, i ^ step) for i in range(count)])  89.9 us
    pallas_call x2, Pallas kernels, expert_grads(): pl.pallas_call(functools.partial(grads_kernel, min(512, width), chunks, l...  81.3 us
    pallas_call x4, Pallas kernels, back_columns(): pl.pallas_call(functools.partial(back_columns_kernel, min(512, tokens), c...  72.6 us
    pallas_call x2, Pallas kernels, expert_acts(): pl.pallas_call(functools.partial(expert_kernel, min(512, tokens), len(aft...  62.3 us
    pallas_call x2, Pallas kernels, back_rows(): pl.pallas_call(functools.partial(back_rows_kernel, min(512, tokens), coun...  54.6 us
    pallas_call x12, Pallas kernels, stage(): pl.pallas_call(functools.partial(stage_kernel, len(terms), parts, len(pas...  48.5 us
    pallas_call x2, Pallas kernels, branch(): pl.pallas_call(functools.partial(branch_kernel, len(pieces), len(after)),...  37.6 us
  transfers between devices with their start and end apart: 75, of which 46 were waited for; matrix products, arithmetic and copies ran while one was open for 6% of the time, Pallas kernels for 39%

profile of v5, /device:TPU:0, one launch (start us, length us, event | category | flops | bytes accessed | tf_op | source)
XLA Modules:
  0.0 1292.9 jit_solution(14006486052178258491)
XLA Ops:
  10.4 13.7 %project.1 = (bf16[2048,2048]{1,0:T(8,128)(2,1)}, f32[2048,256]{1,0:T(8,128)}, f32[2048,256]{1,0:T(8,128)}, bf16[2048,256]{1,0:T(8,128)(2,1)}, f32[8,2048]{1,0:T(8,128)}) custom-call(bf16[2048,2048]{1,0:T(8,128)(2,1)} %refs_16_.1, bf16[1,2048]{1,0:T(2,128)(2,1)} %reshape.153.gain_ref.refs_21_, bf16[2048,256]{1,0:T(8,128)(2,1)} %wq_ref.1, ...), custom_call_target="tpu_custom_call" | custom-call | flops 6442450944 | bytes 16777216 | tf_op jit(solution)/shard_map/project/pallas_call | solution.py:95
  67.7 28.0 %collective-permute-done.4.refs_2_.refs_1_ = f32[1024,256]{1,0:T(8,128)S(1)} collective-permute-done((f32[1024,256]{1,0:T(8,128)}, f32[1024,256]{1,0:T(8,128)S(1)}, u32[]{:S(2)}, u32[]{:S(2)}) %collective-permute-start.4) | collective-permute-done | bytes 1048608 | tf_op jit(solution)/shard_map/ppermute | solution.py:1085
  112.6 16.1 %low_grads.2.refs_0_.low_ref = f32[1024,2048]{1,0:T(8,128)} custom-call(bf16[2048,2048]{1,0:T(8,128)(2,1)} %refs_15_.1, bf16[16,2048,128]{2,1,0:T(8,128)(2,1)} %refs_1_.5, f32[1024,256]{1,0:T(8,128)} %get-tuple-element.143.refs_0_.refs_1_.refs_2_), custom_call_target="tpu_custom_call" | custom-call | flops 34359738368 | bytes 16777216 | tf_op jit(solution)/shard_map/low_grads/pallas_call | solution.py:405
  128.7 15.4 %low_grads.3.refs_2_.low_ref = f32[1024,2048]{1,0:T(8,128)} custom-call(bf16[2048,2048]{1,0:T(8,128)(2,1)} %refs_15_.1, bf16[16,2048,128]{2,1,0:T(8,128)(2,1)} %refs_1_.5, f32[1024,2048]{1,0:T(8,128)} %low_grads.2.refs_0_.low_ref), custom_call_target="tpu_custom_call" | custom-call | flops 1024 | bytes 1024 | tf_op jit(solution)/shard_map/low_grads/pallas_call | solution.py:405
  144.1 14.4 %collective-permute-done.6.refs_0_ = f32[1024,256]{1,0:T(8,128)S(1)} collective-permute-done((f32[1024,256]{1,0:T(8,128)S(1)}, f32[1024,256]{1,0:T(8,128)S(1)}, u32[]{:S(2)}, u32[]{:S(2)}) %collective-permute-start.6) | collective-permute-done | bytes 1048608 | tf_op jit(solution)/shard_map/ppermute | solution.py:1085
  161.2 24.7 %collective-permute-done.8.refs_0_ = f32[1024,256]{1,0:T(8,128)S(1)} collective-permute-done((f32[1024,256]{1,0:T(8,128)}, f32[1024,256]{1,0:T(8,128)S(1)}, u32[]{:S(2)}, u32[]{:S(2)}) %collective-permute-start.8) | collective-permute-done | bytes 1048608 | tf_op jit(solution)/shard_map/ppermute | solution.py:1085
  195.8 16.6 %collective-permute-done.9.refs_7_.refs_2_ = f32[1024,256]{1,0:T(8,128)S(1)} collective-permute-done((f32[1024,256]{1,0:T(8,128)}, f32[1024,256]{1,0:T(8,128)S(1)}, u32[]{:S(2)}, u32[]{:S(2)}) %collective-permute-start.9) | collective-permute-done | bytes 1048608 | tf_op jit(solution)/shard_map/ppermute | solution.py:1085
  231.6 18.8 %branch.2 = (f32[1024,2048]{1,0:T(8,128)}, bf16[1024,2048]{1,0:T(8,128)(2,1)}, f32[1024,16]{1,0:T(8,128)}, f32[1024,16]{1,0:T(8,128)}, bf16[1024,2048]{1,0:T(8,128)(2,1)}) custom-call(f32[1024,256]{1,0:T(8,128)} %get-tuple-element.142.refs_0_, f32[1024,256]{1,0:T(8,128)} %copy-done.57, f32[1024,256]{1,0:T(8,128)} %get-tuple-element.143.refs_0_.refs_1_.refs_2_, ...), custom_call_target="tpu_custom_call" | custom-call | flops 8589934592 | bytes 33554432 | tf_op jit(solution)/shard_map/branch/pallas_call | solution.py:731
  262.2 31.1 %expert_acts.2 = (bf16[1024,2048]{1,0:T(8,128)(2,1)}, bf16[1024,2048]{1,0:T(8,128)(2,1)}, bf16[1024,2048]{1,0:T(8,128)(2,1)}, f32[1024,128]{1,0:T(8,128)}) custom-call(bf16[1024,2048]{1,0:T(8,128)(2,1)} %get-tuple-element.146.mixed_ref.refs_0_.refs_13_, f32[1024,2048]{1,0:T(8,128)} %low_grads.2.refs_0_.low_ref, f32[1024,16]{1,0:T(8,128)} %get-tuple-element.147.gates_ref, ...), custom_call_target="tpu_custom_call" | custom-call | flops 17179869184 | bytes 25165824 | tf_op jit(solution)/shard_map/expert_acts/pallas_call | solution.py:469
  296.1 27.5 %back_rows.2 = (f32[2,128,2176]{2,1,0:T(8,128)}, f32[2,128,2176]{2,1,0:T(8,128)}, f32[2,128,2176]{2,1,0:T(8,128)}, f32[2,128,2176]{2,1,0:T(8,128)}) custom-call(s32[8]{0:T(128)} %gather_fusion, bf16[1024,2048]{1,0:T(8,128)(2,1)} %get-tuple-element.152.refs_0_.refs_3_, bf16[1024,2048]{1,0:T(8,128)(2,1)} %get-tuple-element.153.refs_1_.refs_4_, ...), custom_call_target="tpu_custom_call" | custom-call | flops 17179869184 | bytes 25165824 | tf_op jit(solution)/shard_map/back_rows/pallas_call | solution.py:601
  325.2 18.8 %branch.3 = (f32[1024,2048]{1,0:T(8,128)}, bf16[1024,2048]{1,0:T(8,128)(2,1)}, f32[1024,16]{1,0:T(8,128)}, f32[1024,16]{1,0:T(8,128)}, bf16[1024,2048]{1,0:T(8,128)(2,1)}) custom-call(f32[1024,256]{1,0:T(8,128)} %get-tuple-element.150.refs_0_, f32[1024,256]{1,0:T(8,128)} %copy-done.49, f32[1024,256]{1,0:T(8,128)} %get-tuple-element.151.refs_2_, ...), custom_call_target="tpu_custom_call" | custom-call | flops 8589934592 | bytes 33554432 | tf_op jit(solution)/shard_map/branch/pallas_call | solution.py:731
  344.0 31.2 %expert_acts.3 = (bf16[1024,2048]{1,0:T(8,128)(2,1)}, bf16[1024,2048]{1,0:T(8,128)(2,1)}, bf16[1024,2048]{1,0:T(8,128)(2,1)}, f32[1024,128]{1,0:T(8,128)}) custom-call(bf16[1024,2048]{1,0:T(8,128)(2,1)} %get-tuple-element.156.mixed_ref.refs_1_.refs_19_, f32[1024,2048]{1,0:T(8,128)} %low_grads.3.refs_2_.low_ref, f32[1024,16]{1,0:T(8,128)} %get-tuple-element.157.gates_ref, ...), custom_call_target="tpu_custom_call" | custom-call | flops 1024 | bytes 1024 | tf_op jit(solution)/shard_map/expert_acts/pallas_call | solution.py:469
  384.1 27.1 %back_rows.3 = (f32[2,128,2176]{2,1,0:T(8,128)}, f32[2,128,2176]{2,1,0:T(8,128)}, f32[2,128,2176]{2,1,0:T(8,128)}, f32[2,128,2176]{2,1,0:T(8,128)}) custom-call(s32[8]{0:T(128)} %gather_fusion, bf16[1024,2048]{1,0:T(8,128)(2,1)} %get-tuple-element.158.refs_0_.refs_5_, bf16[1024,2048]{1,0:T(8,128)(2,1)} %get-tuple-element.159.refs_1_.refs_6_, ...), custom_call_target="tpu_custom_call" | custom-call | flops 17179869184 | bytes 25165824 | tf_op jit(solution)/shard_map/back_rows/pallas_call | solution.py:601
  411.2 19.2 %collective-permute-done.18.refs_1_ = f32[2,128,2176]{2,1,0:T(8,128)S(1)} collective-permute-done((f32[2,128,2176]{2,1,0:T(8,128)}, f32[2,128,2176]{2,1,0:T(8,128)S(1)}, u32[]{:S(2)}, u32[]{:S(2)}) %collective-permute-start.18) | collective-permute-done | bytes 2228256 | tf_op jit(solution)/shard_map/ppermute | solution.py:1085
  438.1 31.2 %expert_grads.2.refs_2_ = f32[16,2048,128]{2,1,0:T(8,128)} custom-call(bf16[2048,2048]{1,0:T(8,128)(2,1)} %refs_15_.1, bf16[2048,2048]{1,0:T(8,128)(2,1)} %refs_15_.1, f32[1,128,2176]{2,1,0:T(8,128)} %get-tuple-element.170.refs_2_, bf16[1024,2048]{1,0:T(8,128)(2,1)} %get-tuple-element.148.refs_1_.refs_3_.refs_0_, ...), custom_call_target="tpu_custom_call" | custom-call | flops 17179869184 | bytes 25165824 | tf_op jit(solution)/shard_map/expert_grads/pallas_call | solution.py:688
  469.3 17.6 %collective-permute-done.21.refs_4_.refs_3_ = f32[1,128,2176]{2,1,0:T(8,128)S(1)} collective-permute-done((f32[1,128,2176]{2,1,0:T(8,128)}, f32[1,128,2176]{2,1,0:T(8,128)S(1)}, u32[]{:S(2)}, u32[]{:S(2)}) %collective-permute-start.21) | collective-permute-done | bytes 1114144 | tf_op jit(solution)/shard_map/ppermute | solution.py:1085
  493.9 22.3 %back_columns.4 = (f32[2,1024,256]{2,1,0:T(8,128)}, f32[2,1024,256]{2,1,0:T(8,128)}, f32[2,1024,256]{2,1,0:T(8,128)}, f32[2,1024,256]{2,1,0:T(8,128)}) custom-call(s32[8]{0:T(128)} %gather_fusion, s32[1]{0:T(128)} %constant.53.clone.1.rank_ref, bf16[1024,2048]{1,0:T(8,128)(2,1)} %get-tuple-element.148.refs_1_.refs_3_.refs_0_, ...), custom_call_target="tpu_custom_call" | custom-call | flops 8589934592 | bytes 16777216 | tf_op jit(solution)/shard_map/back_columns/pallas_call | solution.py:531
  516.2 26.3 %collective-permute-done.22.refs_1_.refs_5_ = f32[2,128,2176]{2,1,0:T(8,128)S(1)} collective-permute-done((f32[2,128,2176]{2,1,0:T(8,128)}, f32[2,128,2176]{2,1,0:T(8,128)S(1)}, u32[]{:S(2)}, u32[]{:S(2)}) %collective-permute-start.22) | collective-permute-done | bytes 2228256 | tf_op jit(solution)/shard_map/ppermute | solution.py:1085
  550.5 50.1 %expert_grads.3 = (f32[16,2048,128]{2,1,0:T(8,128)}, f32[16,2048,128]{2,1,0:T(8,128)}) custom-call(bf16[1024,2048]{1,0:T(8,128)(2,1)} %get-tuple-element.146.mixed_ref.refs_0_.refs_13_, bf16[1024,2048]{1,0:T(8,128)(2,1)} %get-tuple-element.156.mixed_ref.refs_1_.refs_19_, f32[1,128,2176]{2,1,0:T(8,128)} %get-tuple-element.179.refs_2_, ...), custom_call_target="tpu_custom_call" | custom-call | flops 34359738368 | bytes 50331648 | tf_op jit(solution)/shard_map/expert_grads/pallas_call | solution.py:688
  620.1 23.1 %back_columns.5 = (f32[2,1024,256]{2,1,0:T(8,128)}, f32[2,1024,256]{2,1,0:T(8,128)}, f32[2,1024,256]{2,1,0:T(8,128)}, f32[2,1024,256]{2,1,0:T(8,128)}) custom-call(s32[8]{0:T(128)} %gather_fusion, s32[1]{0:T(128)} %constant.53.clone.1.rank_ref, bf16[1024,2048]{1,0:T(8,128)(2,1)} %get-tuple-element.164.refs_3_.refs_4_.refs_0_, ...), custom_call_target="tpu_custom_call" | custom-call | flops 1024 | bytes 1024 | tf_op jit(solution)/shard_map/back_columns/pallas_call | solution.py:531
  669.1 18.6 %outer.1 = (f32[4,512,256]{2,1,0:T(8,128)}, f32[4,512,256]{2,1,0:T(8,128)}, f32[4,512,256]{2,1,0:T(8,128)}, f32[4,512,256]{2,1,0:T(8,128)}, f32[4,512,256]{2,1,0...) custom-call(s32[4]{0:T(128)} %iota_xor_fusion.table_ref, ...), custom_call_target="tpu_custom_call" | custom-call | flops 2147483648 | bytes 16777216 | tf_op jit(solution)/shard_map/outer/pallas_call | solution.py:940
  738.0 24.8 %attend_back.1 = (f32[2048,256]{1,0:T(8,128)}, f32[2048,256]{1,0:T(8,128)}, bf16[2048,256]{1,0:T(8,128)(2,1)}, f32[8,2048]{1,0:T(8,128)}, f32[16,256]{1,0:T(8,128)}) custom-call(s32[8]{0:T(128)} %copy-done, bf16[2048,256]{1,0:T(8,128)(2,1)} %get-tuple-element.286.q_ref, bf16[2048,256]{1,0:T(8,128)(2,1)} %get-tuple-element.287.k_ref, ...), custom_call_target="tpu_custom_call" | custom-call | flops 5368709120 | bytes 15728640 | tf_op jit(solution)/shard_map/attend_back/pallas_call | solution.py:290
  796.8 80.1 %collective-permute-done.54 = f32[4,512,256]{2,1,0:T(8,128)} collective-permute-done((f32[4,512,256]{2,1,0:T(8,128)S(1)}, f32[4,512,256]{2,1,0:T(8,128)}, u32[]{:S(2)}, u32[]{:S(2)}) %collective-permute-start.54) | collective-permute-done | bytes 2097184 | tf_op jit(solution)/shard_map/ppermute | solution.py:1085
  902.7 13.7 %back_columns.7 = (f32[2,1024,256]{2,1,0:T(8,128)}, f32[2,1024,256]{2,1,0:T(8,128)}, f32[2,1024,256]{2,1,0:T(8,128)}, f32[2,1024,256]{2,1,0:T(8,128)}) custom-call(s32[8]{0:T(128)} %gather_fusion, s32[1]{0:T(128)} %bitcast.6.rank_ref, bf16[1024,256]{1,0:T(8,128)(2,1)} %get-tuple-element.273.refs_0_, bf16[1024,256]{1,0:T(8,128)(2,1)} %get-tuple-element.271.refs_1_, ...), custom_call_target="tpu_custom_call" | custom-call | flops 3221225472 | bytes 33554432 | tf_op jit(solution)/shard_map/back_columns/pallas_call | solution.py:531
  916.4 13.5 %back_columns.6 = (f32[2,1024,256]{2,1,0:T(8,128)}, f32[2,1024,256]{2,1,0:T(8,128)}, f32[2,1024,256]{2,1,0:T(8,128)}, f32[2,1024,256]{2,1,0:T(8,128)}) custom-call(s32[8]{0:T(128)} %gather_fusion, s32[1]{0:T(128)} %bitcast.6.rank_ref, bf16[1024,256]{1,0:T(8,128)(2,1)} %get-tuple-element.274.refs_0_, bf16[1024,256]{1,0:T(8,128)(2,1)} %get-tuple-element.272.refs_1_, ...), custom_call_target="tpu_custom_call" | custom-call | flops 3221225472 | bytes 33554432 | tf_op jit(solution)/shard_map/back_columns/pallas_call | solution.py:531
  961.8 33.7 %collective-permute-done.58 = f32[512,768]{1,0:T(8,128)S(1)} collective-permute-done((f32[512,768]{1,0:T(8,128)S(1)}, f32[512,768]{1,0:T(8,128)S(1)}, u32[]{:S(2)}, u32[]{:S(2)}) %collective-permute-start.58) | collective-permute-done | bytes 1572896 | tf_op jit(solution)/shard_map/ppermute | solution.py:1085
  1014.7 46.2 %collective-permute-done.50.refs_1_ = f32[2,1024,256]{2,1,0:T(8,128)S(1)} collective-permute-done((f32[2,1024,256]{2,1,0:T(8,128)}, f32[2,1024,256]{2,1,0:T(8,128)S(1)}, u32[]{:S(2)}, u32[]{:S(2)}) %collective-permute-start.50) | collective-permute-done | bytes 2097184 | tf_op jit(solution)/shard_map/ppermute | solution.py:1085
  1070.2 44.9 %collective-permute-done.52.refs_4_ = f32[1,1024,256]{2,1,0:T(8,128)S(1)} collective-permute-done((f32[1,1024,256]{2,1,0:T(8,128)}, f32[1,1024,256]{2,1,0:T(8,128)S(1)}, u32[]{:S(2)}, u32[]{:S(2)}) %collective-permute-start.52) | collective-permute-done | bytes 1048608 | tf_op jit(solution)/shard_map/ppermute | solution.py:1085
  1136.2 31.7 %collective-permute-done.55.refs_1_ = f32[2,1024,256]{2,1,0:T(8,128)S(1)} collective-permute-done((f32[2,1024,256]{2,1,0:T(8,128)}, f32[2,1024,256]{2,1,0:T(8,128)S(1)}, u32[]{:S(2)}, u32[]{:S(2)}) %collective-permute-start.55) | collective-permute-done | bytes 2097184 | tf_op jit(solution)/shard_map/ppermute | solution.py:1085
  1184.1 36.8 %collective-permute-done.59 = f32[1,1024,256]{2,1,0:T(8,128)S(1)} collective-permute-done((f32[1,1024,256]{2,1,0:T(8,128)}, f32[1,1024,256]{2,1,0:T(8,128)S(1)}, u32[]{:S(2)}, u32[]{:S(2)}) %collective-permute-start.59) | collective-permute-done | bytes 1048608 | tf_op jit(solution)/shard_map/ppermute | solution.py:1085
  1239.8 17.9 %collective-permute-done.64 = f32[1,12800]{1,0:T(1,128)S(1)} collective-permute-done((f32[1,12800]{1,0:T(1,128)S(1)}, f32[1,12800]{1,0:T(1,128)S(1)}, u32[]{:S(2)}, u32[]{:S(2)}) %collective-permute-start.64) | collective-permute-done | bytes 51232 | tf_op jit(solution)/shard_map/ppermute | solution.py:1085
  1266.8 17.3 %collective-permute-done.67 = f32[1,512,256]{2,1,0:T(8,128)} collective-permute-done((f32[1,512,256]{2,1,0:T(8,128)}, f32[1,512,256]{2,1,0:T(8,128)}, u32[]{:S(2)}, u32[]{:S(2)}) %collective-permute-start.67) | collective-permute-done | bytes 524320 | tf_op jit(solution)/shard_map/ppermute | solution.py:1085
  (436 shorter events, 425.5 us)
Async XLA Ops:
  7.2 100.7 %all-gather.5.cloned.1.call-start = ((), (), s32[]{:S(2)}) async-start(), calls=%async_computation.6 | async-start | bytes 4718592 | tf_op jit(solution)/shard_map/all_gather | solution.py:1284
  9.0 210.7 %all-gather.7.cloned.1.call-start = ((), (), s32[]{:S(2)}) async-start(), calls=%async_computation.7 | async-start | bytes 20971520 | tf_op jit(solution)/shard_map/all_gather | solution.py:1326
  57.0 50.0 %collective-permute-start.3 = (f32[1024,256]{1,0:T(8,128)}, f32[1024,256]{1,0:T(8,128)S(1)}, u32[]{:S(2)}, u32[]{:S(2)}) collective-permute-start(f32[1024,256]{1,0:T(8,128)} %get-tuple-element.140.refs_0_.refs_1_), channel_id=1, source_target_pairs={{0,2},{1,3},{2,0},{3,1},{4,6},{5,7},{6,4},{7,5},{8,10},{9,11},{10,... | collective-permute-start | bytes 3145736 | tf_op jit(solution)/shard_map/ppermute | solution.py:1085
  108.0 1178.0 %reduce-scatter.8.cloned.1.call-start = ((), (), s32[]{:S(2)}) async-start(), calls=%async_computation.5 | async-start | bytes 20971520 | tf_op jit(solution)/shard_map/reduce_scatter | solution.py:1492
  109.1 49.4 %collective-permute-start.5 = (f32[1024,256]{1,0:T(8,128)S(1)}, f32[1024,256]{1,0:T(8,128)S(1)}, u32[]{:S(2)}, u32[]{:S(2)}) collective-permute-start(f32[1024,256]{1,0:T(8,128)S(1)} %copy-done.38), channel_id=1, source_target_pairs={{0,1},{1,0},{2,3},{3,2},{4,5},{5,4},{6,7},{7,6},{8,9},{9,8},{10,11... | collective-permute-start | bytes 3145736 | tf_op jit(solution)/shard_map/ppermute | solution.py:1085
  110.6 48.0 %collective-permute-start.6 = (f32[1024,256]{1,0:T(8,128)S(1)}, f32[1024,256]{1,0:T(8,128)S(1)}, u32[]{:S(2)}, u32[]{:S(2)}) collective-permute-start(f32[1024,256]{1,0:T(8,128)S(1)} %copy-done.59), channel_id=1, source_target_pairs={{0,4},{1,5},{2,6},{3,7},{4,0},{5,1},{6,2},{7,3},{8,12},{9,13},{10,... | collective-permute-start | bytes 3145736 | tf_op jit(solution)/shard_map/ppermute | solution.py:1085
  213.4 47.1 %collective-permute-start.13 = (f32[1024,256]{1,0:T(8,128)}, f32[1024,256]{1,0:T(8,128)}, u32[]{:S(2)}, u32[]{:S(2)}) collective-permute-start(f32[1024,256]{1,0:T(8,128)} %get-tuple-element.150.refs_0_), channel_id=1, source_target_pairs={{0,4},{1,5},{2,6},{3,7},{4,0},{5,1},{6,2},{7,3},{8,12},{9,13},{10,... | collective-permute-start | bytes 3145736 | tf_op jit(solution)/shard_map/ppermute | solution.py:1085
  324.6 50.6 %collective-permute-start.17 = (f32[2,128,2176]{2,1,0:T(8,128)}, f32[2,128,2176]{2,1,0:T(8,128)S(1)}, u32[]{:S(2)}, u32[]{:S(2)}) collective-permute-start(f32[2,128,2176]{2,1,0:T(8,128)} %tie.16), channel_id=1, source_target_pairs={{0,1},{1,0},{2,3},{3,2},{4,5},{5,4},{6,7},{7,6},{8,9},{9,8},{10,11... | collective-permute-start | bytes 6684680 | tf_op jit(solution)/shard_map/ppermute | solution.py:1085
  380.8 49.6 %collective-permute-start.18 = (f32[2,128,2176]{2,1,0:T(8,128)}, f32[2,128,2176]{2,1,0:T(8,128)S(1)}, u32[]{:S(2)}, u32[]{:S(2)}) collective-permute-start(f32[2,128,2176]{2,1,0:T(8,128)} %get-tuple-element.167), channel_id=1, source_target_pairs={{0,1},{1,0},{2,3},{3,2},{4,5},{5,4},{6,7},{7,6},{8,9},{9,8},{10,11... | collective-permute-start | bytes 6684680 | tf_op jit(solution)/shard_map/ppermute | solution.py:1085
  382.2 49.3 %collective-permute-start.19 = (f32[2,128,2176]{2,1,0:T(8,128)}, f32[2,128,2176]{2,1,0:T(8,128)S(1)}, u32[]{:S(2)}, u32[]{:S(2)}) collective-permute-start(f32[2,128,2176]{2,1,0:T(8,128)} %get-tuple-element.165.refs_5_), channel_id=1, source_target_pairs={{0,2},{1,3},{2,0},{3,1},{4,6},{5,7},{6,4},{7,5},{8,10},{9,11},{10,... | collective-permute-start | bytes 6684680 | tf_op jit(solution)/shard_map/ppermute | solution.py:1085
  436.7 50.2 %collective-permute-start.20 = (f32[2,128,2176]{2,1,0:T(8,128)}, f32[2,128,2176]{2,1,0:T(8,128)S(1)}, u32[]{:S(2)}, u32[]{:S(2)}) collective-permute-start(f32[2,128,2176]{2,1,0:T(8,128)} %get-tuple-element.169), channel_id=1, source_target_pairs={{0,1},{1,0},{2,3},{3,2},{4,5},{5,4},{6,7},{7,6},{8,9},{9,8},{10,11... | collective-permute-start | bytes 6684680 | tf_op jit(solution)/shard_map/ppermute | solution.py:1085
  437.7 49.2 %collective-permute-start.21 = (f32[1,128,2176]{2,1,0:T(8,128)}, f32[1,128,2176]{2,1,0:T(8,128)S(1)}, u32[]{:S(2)}, u32[]{:S(2)}) collective-permute-start(f32[1,128,2176]{2,1,0:T(8,128)} %get-tuple-element.170.refs_2_), channel_id=1, source_target_pairs={{0,4},{1,5},{2,6},{3,7},{4,0},{5,1},{6,2},{7,3},{8,12},{9,13},{10,... | collective-permute-start | bytes 3342344 | tf_op jit(solution)/shard_map/ppermute | solution.py:1085
  492.9 793.1 %reduce-scatter.4.cloned.1.call-start = ((), (), s32[]{:S(2)}) async-start(), calls=%async_computation.3 | async-start | bytes 20971520 | tf_op jit(solution)/shard_map/reduce_scatter | solution.py:1492
  493.0 49.5 %collective-permute-start.22 = (f32[2,128,2176]{2,1,0:T(8,128)}, f32[2,128,2176]{2,1,0:T(8,128)S(1)}, u32[]{:S(2)}, u32[]{:S(2)}) collective-permute-start(f32[2,128,2176]{2,1,0:T(8,128)} %get-tuple-element.176), channel_id=1, source_target_pairs={{0,1},{1,0},{2,3},{3,2},{4,5},{5,4},{6,7},{7,6},{8,9},{9,8},{10,11... | collective-permute-start | bytes 6684680 | tf_op jit(solution)/shard_map/ppermute | solution.py:1085
  493.9 49.2 %collective-permute-start.23 = (f32[2,128,2176]{2,1,0:T(8,128)}, f32[2,128,2176]{2,1,0:T(8,128)S(1)}, u32[]{:S(2)}, u32[]{:S(2)}) collective-permute-start(f32[2,128,2176]{2,1,0:T(8,128)} %get-tuple-element.172.refs_2_), channel_id=1, source_target_pairs={{0,2},{1,3},{2,0},{3,1},{4,6},{5,7},{6,4},{7,5},{8,10},{9,11},{10,... | collective-permute-start | bytes 6684680 | tf_op jit(solution)/shard_map/ppermute | solution.py:1085
  548.4 52.3 %collective-permute-start.25 = (f32[1,128,2176]{2,1,0:T(8,128)}, f32[1,128,2176]{2,1,0:T(8,128)S(1)}, u32[]{:S(2)}, u32[]{:S(2)}) collective-permute-start(f32[1,128,2176]{2,1,0:T(8,128)} %get-tuple-element.179.refs_2_), channel_id=1, source_target_pairs={{0,4},{1,5},{2,6},{3,7},{4,0},{5,1},{6,2},{7,3},{8,12},{9,13},{10,... | collective-permute-start | bytes 3342344 | tf_op jit(solution)/shard_map/ppermute | solution.py:1085
  549.3 51.3 %collective-permute-start.24 = (f32[2,1024,256]{2,1,0:T(8,128)}, f32[2,1024,256]{2,1,0:T(8,128)S(1)}, u32[]{:S(2)}, u32[]{:S(2)}) collective-permute-start(f32[2,1024,256]{2,1,0:T(8,128)} %get-tuple-element.178), channel_id=1, source_target_pairs={{0,1},{1,0},{2,3},{3,2},{4,5},{5,4},{6,7},{7,6},{8,9},{9,8},{10,11... | collective-permute-start | bytes 6291464 | tf_op jit(solution)/shard_map/ppermute | solution.py:1085
  606.6 679.4 %reduce-scatter.6.cloned.1.call-start = ((), (), s32[]{:S(2)}) async-start(), calls=%async_computation.4 | async-start | bytes 20971520 | tf_op jit(solution)/shard_map/reduce_scatter | solution.py:1492
  732.2 64.6 %collective-permute-start.37 = (f32[4,512,256]{2,1,0:T(8,128)}, f32[4,512,256]{2,1,0:T(8,128)}, u32[]{:S(2)}, u32[]{:S(2)}) collective-permute-start(f32[4,512,256]{2,1,0:T(8,128)} %get-tuple-element.213), channel_id=1, source_target_pairs={{0,8},{8,0},{16,24},{24,16},{1,9},{9,1},{17,25},{25,17},{2,10},{10... | collective-permute-start | bytes 6291464 | tf_op jit(solution)/shard_map/ppermute | solution.py:1085
  732.2 54.9 %collective-permute-start.39 = (f32[4,512,256]{2,1,0:T(8,128)}, f32[4,512,256]{2,1,0:T(8,128)}, u32[]{:S(2)}, u32[]{:S(2)}) collective-permute-start(f32[4,512,256]{2,1,0:T(8,128)} %get-tuple-element.216), channel_id=1, source_target_pairs={{0,8},{8,0},{16,24},{24,16},{1,9},{9,1},{17,25},{25,17},{2,10},{10... | collective-permute-start | bytes 6291464 | tf_op jit(solution)/shard_map/ppermute | solution.py:1085
  733.1 57.6 %collective-permute-start.57 = (f32[4,512,256]{2,1,0:T(8,128)S(1)}, f32[4,512,256]{2,1,0:T(8,128)}, u32[]{:S(2)}, u32[]{:S(2)}) collective-permute-start(f32[4,512,256]{2,1,0:T(8,128)S(1)} %add.205.refs_7_), channel_id=1, source_target_pairs={{0,16},{8,24},{16,0},{24,8},{1,17},{9,25},{17,1},{25,9},{2,18},{10... | collective-permute-start | bytes 6291464 | tf_op jit(solution)/shard_map/ppermute | solution.py:1085
  736.7 140.3 %collective-permute-start.54 = (f32[4,512,256]{2,1,0:T(8,128)S(1)}, f32[4,512,256]{2,1,0:T(8,128)}, u32[]{:S(2)}, u32[]{:S(2)}) collective-permute-start(f32[4,512,256]{2,1,0:T(8,128)S(1)} %add.203.refs_5_), channel_id=1, source_target_pairs={{0,16},{8,24},{16,0},{24,8},{1,17},{9,25},{17,1},{25,9},{2,18},{10... | collective-permute-start | bytes 6291464 | tf_op jit(solution)/shard_map/ppermute | solution.py:1085
  786.1 95.5 %collective-permute-start.29 = (f32[2,1024,256]{2,1,0:T(8,128)}, f32[2,1024,256]{2,1,0:T(8,128)}, u32[]{:S(2)}, u32[]{:S(2)}) collective-permute-start(f32[2,1024,256]{2,1,0:T(8,128)} %get-tuple-element.193), channel_id=1, source_target_pairs={{0,1},{1,0},{2,3},{3,2},{4,5},{5,4},{6,7},{7,6},{8,9},{9,8},{10,11... | collective-permute-start | bytes 6291464 | tf_op jit(solution)/shard_map/ppermute | solution.py:1085
  787.2 94.5 %collective-permute-start.28 = (f32[1,1024,256]{2,1,0:T(8,128)}, f32[1,1024,256]{2,1,0:T(8,128)S(1)}, u32[]{:S(2)}, u32[]{:S(2)}) collective-permute-start(f32[1,1024,256]{2,1,0:T(8,128)} %get-tuple-element.190), channel_id=1, source_target_pairs={{0,4},{1,5},{2,6},{3,7},{4,0},{5,1},{6,2},{7,3},{8,12},{9,13},{10,... | collective-permute-start | bytes 3145736 | tf_op jit(solution)/shard_map/ppermute | solution.py:1085
  886.8 46.9 %collective-permute-start.44 = (f32[2,1024,256]{2,1,0:T(8,128)}, f32[2,1024,256]{2,1,0:T(8,128)S(1)}, u32[]{:S(2)}, u32[]{:S(2)}) collective-permute-start(f32[2,1024,256]{2,1,0:T(8,128)} %get-tuple-element.222), channel_id=1, source_target_pairs={{0,1},{1,0},{2,3},{3,2},{4,5},{5,4},{6,7},{7,6},{8,9},{9,8},{10,11... | collective-permute-start | bytes 6291464 | tf_op jit(solution)/shard_map/ppermute | solution.py:1085
  953.6 54.3 %collective-permute-start.47 = (f32[2,1024,256]{2,1,0:T(8,128)S(1)}, f32[2,1024,256]{2,1,0:T(8,128)S(1)}, u32[]{:S(2)}, u32[]{:S(2)}) collective-permute-start(f32[2,1024,256]{2,1,0:T(8,128)S(1)} %copy-done.46), channel_id=1, source_target_pairs={{0,1},{1,0},{2,3},{3,2},{4,5},{5,4},{6,7},{7,6},{8,9},{9,8},{10,11... | collective-permute-start | bytes 6291464 | tf_op jit(solution)/shard_map/ppermute | solution.py:1085
  959.6 48.3 %collective-permute-start.46 = (f32[1,1024,256]{2,1,0:T(8,128)S(1)}, f32[1,1024,256]{2,1,0:T(8,128)S(1)}, u32[]{:S(2)}, u32[]{:S(2)}) collective-permute-start(f32[1,1024,256]{2,1,0:T(8,128)S(1)} %copy-done.52), channel_id=1, source_target_pairs={{0,4},{1,5},{2,6},{3,7},{4,0},{5,1},{6,2},{7,3},{8,12},{9,13},{10,... | collective-permute-start | bytes 3145736 | tf_op jit(solution)/shard_map/ppermute | solution.py:1085
  1013.8 47.1 %collective-permute-start.50 = (f32[2,1024,256]{2,1,0:T(8,128)}, f32[2,1024,256]{2,1,0:T(8,128)S(1)}, u32[]{:S(2)}, u32[]{:S(2)}) collective-permute-start(f32[2,1024,256]{2,1,0:T(8,128)} %get-tuple-element.241), channel_id=1, source_target_pairs={{0,1},{1,0},{2,3},{3,2},{4,5},{5,4},{6,7},{7,6},{8,9},{9,8},{10,11... | collective-permute-start | bytes 6291464 | tf_op jit(solution)/shard_map/ppermute | solution.py:1085
  1066.6 48.5 %collective-permute-start.53 = (f32[2,1024,256]{2,1,0:T(8,128)}, f32[2,1024,256]{2,1,0:T(8,128)S(1)}, u32[]{:S(2)}, u32[]{:S(2)}) collective-permute-start(f32[2,1024,256]{2,1,0:T(8,128)} %get-tuple-element.246), channel_id=1, source_target_pairs={{0,1},{1,0},{2,3},{3,2},{4,5},{5,4},{6,7},{7,6},{8,9},{9,8},{10,11... | collective-permute-start | bytes 6291464 | tf_op jit(solution)/shard_map/ppermute | solution.py:1085
  1067.7 47.5 %collective-permute-start.52 = (f32[1,1024,256]{2,1,0:T(8,128)}, f32[1,1024,256]{2,1,0:T(8,128)S(1)}, u32[]{:S(2)}, u32[]{:S(2)}) collective-permute-start(f32[1,1024,256]{2,1,0:T(8,128)} %get-tuple-element.244), channel_id=1, source_target_pairs={{0,4},{1,5},{2,6},{3,7},{4,0},{5,1},{6,2},{7,3},{8,12},{9,13},{10,... | collective-permute-start | bytes 3145736 | tf_op jit(solution)/shard_map/ppermute | solution.py:1085
  1173.4 47.5 %collective-permute-start.59 = (f32[1,1024,256]{2,1,0:T(8,128)}, f32[1,1024,256]{2,1,0:T(8,128)S(1)}, u32[]{:S(2)}, u32[]{:S(2)}) collective-permute-start(f32[1,1024,256]{2,1,0:T(8,128)} %get-tuple-element.250), channel_id=1, source_target_pairs={{0,4},{1,5},{2,6},{3,7},{4,0},{5,1},{6,2},{7,3},{8,12},{9,13},{10,... | collective-permute-start | bytes 3145736 | tf_op jit(solution)/shard_map/ppermute | solution.py:1085
  1182.7 50.6 %collective-permute-start.65 = (f32[4,512,256]{2,1,0:T(8,128)}, f32[4,512,256]{2,1,0:T(8,128)}, u32[]{:S(2)}, u32[]{:S(2)}) collective-permute-start(f32[4,512,256]{2,1,0:T(8,128)} %get-tuple-element.253), channel_id=1, source_target_pairs={{0,1},{1,0},{2,3},{3,2},{4,5},{5,4},{6,7},{7,6},{8,9},{9,8},{10,11... | collective-permute-start | bytes 6291464 | tf_op jit(solution)/shard_map/ppermute | solution.py:1085
  (127 other events, 1753.2 us)
Sparse Core Ops, SparseCore 0:
  10.1 97.2 all-gather.4
  109.0 105.9 all-gather.6
  493.0 124.3 reduce-scatter.7
  620.6 135.6 reduce-scatter.3
  759.3 167.2 reduce-scatter.5

commit v6 on v4

--- a/solution.py
+++ b/solution.py
@@ -1384,10 +1384,10 @@
 
     if staged:
         acts = [forward(0, ())]
-        (far,) = tie((far,), (middle[0], odd[0], odd[1]))
+        (far,) = tie((far,), (middle[0], odd[0]))
         both = swap(far, "tensor", 2)
         odd.append(swap(far, "tensor", 1))
-        (both,) = tie((both,), (acts[0][0], odd[2]))
+        (both,) = tie((both,), (acts[0][0], odd[1], odd[2]))
         odd.append(swap(both, "tensor", 1))
         even = [again, near, far, both]
         pieces.append([item for pair in zip(even, odd) for item in pair])

time: 1180 us -> 1180 us (level)
    unnamed x156 -> x158, local copies, waits for them, and re-layouts: 36.9 us -> 37.3 us
where the time goes in v6:
time: 1180 us; the launch traced here: 1170 us
  Pallas kernels  514 us (44%)
  waiting for transfers between devices  425 us (36%)
  starting transfers between devices  97.3 us (8%)
  other arithmetic  64 us (5%)
  local copies, waits for them, and re-layouts  52.6 us (4%)
  between operations  15 us (1%)
    ppermute x70, waiting for transfers between devices, swap(): return lax.ppermute(value, axis, [(i, i ^ step) for i in range(count)])  424 us
    ppermute x70, starting transfers between devices, swap(): return lax.ppermute(value, axis, [(i, i ^ step) for i in range(count)])  96.2 us
    pallas_call x2, Pallas kernels, expert_grads(): pl.pallas_call(functools.partial(grads_kernel, min(512, width), chunks, l...  81.3 us
    pallas_call x4, Pallas kernels, back_columns(): pl.pallas_call(functools.partial(back_columns_kernel, min(512, tokens), c...  71.7 us
    pallas_call x2, Pallas kernels, expert_acts(): pl.pallas_call(functools.partial(expert_kernel, min(512, tokens), len(aft...  62.3 us
    pallas_call x2, Pallas kernels, back_rows(): pl.pallas_call(functools.partial(back_rows_kernel, min(512, tokens), coun...  54.5 us
    pallas_call x12, Pallas kernels, stage(): pl.pallas_call(functools.partial(stage_kernel, len(terms), parts, len(pas...  48.4 us
    pallas_call x2, Pallas kernels, branch(): pl.pallas_call(functools.partial(branch_kernel, len(pieces), len(after)),...  37.5 us
  transfers between devices with their start and end apart: 75, of which 37 were waited for; matrix products, arithmetic and copies ran while one was open for 7% of the time, Pallas kernels for 43%

profile of v6, /device:TPU:0, one launch (start us, length us, event | category | flops | bytes accessed | tf_op | source)
XLA Modules:
  0.0 1167.8 jit_solution(14832628443803168857)
XLA Ops:
  10.4 13.7 %project.1 = (bf16[2048,2048]{1,0:T(8,128)(2,1)}, f32[2048,256]{1,0:T(8,128)}, f32[2048,256]{1,0:T(8,128)}, bf16[2048,256]{1,0:T(8,128)(2,1)}, f32[8,2048]{1,0:T(8,128)}) custom-call(bf16[2048,2048]{1,0:T(8,128)(2,1)} %refs_16_.1, bf16[1,2048]{1,0:T(2,128)(2,1)} %reshape.153.gain_ref.refs_21_, bf16[2048,256]{1,0:T(8,128)(2,1)} %wq_ref.1, ...), custom_call_target="tpu_custom_call" | custom-call | flops 6442450944 | bytes 16777216 | tf_op jit(solution)/shard_map/project/pallas_call | solution.py:95
  67.8 27.9 %collective-permute-done.4.refs_2_.refs_1_ = f32[1024,256]{1,0:T(8,128)S(1)} collective-permute-done((f32[1024,256]{1,0:T(8,128)}, f32[1024,256]{1,0:T(8,128)S(1)}, u32[]{:S(2)}, u32[]{:S(2)}) %collective-permute-start.4) | collective-permute-done | bytes 1048608 | tf_op jit(solution)/shard_map/ppermute | solution.py:1085
  112.7 16.2 %low_grads.2.refs_0_.low_ref = f32[1024,2048]{1,0:T(8,128)} custom-call(bf16[2048,2048]{1,0:T(8,128)(2,1)} %refs_15_.1, bf16[16,2048,128]{2,1,0:T(8,128)(2,1)} %refs_1_.5, f32[1024,256]{1,0:T(8,128)} %get-tuple-element.143.refs_0_.refs_1_.refs_2_), custom_call_target="tpu_custom_call" | custom-call | flops 34359738368 | bytes 16777216 | tf_op jit(solution)/shard_map/low_grads/pallas_call | solution.py:405
  128.8 15.3 %low_grads.3.refs_2_.low_ref = f32[1024,2048]{1,0:T(8,128)} custom-call(bf16[2048,2048]{1,0:T(8,128)(2,1)} %refs_15_.1, bf16[16,2048,128]{2,1,0:T(8,128)(2,1)} %refs_1_.5, f32[1024,2048]{1,0:T(8,128)} %low_grads.2.refs_0_.low_ref), custom_call_target="tpu_custom_call" | custom-call | flops 1024 | bytes 1024 | tf_op jit(solution)/shard_map/low_grads/pallas_call | solution.py:405
  144.1 14.5 %collective-permute-done.6.refs_0_ = f32[1024,256]{1,0:T(8,128)S(1)} collective-permute-done((f32[1024,256]{1,0:T(8,128)S(1)}, f32[1024,256]{1,0:T(8,128)S(1)}, u32[]{:S(2)}, u32[]{:S(2)}) %collective-permute-start.6) | collective-permute-done | bytes 1048608 | tf_op jit(solution)/shard_map/ppermute | solution.py:1085
  161.2 24.7 %collective-permute-done.8.refs_0_ = f32[1024,256]{1,0:T(8,128)S(1)} collective-permute-done((f32[1024,256]{1,0:T(8,128)}, f32[1024,256]{1,0:T(8,128)S(1)}, u32[]{:S(2)}, u32[]{:S(2)}) %collective-permute-start.8) | collective-permute-done | bytes 1048608 | tf_op jit(solution)/shard_map/ppermute | solution.py:1085
  195.9 16.6 %collective-permute-done.9.refs_7_.refs_2_ = f32[1024,256]{1,0:T(8,128)S(1)} collective-permute-done((f32[1024,256]{1,0:T(8,128)}, f32[1024,256]{1,0:T(8,128)S(1)}, u32[]{:S(2)}, u32[]{:S(2)}) %collective-permute-start.9) | collective-permute-done | bytes 1048608 | tf_op jit(solution)/shard_map/ppermute | solution.py:1085
  231.7 18.8 %branch.2 = (f32[1024,2048]{1,0:T(8,128)}, bf16[1024,2048]{1,0:T(8,128)(2,1)}, f32[1024,16]{1,0:T(8,128)}, f32[1024,16]{1,0:T(8,128)}, bf16[1024,2048]{1,0:T(8,128)(2,1)}) custom-call(f32[1024,256]{1,0:T(8,128)} %get-tuple-element.142.refs_0_, f32[1024,256]{1,0:T(8,128)} %copy-done.49, f32[1024,256]{1,0:T(8,128)} %get-tuple-element.143.refs_0_.refs_1_.refs_2_, ...), custom_call_target="tpu_custom_call" | custom-call | flops 8589934592 | bytes 33554432 | tf_op jit(solution)/shard_map/branch/pallas_call | solution.py:731
  262.2 31.1 %expert_acts.2 = (bf16[1024,2048]{1,0:T(8,128)(2,1)}, bf16[1024,2048]{1,0:T(8,128)(2,1)}, bf16[1024,2048]{1,0:T(8,128)(2,1)}, f32[1024,128]{1,0:T(8,128)}) custom-call(bf16[1024,2048]{1,0:T(8,128)(2,1)} %get-tuple-element.146.mixed_ref.refs_0_.refs_13_, f32[1024,2048]{1,0:T(8,128)} %low_grads.2.refs_0_.low_ref, f32[1024,16]{1,0:T(8,128)} %get-tuple-element.147.gates_ref, ...), custom_call_target="tpu_custom_call" | custom-call | flops 17179869184 | bytes 25165824 | tf_op jit(solution)/shard_map/expert_acts/pallas_call | solution.py:469
  296.4 27.3 %back_rows.2 = (f32[2,128,2176]{2,1,0:T(8,128)}, f32[2,128,2176]{2,1,0:T(8,128)}, f32[2,128,2176]{2,1,0:T(8,128)}, f32[2,128,2176]{2,1,0:T(8,128)}) custom-call(s32[8]{0:T(128)} %gather_fusion, bf16[1024,2048]{1,0:T(8,128)(2,1)} %get-tuple-element.152.refs_0_.refs_3_, bf16[1024,2048]{1,0:T(8,128)(2,1)} %get-tuple-element.153.refs_1_.refs_4_, ...), custom_call_target="tpu_custom_call" | custom-call | flops 17179869184 | bytes 25165824 | tf_op jit(solution)/shard_map/back_rows/pallas_call | solution.py:601
  325.3 18.7 %branch.3 = (f32[1024,2048]{1,0:T(8,128)}, bf16[1024,2048]{1,0:T(8,128)(2,1)}, f32[1024,16]{1,0:T(8,128)}, f32[1024,16]{1,0:T(8,128)}, bf16[1024,2048]{1,0:T(8,128)(2,1)}) custom-call(f32[1024,256]{1,0:T(8,128)} %get-tuple-element.150.refs_0_, f32[1024,256]{1,0:T(8,128)} %copy-done.53, f32[1024,256]{1,0:T(8,128)} %get-tuple-element.151.refs_2_, ...), custom_call_target="tpu_custom_call" | custom-call | flops 8589934592 | bytes 33554432 | tf_op jit(solution)/shard_map/branch/pallas_call | solution.py:731
  344.0 31.2 %expert_acts.3 = (bf16[1024,2048]{1,0:T(8,128)(2,1)}, bf16[1024,2048]{1,0:T(8,128)(2,1)}, bf16[1024,2048]{1,0:T(8,128)(2,1)}, f32[1024,128]{1,0:T(8,128)}) custom-call(bf16[1024,2048]{1,0:T(8,128)(2,1)} %get-tuple-element.156.mixed_ref.refs_1_.refs_19_, f32[1024,2048]{1,0:T(8,128)} %low_grads.3.refs_2_.low_ref, f32[1024,16]{1,0:T(8,128)} %get-tuple-element.157.gates_ref, ...), custom_call_target="tpu_custom_call" | custom-call | flops 1024 | bytes 1024 | tf_op jit(solution)/shard_map/expert_acts/pallas_call | solution.py:469
  384.3 27.1 %back_rows.3 = (f32[2,128,2176]{2,1,0:T(8,128)}, f32[2,128,2176]{2,1,0:T(8,128)}, f32[2,128,2176]{2,1,0:T(8,128)}, f32[2,128,2176]{2,1,0:T(8,128)}) custom-call(s32[8]{0:T(128)} %gather_fusion, bf16[1024,2048]{1,0:T(8,128)(2,1)} %get-tuple-element.158.refs_0_.refs_5_, bf16[1024,2048]{1,0:T(8,128)(2,1)} %get-tuple-element.159.refs_1_.refs_6_, ...), custom_call_target="tpu_custom_call" | custom-call | flops 17179869184 | bytes 25165824 | tf_op jit(solution)/shard_map/back_rows/pallas_call | solution.py:601
  411.4 19.1 %collective-permute-done.18.refs_1_ = f32[2,128,2176]{2,1,0:T(8,128)S(1)} collective-permute-done((f32[2,128,2176]{2,1,0:T(8,128)}, f32[2,128,2176]{2,1,0:T(8,128)S(1)}, u32[]{:S(2)}, u32[]{:S(2)}) %collective-permute-start.18) | collective-permute-done | bytes 2228256 | tf_op jit(solution)/shard_map/ppermute | solution.py:1085
  438.2 31.2 %expert_grads.2.refs_2_ = f32[16,2048,128]{2,1,0:T(8,128)} custom-call(bf16[2048,2048]{1,0:T(8,128)(2,1)} %refs_15_.1, bf16[2048,2048]{1,0:T(8,128)(2,1)} %refs_15_.1, f32[1,128,2176]{2,1,0:T(8,128)} %get-tuple-element.170.refs_2_, bf16[1024,2048]{1,0:T(8,128)(2,1)} %get-tuple-element.148.refs_1_.refs_3_.refs_0_, ...), custom_call_target="tpu_custom_call" | custom-call | flops 17179869184 | bytes 25165824 | tf_op jit(solution)/shard_map/expert_grads/pallas_call | solution.py:688
  469.4 17.8 %collective-permute-done.21.refs_4_.refs_3_ = f32[1,128,2176]{2,1,0:T(8,128)S(1)} collective-permute-done((f32[1,128,2176]{2,1,0:T(8,128)}, f32[1,128,2176]{2,1,0:T(8,128)S(1)}, u32[]{:S(2)}, u32[]{:S(2)}) %collective-permute-start.21) | collective-permute-done | bytes 1114144 | tf_op jit(solution)/shard_map/ppermute | solution.py:1085
  494.2 22.3 %back_columns.4 = (f32[2,1024,256]{2,1,0:T(8,128)}, f32[2,1024,256]{2,1,0:T(8,128)}, f32[2,1024,256]{2,1,0:T(8,128)}, f32[2,1024,256]{2,1,0:T(8,128)}) custom-call(s32[8]{0:T(128)} %gather_fusion, s32[1]{0:T(128)} %constant.53.clone.1.rank_ref, bf16[1024,2048]{1,0:T(8,128)(2,1)} %get-tuple-element.148.refs_1_.refs_3_.refs_0_, ...), custom_call_target="tpu_custom_call" | custom-call | flops 8589934592 | bytes 16777216 | tf_op jit(solution)/shard_map/back_columns/pallas_call | solution.py:531
  516.5 26.5 %collective-permute-done.22.refs_1_.refs_5_ = f32[2,128,2176]{2,1,0:T(8,128)S(1)} collective-permute-done((f32[2,128,2176]{2,1,0:T(8,128)}, f32[2,128,2176]{2,1,0:T(8,128)S(1)}, u32[]{:S(2)}, u32[]{:S(2)}) %collective-permute-start.22) | collective-permute-done | bytes 2228256 | tf_op jit(solution)/shard_map/ppermute | solution.py:1085
  550.9 50.0 %expert_grads.3 = (f32[16,2048,128]{2,1,0:T(8,128)}, f32[16,2048,128]{2,1,0:T(8,128)}) custom-call(bf16[1024,2048]{1,0:T(8,128)(2,1)} %get-tuple-element.146.mixed_ref.refs_0_.refs_13_, bf16[1024,2048]{1,0:T(8,128)(2,1)} %get-tuple-element.156.mixed_ref.refs_1_.refs_19_, f32[1,128,2176]{2,1,0:T(8,128)} %get-tuple-element.179.refs_2_, ...), custom_call_target="tpu_custom_call" | custom-call | flops 34359738368 | bytes 50331648 | tf_op jit(solution)/shard_map/expert_grads/pallas_call | solution.py:688
  623.0 22.2 %back_columns.5 = (f32[2,1024,256]{2,1,0:T(8,128)}, f32[2,1024,256]{2,1,0:T(8,128)}, f32[2,1024,256]{2,1,0:T(8,128)}, f32[2,1024,256]{2,1,0:T(8,128)}) custom-call(s32[8]{0:T(128)} %gather_fusion, s32[1]{0:T(128)} %constant.53.clone.1.rank_ref, bf16[1024,2048]{1,0:T(8,128)(2,1)} %get-tuple-element.164.refs_3_.refs_4_.refs_0_, ...), custom_call_target="tpu_custom_call" | custom-call | flops 1024 | bytes 1024 | tf_op jit(solution)/shard_map/back_columns/pallas_call | solution.py:531
  677.7 18.6 %outer.1 = (f32[4,512,256]{2,1,0:T(8,128)}, f32[4,512,256]{2,1,0:T(8,128)}, f32[4,512,256]{2,1,0:T(8,128)}, f32[4,512,256]{2,1,0:T(8,128)}, f32[4,512,256]{2,1,0...) custom-call(s32[4]{0:T(128)} %iota_xor_fusion.table_ref, ...), custom_call_target="tpu_custom_call" | custom-call | flops 2147483648 | bytes 16777216 | tf_op jit(solution)/shard_map/outer/pallas_call | solution.py:940
  714.4 24.8 %attend_back.1 = (f32[2048,256]{1,0:T(8,128)}, f32[2048,256]{1,0:T(8,128)}, bf16[2048,256]{1,0:T(8,128)(2,1)}, f32[8,2048]{1,0:T(8,128)}, f32[16,256]{1,0:T(8,128)}) custom-call(s32[8]{0:T(128)} %copy-done, bf16[2048,256]{1,0:T(8,128)(2,1)} %get-tuple-element.280.q_ref, bf16[2048,256]{1,0:T(8,128)(2,1)} %get-tuple-element.281.k_ref, ...), custom_call_target="tpu_custom_call" | custom-call | flops 5368709120 | bytes 15728640 | tf_op jit(solution)/shard_map/attend_back/pallas_call | solution.py:290
  750.6 24.9 %collective-permute-start.38 = (f32[8,2048]{1,0:T(8,128)S(1)}, f32[8,2048]{1,0:T(8,128)S(1)}, u32[]{:S(2)}, u32[]{:S(2)}) collective-permute-start(f32[8,2048]{1,0:T(8,128)S(1)} %add.202), channel_id=1, source_target_pairs={{0,2},{1,3},{2,0},{3,1},{4,6},{5,7},{6,4},{7,5},{8,10},{9,11},{10,... | collective-permute-start | bytes 196616 | tf_op jit(solution)/shard_map/ppermute | solution.py:1085
  818.6 13.7 %back_columns.6 = (f32[2,1024,256]{2,1,0:T(8,128)}, f32[2,1024,256]{2,1,0:T(8,128)}, f32[2,1024,256]{2,1,0:T(8,128)}, f32[2,1024,256]{2,1,0:T(8,128)}) custom-call(s32[8]{0:T(128)} %gather_fusion, s32[1]{0:T(128)} %bitcast.6.rank_ref, bf16[1024,256]{1,0:T(8,128)(2,1)} %get-tuple-element.268.refs_0_, bf16[1024,256]{1,0:T(8,128)(2,1)} %get-tuple-element.266.refs_1_, ...), custom_call_target="tpu_custom_call" | custom-call | flops 3221225472 | bytes 33554432 | tf_op jit(solution)/shard_map/back_columns/pallas_call | solution.py:531
  839.7 13.7 %in_grads.1 = (f32[512,768]{1,0:T(8,128)}, f32[512,768]{1,0:T(8,128)}, f32[512,768]{1,0:T(8,128)}, f32[512,768]{1,0:T(8,128)}) custom-call(s32[4]{0:T(128)} %iota_xor_fusion.table_ref, bf16[2048,2048]{1,0:T(8,128)(2,1)} %get-tuple-element.229.left_ref, bf16[2048,256]{1,0:T(8,128)(2,1)} %get-tuple-element.218.refs_0_, ...), custom_call_target="tpu_custom_call" | custom-call | flops 1024 | bytes 1024 | tf_op jit(solution)/shard_map/in_grads/pallas_call | solution.py:996
  853.4 26.6 %collective-permute-done.42.refs_4_ = f32[1,1024,256]{2,1,0:T(8,128)S(1)} collective-permute-done((f32[1,1024,256]{2,1,0:T(8,128)}, f32[1,1024,256]{2,1,0:T(8,128)S(1)}, u32[]{:S(2)}, u32[]{:S(2)}) %collective-permute-start.42) | collective-permute-done | bytes 1048608 | tf_op jit(solution)/shard_map/ppermute | solution.py:1085
  892.8 40.7 %collective-permute-done.44.refs_1_ = f32[2,1024,256]{2,1,0:T(8,128)S(1)} collective-permute-done((f32[2,1024,256]{2,1,0:T(8,128)}, f32[2,1024,256]{2,1,0:T(8,128)S(1)}, u32[]{:S(2)}, u32[]{:S(2)}) %collective-permute-start.44) | collective-permute-done | bytes 2097184 | tf_op jit(solution)/shard_map/ppermute | solution.py:1085
  954.1 35.3 %collective-permute-done.46.refs_4_ = f32[1,1024,256]{2,1,0:T(8,128)S(1)} collective-permute-done((f32[1,1024,256]{2,1,0:T(8,128)}, f32[1,1024,256]{2,1,0:T(8,128)S(1)}, u32[]{:S(2)}, u32[]{:S(2)}) %collective-permute-start.46) | collective-permute-done | bytes 1048608 | tf_op jit(solution)/shard_map/ppermute | solution.py:1085
  1011.5 19.8 %collective-permute-done.58 = f32[512,768]{1,0:T(8,128)} collective-permute-done((f32[512,768]{1,0:T(8,128)}, f32[512,768]{1,0:T(8,128)}, u32[]{:S(2)}, u32[]{:S(2)}) %collective-permute-start.58) | collective-permute-done | bytes 1572896 | tf_op jit(solution)/shard_map/ppermute | solution.py:1085
  1060.4 35.3 %collective-permute-done.59 = f32[1,1024,256]{2,1,0:T(8,128)S(1)} collective-permute-done((f32[1,1024,256]{2,1,0:T(8,128)}, f32[1,1024,256]{2,1,0:T(8,128)S(1)}, u32[]{:S(2)}, u32[]{:S(2)}) %collective-permute-start.59) | collective-permute-done | bytes 1048608 | tf_op jit(solution)/shard_map/ppermute | solution.py:1085
  1113.1 19.1 %collective-permute-done.64 = f32[1,12800]{1,0:T(1,128)S(1)} collective-permute-done((f32[1,12800]{1,0:T(1,128)S(1)}, f32[1,12800]{1,0:T(1,128)S(1)}, u32[]{:S(2)}, u32[]{:S(2)}) %collective-permute-start.64) | collective-permute-done | bytes 51232 | tf_op jit(solution)/shard_map/ppermute | solution.py:1085
  1141.2 17.7 %collective-permute-done.67 = f32[1,512,256]{2,1,0:T(8,128)} collective-permute-done((f32[1,512,256]{2,1,0:T(8,128)}, f32[1,512,256]{2,1,0:T(8,128)}, u32[]{:S(2)}, u32[]{:S(2)}) %collective-permute-start.67) | collective-permute-done | bytes 524320 | tf_op jit(solution)/shard_map/ppermute | solution.py:1085
  (412 shorter events, 390.3 us)
Async XLA Ops:
  7.2 100.8 %all-gather.5.cloned.1.call-start = ((), (), s32[]{:S(2)}) async-start(), calls=%async_computation.6 | async-start | bytes 4718592 | tf_op jit(solution)/shard_map/all_gather | solution.py:1284
  9.1 210.8 %all-gather.7.cloned.1.call-start = ((), (), s32[]{:S(2)}) async-start(), calls=%async_computation.7 | async-start | bytes 20971520 | tf_op jit(solution)/shard_map/all_gather | solution.py:1326
  57.0 50.0 %collective-permute-start.3 = (f32[1024,256]{1,0:T(8,128)}, f32[1024,256]{1,0:T(8,128)S(1)}, u32[]{:S(2)}, u32[]{:S(2)}) collective-permute-start(f32[1024,256]{1,0:T(8,128)} %get-tuple-element.140.refs_0_.refs_1_), channel_id=1, source_target_pairs={{0,2},{1,3},{2,0},{3,1},{4,6},{5,7},{6,4},{7,5},{8,10},{9,11},{10,... | collective-permute-start | bytes 3145736 | tf_op jit(solution)/shard_map/ppermute | solution.py:1085
  108.0 1052.9 %reduce-scatter.8.cloned.1.call-start = ((), (), s32[]{:S(2)}) async-start(), calls=%async_computation.5 | async-start | bytes 20971520 | tf_op jit(solution)/shard_map/reduce_scatter | solution.py:1488
  109.2 49.5 %collective-permute-start.5 = (f32[1024,256]{1,0:T(8,128)S(1)}, f32[1024,256]{1,0:T(8,128)S(1)}, u32[]{:S(2)}, u32[]{:S(2)}) collective-permute-start(f32[1024,256]{1,0:T(8,128)S(1)} %copy-done.36), channel_id=1, source_target_pairs={{0,1},{1,0},{2,3},{3,2},{4,5},{5,4},{6,7},{7,6},{8,9},{9,8},{10,11... | collective-permute-start | bytes 3145736 | tf_op jit(solution)/shard_map/ppermute | solution.py:1085
  110.7 48.0 %collective-permute-start.6 = (f32[1024,256]{1,0:T(8,128)S(1)}, f32[1024,256]{1,0:T(8,128)S(1)}, u32[]{:S(2)}, u32[]{:S(2)}) collective-permute-start(f32[1024,256]{1,0:T(8,128)S(1)} %copy-done.51), channel_id=1, source_target_pairs={{0,4},{1,5},{2,6},{3,7},{4,0},{5,1},{6,2},{7,3},{8,12},{9,13},{10,... | collective-permute-start | bytes 3145736 | tf_op jit(solution)/shard_map/ppermute | solution.py:1085
  213.5 47.1 %collective-permute-start.13 = (f32[1024,256]{1,0:T(8,128)}, f32[1024,256]{1,0:T(8,128)}, u32[]{:S(2)}, u32[]{:S(2)}) collective-permute-start(f32[1024,256]{1,0:T(8,128)} %get-tuple-element.150.refs_0_), channel_id=1, source_target_pairs={{0,4},{1,5},{2,6},{3,7},{4,0},{5,1},{6,2},{7,3},{8,12},{9,13},{10,... | collective-permute-start | bytes 3145736 | tf_op jit(solution)/shard_map/ppermute | solution.py:1085
  218.7 74.6 %collective-permute-start.12 = (f32[1024,256]{1,0:T(8,128)}, f32[1024,256]{1,0:T(8,128)S(1)}, u32[]{:S(2)}, u32[]{:S(2)}) collective-permute-start(f32[1024,256]{1,0:T(8,128)} %get-tuple-element.151.refs_2_), channel_id=1, source_target_pairs={{0,1},{1,0},{2,3},{3,2},{4,5},{5,4},{6,7},{7,6},{8,9},{9,8},{10,11... | collective-permute-start | bytes 3145736 | tf_op jit(solution)/shard_map/ppermute | solution.py:1085
  324.7 50.5 %collective-permute-start.17 = (f32[2,128,2176]{2,1,0:T(8,128)}, f32[2,128,2176]{2,1,0:T(8,128)S(1)}, u32[]{:S(2)}, u32[]{:S(2)}) collective-permute-start(f32[2,128,2176]{2,1,0:T(8,128)} %tie.16), channel_id=1, source_target_pairs={{0,1},{1,0},{2,3},{3,2},{4,5},{5,4},{6,7},{7,6},{8,9},{9,8},{10,11... | collective-permute-start | bytes 6684680 | tf_op jit(solution)/shard_map/ppermute | solution.py:1085
  380.8 49.7 %collective-permute-start.18 = (f32[2,128,2176]{2,1,0:T(8,128)}, f32[2,128,2176]{2,1,0:T(8,128)S(1)}, u32[]{:S(2)}, u32[]{:S(2)}) collective-permute-start(f32[2,128,2176]{2,1,0:T(8,128)} %get-tuple-element.167), channel_id=1, source_target_pairs={{0,1},{1,0},{2,3},{3,2},{4,5},{5,4},{6,7},{7,6},{8,9},{9,8},{10,11... | collective-permute-start | bytes 6684680 | tf_op jit(solution)/shard_map/ppermute | solution.py:1085
  382.2 49.5 %collective-permute-start.19 = (f32[2,128,2176]{2,1,0:T(8,128)}, f32[2,128,2176]{2,1,0:T(8,128)S(1)}, u32[]{:S(2)}, u32[]{:S(2)}) collective-permute-start(f32[2,128,2176]{2,1,0:T(8,128)} %get-tuple-element.165.refs_5_), channel_id=1, source_target_pairs={{0,2},{1,3},{2,0},{3,1},{4,6},{5,7},{6,4},{7,5},{8,10},{9,11},{10,... | collective-permute-start | bytes 6684680 | tf_op jit(solution)/shard_map/ppermute | solution.py:1085
  436.9 50.4 %collective-permute-start.20 = (f32[2,128,2176]{2,1,0:T(8,128)}, f32[2,128,2176]{2,1,0:T(8,128)S(1)}, u32[]{:S(2)}, u32[]{:S(2)}) collective-permute-start(f32[2,128,2176]{2,1,0:T(8,128)} %get-tuple-element.169), channel_id=1, source_target_pairs={{0,1},{1,0},{2,3},{3,2},{4,5},{5,4},{6,7},{7,6},{8,9},{9,8},{10,11... | collective-permute-start | bytes 6684680 | tf_op jit(solution)/shard_map/ppermute | solution.py:1085
  437.8 49.4 %collective-permute-start.21 = (f32[1,128,2176]{2,1,0:T(8,128)}, f32[1,128,2176]{2,1,0:T(8,128)S(1)}, u32[]{:S(2)}, u32[]{:S(2)}) collective-permute-start(f32[1,128,2176]{2,1,0:T(8,128)} %get-tuple-element.170.refs_2_), channel_id=1, source_target_pairs={{0,4},{1,5},{2,6},{3,7},{4,0},{5,1},{6,2},{7,3},{8,12},{9,13},{10,... | collective-permute-start | bytes 3342344 | tf_op jit(solution)/shard_map/ppermute | solution.py:1085
  493.3 667.6 %reduce-scatter.4.cloned.1.call-start = ((), (), s32[]{:S(2)}) async-start(), calls=%async_computation.3 | async-start | bytes 20971520 | tf_op jit(solution)/shard_map/reduce_scatter | solution.py:1488
  493.3 49.7 %collective-permute-start.22 = (f32[2,128,2176]{2,1,0:T(8,128)}, f32[2,128,2176]{2,1,0:T(8,128)S(1)}, u32[]{:S(2)}, u32[]{:S(2)}) collective-permute-start(f32[2,128,2176]{2,1,0:T(8,128)} %get-tuple-element.176), channel_id=1, source_target_pairs={{0,1},{1,0},{2,3},{3,2},{4,5},{5,4},{6,7},{7,6},{8,9},{9,8},{10,11... | collective-permute-start | bytes 6684680 | tf_op jit(solution)/shard_map/ppermute | solution.py:1085
  494.2 49.3 %collective-permute-start.23 = (f32[2,128,2176]{2,1,0:T(8,128)}, f32[2,128,2176]{2,1,0:T(8,128)S(1)}, u32[]{:S(2)}, u32[]{:S(2)}) collective-permute-start(f32[2,128,2176]{2,1,0:T(8,128)} %get-tuple-element.172.refs_2_), channel_id=1, source_target_pairs={{0,2},{1,3},{2,0},{3,1},{4,6},{5,7},{6,4},{7,5},{8,10},{9,11},{10,... | collective-permute-start | bytes 6684680 | tf_op jit(solution)/shard_map/ppermute | solution.py:1085
  548.9 52.0 %collective-permute-start.25 = (f32[1,128,2176]{2,1,0:T(8,128)}, f32[1,128,2176]{2,1,0:T(8,128)S(1)}, u32[]{:S(2)}, u32[]{:S(2)}) collective-permute-start(f32[1,128,2176]{2,1,0:T(8,128)} %get-tuple-element.179.refs_2_), channel_id=1, source_target_pairs={{0,4},{1,5},{2,6},{3,7},{4,0},{5,1},{6,2},{7,3},{8,12},{9,13},{10,... | collective-permute-start | bytes 3342344 | tf_op jit(solution)/shard_map/ppermute | solution.py:1085
  549.6 51.3 %collective-permute-start.24 = (f32[2,1024,256]{2,1,0:T(8,128)}, f32[2,1024,256]{2,1,0:T(8,128)S(1)}, u32[]{:S(2)}, u32[]{:S(2)}) collective-permute-start(f32[2,1024,256]{2,1,0:T(8,128)} %get-tuple-element.178), channel_id=1, source_target_pairs={{0,1},{1,0},{2,3},{3,2},{4,5},{5,4},{6,7},{7,6},{8,9},{9,8},{10,11... | collective-permute-start | bytes 6291464 | tf_op jit(solution)/shard_map/ppermute | solution.py:1085
  606.8 554.0 %reduce-scatter.6.cloned.1.call-start = ((), (), s32[]{:S(2)}) async-start(), calls=%async_computation.4 | async-start | bytes 20971520 | tf_op jit(solution)/shard_map/reduce_scatter | solution.py:1488
  699.0 84.6 %collective-permute-start.29 = (f32[2,1024,256]{2,1,0:T(8,128)S(1)}, f32[2,1024,256]{2,1,0:T(8,128)S(1)}, u32[]{:S(2)}, u32[]{:S(2)}) collective-permute-start(f32[2,1024,256]{2,1,0:T(8,128)S(1)} %copy-done.44), channel_id=1, source_target_pairs={{0,1},{1,0},{2,3},{3,2},{4,5},{5,4},{6,7},{7,6},{8,9},{9,8},{10,11... | collective-permute-start | bytes 6291464 | tf_op jit(solution)/shard_map/ppermute | solution.py:1085
  703.9 79.8 %collective-permute-start.28 = (f32[1,1024,256]{2,1,0:T(8,128)}, f32[1,1024,256]{2,1,0:T(8,128)S(1)}, u32[]{:S(2)}, u32[]{:S(2)}) collective-permute-start(f32[1,1024,256]{2,1,0:T(8,128)} %get-tuple-element.190), channel_id=1, source_target_pairs={{0,4},{1,5},{2,6},{3,7},{4,0},{5,1},{6,2},{7,3},{8,12},{9,13},{10,... | collective-permute-start | bytes 3145736 | tf_op jit(solution)/shard_map/ppermute | solution.py:1085
  839.7 48.5 %collective-permute-start.49 = (f32[4,512,256]{2,1,0:T(8,128)}, f32[4,512,256]{2,1,0:T(8,128)}, u32[]{:S(2)}, u32[]{:S(2)}) collective-permute-start(f32[4,512,256]{2,1,0:T(8,128)} %get-tuple-element.241), channel_id=1, source_target_pairs={{0,8},{8,0},{16,24},{24,16},{1,9},{9,1},{17,25},{25,17},{2,10},{10... | collective-permute-start | bytes 6291464 | tf_op jit(solution)/shard_map/ppermute | solution.py:1085
  885.9 47.6 %collective-permute-start.44 = (f32[2,1024,256]{2,1,0:T(8,128)}, f32[2,1024,256]{2,1,0:T(8,128)S(1)}, u32[]{:S(2)}, u32[]{:S(2)}) collective-permute-start(f32[2,1024,256]{2,1,0:T(8,128)} %get-tuple-element.231), channel_id=1, source_target_pairs={{0,1},{1,0},{2,3},{3,2},{4,5},{5,4},{6,7},{7,6},{8,9},{9,8},{10,11... | collective-permute-start | bytes 6291464 | tf_op jit(solution)/shard_map/ppermute | solution.py:1085
  887.6 47.3 %collective-permute-start.45 = (f32[2,1024,256]{2,1,0:T(8,128)}, f32[2,1024,256]{2,1,0:T(8,128)S(1)}, u32[]{:S(2)}, u32[]{:S(2)}) collective-permute-start(f32[2,1024,256]{2,1,0:T(8,128)} %get-tuple-element.232), channel_id=1, source_target_pairs={{0,2},{1,3},{2,0},{3,1},{4,6},{5,7},{6,4},{7,5},{8,10},{9,11},{10,... | collective-permute-start | bytes 6291464 | tf_op jit(solution)/shard_map/ppermute | solution.py:1085
  887.6 53.4 %collective-permute-start.48 = (f32[4,512,256]{2,1,0:T(8,128)}, f32[4,512,256]{2,1,0:T(8,128)}, u32[]{:S(2)}, u32[]{:S(2)}) collective-permute-start(f32[4,512,256]{2,1,0:T(8,128)} %get-tuple-element.239), channel_id=1, source_target_pairs={{0,8},{8,0},{16,24},{24,16},{1,9},{9,1},{17,25},{25,17},{2,10},{10... | collective-permute-start | bytes 6291464 | tf_op jit(solution)/shard_map/ppermute | solution.py:1085
  887.6 53.9 %collective-permute-start.54 = (f32[4,512,256]{2,1,0:T(8,128)}, f32[4,512,256]{2,1,0:T(8,128)}, u32[]{:S(2)}, u32[]{:S(2)}) collective-permute-start(f32[4,512,256]{2,1,0:T(8,128)} %get-tuple-element.246), channel_id=1, source_target_pairs={{0,8},{8,0},{16,24},{24,16},{1,9},{9,1},{17,25},{25,17},{2,10},{10... | collective-permute-start | bytes 6291464 | tf_op jit(solution)/shard_map/ppermute | solution.py:1085
  892.0 53.5 %collective-permute-start.50 = (f32[4,512,256]{2,1,0:T(8,128)}, f32[4,512,256]{2,1,0:T(8,128)}, u32[]{:S(2)}, u32[]{:S(2)}) collective-permute-start(f32[4,512,256]{2,1,0:T(8,128)} %add.219), channel_id=1, source_target_pairs={{0,16},{8,24},{16,0},{24,8},{1,17},{9,25},{17,1},{25,9},{2,18},{10... | collective-permute-start | bytes 6291464 | tf_op jit(solution)/shard_map/ppermute | solution.py:1085
  940.1 49.3 %collective-permute-start.47 = (f32[2,1024,256]{2,1,0:T(8,128)}, f32[2,1024,256]{2,1,0:T(8,128)S(1)}, u32[]{:S(2)}, u32[]{:S(2)}) collective-permute-start(f32[2,1024,256]{2,1,0:T(8,128)} %get-tuple-element.236), channel_id=1, source_target_pairs={{0,1},{1,0},{2,3},{3,2},{4,5},{5,4},{6,7},{7,6},{8,9},{9,8},{10,11... | collective-permute-start | bytes 6291464 | tf_op jit(solution)/shard_map/ppermute | solution.py:1085
  941.0 58.4 %collective-permute-start.53 = (f32[4,512,256]{2,1,0:T(8,128)}, f32[4,512,256]{2,1,0:T(8,128)}, u32[]{:S(2)}, u32[]{:S(2)}) collective-permute-start(f32[4,512,256]{2,1,0:T(8,128)} %get-tuple-element.244), channel_id=1, source_target_pairs={{0,8},{8,0},{16,24},{24,16},{1,9},{9,1},{17,25},{25,17},{2,10},{10... | collective-permute-start | bytes 6291464 | tf_op jit(solution)/shard_map/ppermute | solution.py:1085
  941.6 47.7 %collective-permute-start.46 = (f32[1,1024,256]{2,1,0:T(8,128)}, f32[1,1024,256]{2,1,0:T(8,128)S(1)}, u32[]{:S(2)}, u32[]{:S(2)}) collective-permute-start(f32[1,1024,256]{2,1,0:T(8,128)} %get-tuple-element.234), channel_id=1, source_target_pairs={{0,4},{1,5},{2,6},{3,7},{4,0},{5,1},{6,2},{7,3},{8,12},{9,13},{10,... | collective-permute-start | bytes 3145736 | tf_op jit(solution)/shard_map/ppermute | solution.py:1085
  945.5 61.3 %collective-permute-start.55 = (f32[4,512,256]{2,1,0:T(8,128)}, f32[4,512,256]{2,1,0:T(8,128)}, u32[]{:S(2)}, u32[]{:S(2)}) collective-permute-start(f32[4,512,256]{2,1,0:T(8,128)} %add.224), channel_id=1, source_target_pairs={{0,16},{8,24},{16,0},{24,8},{1,17},{9,25},{17,1},{25,9},{2,18},{10... | collective-permute-start | bytes 6291464 | tf_op jit(solution)/shard_map/ppermute | solution.py:1085
  947.7 50.8 %collective-permute-start.61 = (f32[24,2048]{1,0:T(8,128)S(1)}, f32[24,2048]{1,0:T(8,128)S(1)}, u32[]{:S(2)}, u32[]{:S(2)}) collective-permute-start(f32[24,2048]{1,0:T(8,128)S(1)} %add.232), channel_id=1, source_target_pairs={{0,16},{8,24},{16,0},{24,8},{1,17},{9,25},{17,1},{25,9},{2,18},{10... | collective-permute-start | bytes 589832 | tf_op jit(solution)/shard_map/ppermute | solution.py:1085
  (115 other events, 1557.6 us)
Sparse Core Ops, SparseCore 0:
  10.1 97.2 all-gather.4
  109.0 105.9 all-gather.6
  493.4 124.1 reduce-scatter.7
  620.7 126.0 reduce-scatter.3
  749.9 126.0 reduce-scatter.5
